TPU v7x, 32 devices: a whole 2x2x4 slice. The times are simulated.
32 devices in a mesh: row: 16 (over z, x, core), col: 2 (over y).
Axes of the slice: x: 2, y: 2, z: 4, core: 2. Of those that a mesh axis runs over, the one named last changes fastest.
Arguments:
- tokens: bfloat16 [1024, 12288], P('col', 'row'), may hold values from -6 to 6
- weight: bfloat16 [12288, 24576], P('row', 'col'), may hold values from -0.0546875 to 0.0546875
- pre_act: bfloat16 [1024, 24576], P('row', 'col'), may hold values from -6 to 6
- out_grad: bfloat16 [1024, 24576], P('row', 'col'), may hold values from -6 to 6
Outputs:
- input_grad: bfloat16 [1024, 12288], P('col', 'row')
- weight_grad: bfloat16 [12288, 24576], P('row', 'col')
- left_stats: bfloat16 [12288, 24576], P('row', 'col')
- right_stats: bfloat16 [12288, 24576], P('row', 'col')
All inputs are finite; a program needn't handle non-finite values.
Results may differ from a plain program's by a relative error of at most 0.0054.
Values may be sent and summed in bfloat16 or wider, within the bound.
No kernel may reach another device: no remote copies, remote signals or barrier semaphores. Data moves between devices by JAX's collectives and lax.ppermute only.
A program may use at most 256 MiB of HBM per device.

v0:
```python
import math

import jax
import jax.numpy as jnp
from jax import lax
from jax.sharding import PartitionSpec as P

BLOCK = 384


def gelu_slope(value):
    coeff = math.sqrt(2.0 / math.pi)
    inner = coeff * (value + 0.044715 * value * value * value)
    tanh_u = jnp.tanh(inner)
    return 0.5 * (1.0 + tanh_u) + 0.5 * value * (1.0 - tanh_u * tanh_u) * coeff * (
        1.0 + 3.0 * 0.044715 * value * value
    )


def on_device(tokens, weight, pre_act, out_grad):
    x_all = lax.all_gather(tokens, "col", axis=0, tiled=True)
    num_tokens = x_all.shape[0]
    rows_here = weight.shape[0]
    cols_here = weight.shape[1]
    hidden_grad = (out_grad.astype(jnp.float32) * gelu_slope(pre_act.astype(jnp.float32))).astype(
        jnp.bfloat16
    )
    grad_all = lax.all_gather(hidden_grad, "row", axis=0, tiled=True)
    partial_value = lax.dot_general(
        grad_all, weight, (((1,), (1,)), ((), ())), preferred_element_type=jnp.float32
    )
    weight_sum = lax.dot_general(
        x_all, grad_all, (((0,), (0,)), ((), ())), preferred_element_type=jnp.float32
    )
    input_grad = lax.psum_scatter(partial_value, "col", scatter_dimension=0, tiled=True).astype(
        jnp.bfloat16
    )
    scale = 1.0 / (BLOCK * num_tokens)
    tiles = weight_sum.reshape(rows_here // BLOCK, BLOCK, cols_here // BLOCK, BLOCK)
    left = jnp.einsum("ipjq,irjq->ipjr", tiles, tiles, precision=lax.Precision.HIGHEST) * scale
    right = jnp.einsum("ipjq,ipjr->iqjr", tiles, tiles, precision=lax.Precision.HIGHEST) * scale
    left_stats = left.reshape(rows_here, cols_here).astype(jnp.bfloat16)
    right_stats = right.reshape(rows_here, cols_here).astype(jnp.bfloat16)
    return (input_grad, weight_sum.astype(jnp.bfloat16), left_stats, right_stats)


def solution(mesh):
    in_specs = (P("col", "row"), P("row", "col"), P("row", "col"), P("row", "col"))
    out_specs = (P("col", "row"), P("row", "col"), P("row", "col"), P("row", "col"))
    return jax.shard_map(
        on_device, mesh=mesh, in_specs=in_specs, out_specs=out_specs, check_vma=False
    )
```

profile of v0, /device:TPU:0, one launch (start us, length us, event | category | flops | bytes accessed | tf_op | source)
XLA Modules:
  0.0 563.6 jit_solution(3712460784870720206)
XLA Ops:
  7.2 0.0 all-gather.3.cloned.1.call-start
  7.2 4.5 fusion.17
  11.7 0.0 all-gather.3.cloned.1.call-update
  11.7 0.0 all-gather.5.cloned.1.call-start
  11.7 0.7 all-gather.5.cloned.1.call-update
  12.4 0.0 reduce-scatter.2.cloned.1.call-start
  12.5 130.6 %all-gather.3.cloned.1.call-done = bf16[1024,12288]{1,0:T(8,128)(2,1)} async-done(((bf16[64,12288]{1,0:T(8,128)(2,1)}), bf16[1024,12288]{1,0:T(8,128)(2,1)}) %all-gather.3.cloned.1.call-update) | async-done | bytes 25165840 | tf_op jit(solution)/shard_map/all_gather | solution.py:28
  143.1 26.2 %fusion.20 = f32[1024,768]{1,0:T(8,128)} fusion(bf16[1024,12288]{1,0:T(8,128)(2,1)} %all-gather.3.cloned.1.call-done, bf16[768,12288]{1,0:T(8,128)(2,1)} %param.5), kind=kOutput, calls=%fused_computation.26 | convolution fusion | flops 19327352832 | bytes 47185920 | tf_op jit(solution)/shard_map/dot_general | solution.py:29
  169.3 0.0 reduce-scatter.2.cloned.1.call-update
  169.4 2.6 all-gather.5.cloned.1.call-done
  171.9 32.7 %fusion.19 = (bf16[768,12288]{0,1:T(8,128)(2,1)}, f32[768,12288]{0,1:T(8,128)}) fusion(bf16[1024,12288]{1,0:T(8,128)(2,1)} %all-gather.3.cloned.1.call-done, bf16[1024,768]{1,0:T(8,128)(2,1)} %all-gather.5.cloned.1.call-done), kind=kOutput, calls=%fused_computation.25 | convolution fusion | flops 19336790016 | bytes 83361792 | tf_op jit(solution)/shard_map/dot_general | solution.py:32
  204.7 24.6 %copy.19 = bf16[768,12288]{1,0:T(8,128)(2,1)} copy(bf16[768,12288]{0,1:T(8,128)(2,1)} %get-tuple-element.12) | data formatting | bytes 37748736
  229.3 45.0 %reshape.15 = f32[2,384,32,384]{1,0,3,2:T(2,128)} reshape(f32[768,12288]{0,1:T(8,128)} %get-tuple-element.13) | data formatting | bytes 75497472 | tf_op jit(solution)/shard_map/reshape | solution.py:39
  274.2 99.8 %fusion.4 = bf16[2,384,32,384]{1,3,2,0:T(8,128)(2,1)} fusion(f32[2,384,32,384]{1,0,3,2:T(2,128)} %reshape.15), kind=kOutput, calls=%fused_computation.7 | convolution fusion | flops 43505418240 | bytes 56623104 | tf_op jit(solution)/shard_map/ipjq,irjq->ipjr/dot_general | solution.py:40
  374.1 24.5 %copy.15 = bf16[2,384,32,384]{3,2,1,0:T(8,128)(2,1)} copy(bf16[2,384,32,384]{1,3,2,0:T(8,128)(2,1)} %fusion.4) | data formatting | bytes 37748736 | tf_op jit(solution)/shard_map/convert_element_type | solution.py:42
  398.5 20.3 %copy.20 = bf16[96,8,32,384]{3,1,2,0:T(8,128)(2,1)} copy(bf16[96,8,32,384]{3,2,1,0:T(8,128)(2,1)} %bitcast.18) | data formatting | bytes 37748736
  418.8 91.1 %fusion.5 = bf16[2,384,32,384]{1,3,2,0:T(8,128)(2,1)} fusion(f32[2,384,32,384]{1,0,3,2:T(2,128)} %reshape.15), kind=kOutput, calls=%fused_computation.8 | convolution fusion | flops 43505418240 | bytes 56623104 | tf_op jit(solution)/shard_map/ipjq,ipjr->iqjr/dot_general | solution.py:41
  509.9 24.5 %copy.18 = bf16[2,384,32,384]{3,2,1,0:T(8,128)(2,1)} copy(bf16[2,384,32,384]{1,3,2,0:T(8,128)(2,1)} %fusion.5) | data formatting | bytes 37748736 | tf_op jit(solution)/shard_map/convert_element_type | solution.py:43
  534.4 20.3 %copy.21 = bf16[96,8,32,384]{3,1,2,0:T(8,128)(2,1)} copy(bf16[96,8,32,384]{3,2,1,0:T(8,128)(2,1)} %bitcast.19) | data formatting | bytes 37748736
  554.7 0.0 reduce-scatter.2.cloned.1.call-done
  554.7 2.4 convert_element_type.36
Async XLA Ops:
  7.2 136.0 %all-gather.3.cloned.1.call-start = ((), (), s32[]{:S(2)}) async-start(), calls=%async_computation.1 | async-start | bytes 26738688 | tf_op jit(solution)/shard_map/all_gather | solution.py:28
  11.7 160.2 %all-gather.5.cloned.1.call-start = ((), (), s32[]{:S(2)}) async-start(), calls=%async_computation.3 | async-start | bytes 2359296 | tf_op jit(solution)/shard_map/all_gather | solution.py:21
  12.4 542.3 %reduce-scatter.2.cloned.1.call-start = ((), (), s32[]{:S(2)}) async-start(), calls=%async_computation.2 | async-start | bytes 4718592 | tf_op jit(solution)/shard_map/reduce_scatter | solution.py:35
Sparse Core Ops, SparseCore 0:
  11.8 131.2 all-gather.2
  144.7 27.1 all-gather.4
  174.2 43.3 reduce-scatter.1
where the time goes:
time: 567 us; the launch traced here: 564 us
  matrix products  250 us (44%)
  local copies, waits for them, and re-layouts  159 us (28%)
  waiting for transfers between devices  134 us (24%)
  between operations  13.7 us (2%)
  other arithmetic  6.82 us (1%)
    all_gather x1, waiting for transfers between devices, on_device(): grad_all = lax.all_gather(hidden_grad, 'row', axis=0, tiled=True)  131 us
    dot_general x1, matrix products, on_device(): jnp.einsum('ipjq,irjq->ipjr', tiles, tiles, precision=lax.Precision.HIGHEST)  99.8 us
    dot_general x1, matrix products, on_device(): jnp.einsum('ipjq,ipjr->iqjr', tiles, tiles, precision=lax.Precision.HIGHEST)  91.1 us
    unnamed x3, local copies, waits for them, and re-layouts  65.2 us
    reshape x1, local copies, waits for them, and re-layouts, on_device(): weight_sum.reshape(rows_here // BLOCK, BLOCK, cols_here // BLOCK, BLOCK)  45 us
    dot_general x1, matrix products, on_device(): lax.dot_general(x_all, grad_all, (((0,), (0,)), ((), ())), preferred_elem...  32.7 us
    dot_general x1, matrix products, on_device(): lax.dot_general(grad_all, weight, (((1,), (1,)), ((), ())), preferred_ele...  26.2 us
    convert_element_type x1, local copies, waits for them, and re-layouts, on_device(): left_stats = left.reshape(rows_here, cols_here).astype(jnp.bfloat16)  24.5 us
  transfers between devices with their start and end apart: 3, of which 2 were waited for; matrix products, arithmetic and copies ran while one was open for 73% of the time, Pallas kernels for 0%

commit v1 on v0

v1 whole, which is shorter than its diff:
```python
import functools
import math

import jax
import jax.numpy as jnp
from jax import lax
from jax.experimental import pallas as pl
from jax.experimental.pallas import tpu as pltpu
from jax.sharding import PartitionSpec as P

BLOCK = 384
STEP = 2 * BLOCK
SHARES = (6, 5, 3, 2)
VMEM_LIMIT = 56 * 1024 * 1024


def gelu_slope(value):
    coeff = math.sqrt(2.0 / math.pi)
    inner = coeff * (value + 0.044715 * value * value * value)
    tanh_u = jnp.tanh(inner)
    return 0.5 * (1.0 + tanh_u) + 0.5 * value * (1.0 - tanh_u * tanh_u) * coeff * (
        1.0 + 3.0 * 0.044715 * value * value
    )


def chunk_steps(steps):
    bounds, done = [0], 0
    for share in SHARES:
        done += share
        bounds.append(round(steps * done / sum(SHARES)))
    return [(a, b - a) for a, b in zip(bounds, bounds[1:]) if b > a]


def block_stats(scale, grad_f32, wg_ref, left_ref, right_ref):
    rows, cols = grad_f32.shape
    wg_ref[...] = grad_f32.astype(wg_ref.dtype)
    for i in range(rows // BLOCK):
        for j in range(cols // BLOCK):
            at = (pl.ds(i * BLOCK, BLOCK), pl.ds(j * BLOCK, BLOCK))
            tile = wg_ref[at]
            left = lax.dot_general(
                tile, tile, (((1,), (1,)), ((), ())), preferred_element_type=jnp.float32
            )
            left_ref[at] = (left * scale).astype(left_ref.dtype)
            right = lax.dot_general(
                tile, tile, (((0,), (0,)), ((), ())), preferred_element_type=jnp.float32
            )
            right_ref[at] = (right * scale).astype(right_ref.dtype)


def chunk_kernel(scale, with_share, first, *refs):
    n_in = 2 + (1 if with_share else 0) + (1 if with_share and not first else 0)
    ins, outs = refs[:n_in], refs[n_in + (0 if first else 3):]
    xt_ref, hg_ref = ins[:2]
    wg_ref, left_ref, right_ref = outs[:3]
    if with_share:
        w_ref, acc_ref = ins[2], outs[3]

        @pl.when(pl.program_id(0) == 0)
        def _():
            if first:
                acc_ref[...] = jnp.zeros_like(acc_ref)
            else:
                acc_ref[...] = ins[3][...]

        acc_ref[...] += lax.dot_general(
            hg_ref[...], w_ref[...], (((1,), (1,)), ((), ())), preferred_element_type=jnp.float32
        )
    grad = jnp.dot(xt_ref[...], hg_ref[...], preferred_element_type=jnp.float32)
    block_stats(scale, grad, wg_ref, left_ref, right_ref)


def chunk_call(scale, x_t, hg, weight, acc, outs, offset, steps, with_share):
    rows, tokens = x_t.shape
    first = outs is None
    at = lambda s: (0, s + offset)
    args = [x_t, hg]
    in_specs = [
        pl.BlockSpec((rows, tokens), lambda s: (0, 0)),
        pl.BlockSpec((tokens, STEP), lambda s: (0, s)),
    ]
    out_shape = [jax.ShapeDtypeStruct(weight.shape, jnp.bfloat16)] * 3
    out_specs = [pl.BlockSpec((rows, STEP), at)] * 3
    if with_share:
        args.append(weight)
        in_specs.append(pl.BlockSpec((rows, STEP), at))
        out_shape = out_shape + [jax.ShapeDtypeStruct((tokens, rows), jnp.float32)]
        out_specs = out_specs + [pl.BlockSpec((tokens, rows), lambda s: (0, 0))]
        if not first:
            args.append(acc)
            in_specs.append(pl.BlockSpec((tokens, rows), lambda s: (0, 0)))
    aliases = {}
    if not first:
        aliases = {len(args) + i: i for i in range(3)}
        args += list(outs)
        in_specs += [pl.BlockSpec(memory_space=pl.ANY)] * 3
    cells = steps * STEP * rows
    return pl.pallas_call(
        functools.partial(chunk_kernel, scale, with_share, first),
        grid=(steps,),
        in_specs=in_specs,
        out_specs=out_specs,
        out_shape=out_shape,
        input_output_aliases=aliases,
        compiler_params=pltpu.CompilerParams(vmem_limit_bytes=VMEM_LIMIT),
        cost_estimate=pl.CostEstimate(
            flops=cells * (2 * tokens * (2 if with_share else 1) + 4 * BLOCK),
            bytes_accessed=8 * cells + 2 * steps * STEP * tokens,
            transcendentals=0,
        ),
        name="chunk",
    )(*args)


def share_kernel(_, hg_ref, w_ref, acc_ref, out_ref):
    total = acc_ref[...] + lax.dot_general(
        hg_ref[...], w_ref[...], (((1,), (1,)), ((), ())), preferred_element_type=jnp.float32
    )
    out_ref[...] = total[None].astype(out_ref.dtype)


def share_call(which, hg, weight, acc, count, offset, dtype):
    tokens, width = hg.shape
    rows = weight.shape[0]
    group = tokens // count
    tile = 256 if rows % 256 == 0 else BLOCK
    pieces = which.shape[0]
    grid_spec = pltpu.PrefetchScalarGridSpec(
        num_scalar_prefetch=1,
        grid=(pieces, rows // tile),
        in_specs=[
            pl.BlockSpec((group, width), lambda p, d, w: (w[p], 0)),
            pl.BlockSpec((tile, width), lambda p, d, w: (d, 0)),
            pl.BlockSpec((group, tile), lambda p, d, w: (w[p], d)),
        ],
        out_specs=pl.BlockSpec((1, group, tile), lambda p, d, w: (p, 0, d)),
    )
    w_last = weight[:, offset * STEP:]
    return pl.pallas_call(
        share_kernel,
        grid_spec=grid_spec,
        out_shape=jax.ShapeDtypeStruct((pieces, group, rows), dtype),
        compiler_params=pltpu.CompilerParams(vmem_limit_bytes=VMEM_LIMIT),
        cost_estimate=pl.CostEstimate(
            flops=2 * pieces * group * width * rows,
            bytes_accessed=2 * rows * width + pieces * group * (2 * width + 6 * rows),
            transcendentals=0,
        ),
        name="share",
    )(which, hg, w_last, acc)


def on_device(cols, tokens, weight, pre_act, out_grad):
    me = lax.axis_index("col")
    group, rows = tokens.shape
    num_tokens = group * cols
    scale = 1.0 / (BLOCK * num_tokens)
    chunks = chunk_steps(weight.shape[1] // STEP)

    gathered = []
    for offset, steps in chunks:
        at = slice(offset * STEP, (offset + steps) * STEP)
        slope = gelu_slope(pre_act[:, at].astype(jnp.float32))
        hidden = (out_grad[:, at].astype(jnp.float32) * slope).astype(jnp.bfloat16)
        gathered.append(lax.all_gather(hidden, "row", axis=0, tiled=True))

    own_t = tokens.T
    x_t = jnp.zeros((rows, num_tokens), jnp.bfloat16)
    x_t = lax.dynamic_update_slice(x_t, own_t, (0, me * group))
    for s in range(1, cols):
        piece = lax.ppermute(own_t, "col", [(i, (i + s) % cols) for i in range(cols)])
        x_t = lax.dynamic_update_slice(x_t, piece, (0, (me - s) % cols * group))

    acc, outs = None, None
    for (offset, steps), hg in zip(chunks[:-1], gathered[:-1]):
        *outs, acc = chunk_call(scale, x_t, hg, weight, acc, outs, offset, steps, True)

    offset, steps = chunks[-1]
    hg = gathered[-1]
    others = (me + jnp.arange(1, cols, dtype=jnp.int32)) % cols
    shares = share_call(others, hg, weight, acc, cols, offset, jnp.bfloat16)
    arrived = [
        lax.ppermute(shares[s - 1], "col", [(i, (i + s) % cols) for i in range(cols)])
        for s in range(1, cols)
    ]
    own = share_call(me[None], hg, weight, acc, cols, offset, jnp.float32)[0]
    outs = chunk_call(scale, x_t, hg, weight, None, outs, offset, steps, False)
    for piece in arrived:
        own = own + piece.astype(jnp.float32)
    return (own.astype(jnp.bfloat16), *outs)


def solution(mesh):
    in_specs = (P("col", "row"), P("row", "col"), P("row", "col"), P("row", "col"))
    out_specs = (P("col", "row"), P("row", "col"), P("row", "col"), P("row", "col"))
    return jax.shard_map(
        functools.partial(on_device, mesh.shape["col"]),
        mesh=mesh,
        in_specs=in_specs,
        out_specs=out_specs,
        check_vma=False,
    )
```

time: 567 us -> 300 us (0.53)
  matrix products: 250 us -> 0 us
  local copies, waits for them, and re-layouts: 159 us -> 4.22 us
  Pallas kernels: 0 us -> 94.8 us
  waiting for transfers between devices: 134 us -> 171 us
    dot_general x4 -> x0, matrix products: 250 us -> none  [the longest x1 99.8 us: on_device(): jnp.einsum('ipjq,irjq->ipjr', tiles, tiles, precision=lax.Precision.HIGHEST)]
    pallas_call x0 -> x6, Pallas kernels: none -> 94.8 us  [the longest x4 84.3 us: chunk_call(): pl.pallas_call(functools.partial(chunk_kernel, scale, with_share, first),...]
    unnamed x3 -> x9, local copies, waits for them, and re-layouts: 65.2 us -> 0.29 us
    convert_element_type x2 -> x0, local copies, waits for them, and re-layouts: 49 us -> none  [the longest x1 24.5 us: on_device(): left_stats = left.reshape(rows_here, cols_here).astype(jnp.bfloat16)]
    reshape x1 -> x0, local copies, waits for them, and re-layouts: 45 us -> none  [on_device(): weight_sum.reshape(rows_here // BLOCK, BLOCK, cols_here // BLOCK, BLOCK)]
    all_gather x2 -> x4, waiting for transfers between devices: 133 us -> 154 us  [on_device(): gathered.append(lax.all_gather(hidden, 'row', axis=0, tiled=True))]
    ppermute x0 -> x2, waiting for transfers between devices: none -> 17.3 us  [the longest x1 13.7 us: on_device(): lax.ppermute(own_t, 'col', [(i, (i + s) % cols) for i in range(cols)])]
  transfers between devices with their start and end apart: 3 -> 6, of which waited for: 2 -> 6; matrix products, arithmetic and copies ran while one was open for 73% -> 4% of each run, Pallas kernels for 0% -> 30%
where the time goes in v1:
time: 300 us
  waiting for transfers between devices  171 us (57%)
  Pallas kernels  94.8 us (32%)
  between operations  13.8 us (5%)
  other arithmetic  10.6 us (4%)
  starting transfers between devices  4.67 us (2%)
  local copies, waits for them, and re-layouts  4.22 us (1%)
    all_gather x4, waiting for transfers between devices, on_device(): gathered.append(lax.all_gather(hidden, 'row', axis=0, tiled=True))  154 us
    pallas_call x4, Pallas kernels, chunk_call(): pl.pallas_call(functools.partial(chunk_kernel, scale, with_share, first),...  84.3 us
    ppermute x1, waiting for transfers between devices, on_device(): lax.ppermute(own_t, 'col', [(i, (i + s) % cols) for i in range(cols)])  13.7 us
    pallas_call x2, Pallas kernels, share_call(): pl.pallas_call(share_kernel, grid_spec=grid_spec, out_shape=jax.ShapeDtyp...  10.5 us
    convert_element_type x4, other arithmetic, on_device(): hidden = (out_grad[:, at].astype(jnp.float32) * slope).astype(jnp.bfloat16)  9.52 us
  transfers between devices with their start and end apart: 6, of which 6 were waited for; matrix products, arithmetic and copies ran while one was open for 4% of the time, Pallas kernels for 30%

profile of v1, /device:TPU:0, one launch (start us, length us, event | category | flops | bytes accessed | tf_op | source)
XLA Modules:
  0.0 299.5 jit_solution(5016703556396518101)
XLA Ops:
  7.2 0.0 copy-start.2
  7.2 0.0 all-gather.11.cloned.1.call-start
  7.2 3.0 fusion.8
  10.2 0.0 all-gather.11.cloned.1.call-update
  10.2 0.0 all-gather.9.cloned.1.call-start
  10.3 0.0 copy-done.2
  10.3 2.5 fusion.17
  12.8 0.0 copy-start.3
  12.8 0.0 all-gather.9.cloned.1.call-update
  12.8 0.0 all-gather.7.cloned.1.call-start
  12.9 2.1 fusion.26
  15.0 0.0 all-gather.7.cloned.1.call-update
  15.0 0.0 all-gather.5.cloned.1.call-start
  15.1 1.9 fusion.35
  17.0 0.0 all-gather.5.cloned.1.call-update
  17.0 0.0 copy-done.3
  17.0 0.3 copy.17
  17.3 3.0 %collective-permute-start = (bf16[768,512]{1,0:T(8,128)(2,1)S(1)}, bf16[768,512]{1,0:T(8,128)(2,1)S(1)}, u32[]{:S(2)}, u32[]{:S(2)}) collective-permute-start(bf16[768,512]{1,0:T(8,128)(2,1)S(1)} %bitcast.8), channel_id=1, source_target_pairs={{0,1},{1,0},{2,3},{3,2},{4,5},{5,4},{6,7},{7,6},{8,9},{9,8},{10,11... | collective-permute-start | bytes 2359304 | tf_op jit(solution)/shard_map/ppermute | solution.py:171
  20.3 3.5 %slice.30.w_ref = bf16[768,1536]{1,0:T(8,128)(2,1)} slice(bf16[768,12288]{1,0:T(8,128)(2,1)} %refs_2_.5), slice={[0:768], [10752:12288]} | slice | bytes 4718592 | tf_op jit(solution)/shard_map/slice | solution.py:138
  23.9 0.2 broadcast_in_dim.7
  24.0 0.1 constant_dynamic-update-slice_fusion.1
  24.2 13.7 %collective-permute-done = bf16[768,512]{1,0:T(8,128)(2,1)S(1)} collective-permute-done((bf16[768,512]{1,0:T(8,128)(2,1)S(1)}, bf16[768,512]{1,0:T(8,128)(2,1)S(1)}, u32[]{:S(2)}, u32[]{:S(2)}) %collective-permute-start) | collective-permute-done | bytes 786464 | tf_op jit(solution)/shard_map/ppermute | solution.py:171
  37.9 0.1 constant_dynamic-update-slice_fusion.refs_0_
  38.0 0.0 copy-start
  38.0 57.0 %all-gather.11.cloned.1.call-done.refs_1_ = bf16[1024,4608]{1,0:T(8,128)(2,1)} async-done(((bf16[64,4608]{1,0:T(8,128)(2,1)}), bf16[1024,4608]{1,0:T(8,128)(2,1)}) %all-gather.11.cloned.1.call-update) | async-done | bytes 9437200 | tf_op jit(solution)/shard_map/all_gather | solution.py:165
  95.0 0.0 copy-done
  95.0 29.6 %chunk.4 = (bf16[768,12288]{1,0:T(8,128)(2,1)}, bf16[768,12288]{1,0:T(8,128)(2,1)}, bf16[768,12288]{1,0:T(8,128)(2,1)}, f32[1024,768]{1,0:T(8,128)}) custom-call(bf16[768,1024]{1,0:T(8,128)(2,1)} %copy-done, bf16[1024,4608]{1,0:T(8,128)(2,1)} %all-gather.11.cloned.1.call-done.refs_1_, bf16[768,12288]{1,0:T(8,128)(2,1)} %refs_2_.5), custom_call_target="tpu_custom_call" | custom-call | flops 19931332608 | bytes 37748736 | tf_op jit(solution)/shard_map/chunk/pallas_call | solution.py:98
  124.6 42.5 %all-gather.9.cloned.1.call-done.refs_1_ = bf16[1024,3840]{1,0:T(8,128)(2,1)} async-done(((bf16[64,3840]{1,0:T(8,128)(2,1)}), bf16[1024,3840]{1,0:T(8,128)(2,1)}) %all-gather.9.cloned.1.call-update) | async-done | bytes 7864336 | tf_op jit(solution)/shard_map/all_gather | solution.py:165
  167.1 26.8 %chunk.5 = (bf16[768,12288]{1,0:T(8,128)(2,1)}, bf16[768,12288]{1,0:T(8,128)(2,1)}, bf16[768,12288]{1,0:T(8,128)(2,1)}, f32[1024,768]{1,0:T(8,128)}) custom-call(bf16[768,1024]{1,0:T(8,128)(2,1)} %copy-done, bf16[1024,3840]{1,0:T(8,128)(2,1)} %all-gather.9.cloned.1.call-done.refs_1_, ...), custom_call_target="tpu_custom_call", output_to_operand_aliasing={{0}: (4, {}), {1}: (5, {}), {2}: (6, {})} | custom-call | flops 16609443840 | bytes 31457280 | tf_op jit(solution)/shard_map/chunk/pallas_call | solution.py:98
  193.9 27.1 %all-gather.7.cloned.1.call-done.refs_1_ = bf16[1024,2304]{1,0:T(8,128)(2,1)} async-done(((bf16[64,2304]{1,0:T(8,128)(2,1)}), bf16[1024,2304]{1,0:T(8,128)(2,1)}) %all-gather.7.cloned.1.call-update) | async-done | bytes 4718608 | tf_op jit(solution)/shard_map/all_gather | solution.py:165
  221.0 18.5 %chunk.6 = (bf16[768,12288]{1,0:T(8,128)(2,1)}, bf16[768,12288]{1,0:T(8,128)(2,1)}, bf16[768,12288]{1,0:T(8,128)(2,1)}, f32[1024,768]{1,0:T(8,128)}) custom-call(bf16[768,1024]{1,0:T(8,128)(2,1)} %copy-done, bf16[1024,2304]{1,0:T(8,128)(2,1)} %all-gather.7.cloned.1.call-done.refs_1_, ...), custom_call_target="tpu_custom_call", output_to_operand_aliasing={{0}: (4, {}), {1}: (5, {}), {2}: (6, {})} | custom-call | flops 9965666304 | bytes 18874368 | tf_op jit(solution)/shard_map/chunk/pallas_call | solution.py:98
  239.5 27.4 %all-gather.5.cloned.1.call-done.hg_ref.refs_1_ = bf16[1024,1536]{1,0:T(8,128)(2,1)} async-done(((bf16[64,1536]{1,0:T(8,128)(2,1)}), bf16[1024,1536]{1,0:T(8,128)(2,1)}) %all-gather.5.cloned.1.call-update) | async-done | bytes 3145744 | tf_op jit(solution)/shard_map/all_gather | solution.py:165
  266.9 5.1 %share.3 = bf16[1,512,768]{2,1,0:T(8,128)(2,1)} custom-call(s32[1]{0:T(128)S(6)} %select_n.22._, bf16[1024,1536]{1,0:T(8,128)(2,1)} %all-gather.5.cloned.1.call-done.hg_ref.refs_1_, bf16[768,1536]{1,0:T(8,128)(2,1)} %slice.30.w_ref, f32[1024,768]{1,0:T(8,128)} %get-tuple-element.27.acc_ref), custom_call_target="tpu_custom_call" | custom-call | flops 1207959552 | bytes 6291456 | tf_op jit(solution)/shard_map/share/pallas_call | solution.py:139
  272.0 1.5 collective-permute-start.1
  273.5 5.3 %share.2 = f32[1,512,768]{2,1,0:T(8,128)} custom-call(s32[1]{0:T(128)} %bitcast._, bf16[1024,1536]{1,0:T(8,128)(2,1)} %all-gather.5.cloned.1.call-done.hg_ref.refs_1_, bf16[768,1536]{1,0:T(8,128)(2,1)} %slice.30.w_ref, f32[1024,768]{1,0:T(8,128)} %get-tuple-element.27.acc_ref), custom_call_target="tpu_custom_call" | custom-call | flops 1207959552 | bytes 6291456 | tf_op jit(solution)/shard_map/share/pallas_call | solution.py:139
  278.8 0.0 copy-start.1
  278.8 9.5 %chunk.7 = (bf16[768,12288]{1,0:T(8,128)(2,1)}, bf16[768,12288]{1,0:T(8,128)(2,1)}, bf16[768,12288]{1,0:T(8,128)(2,1)}) custom-call(bf16[768,1024]{1,0:T(8,128)(2,1)} %copy-done, bf16[1024,1536]{1,0:T(8,128)(2,1)} %all-gather.5.cloned.1.call-done.hg_ref.refs_1_, ...), custom_call_target="tpu_custom_call", output_to_operand_aliasing={{0}: (2, {}), {1}: (3, {}), {2}: (4, {})} | custom-call | flops 4227858432 | bytes 12582912 | tf_op jit(solution)/shard_map/chunk/pallas_call | solution.py:98
  288.3 3.6 %collective-permute-done.1 = bf16[512,768]{1,0:T(8,128)(2,1)S(1)} collective-permute-done((bf16[512,768]{1,0:T(8,128)(2,1)}, bf16[512,768]{1,0:T(8,128)(2,1)S(1)}, u32[]{:S(2)}, u32[]{:S(2)}) %collective-permute-start.1) | collective-permute-done | bytes 786464 | tf_op jit(solution)/shard_map/ppermute | solution.py:183
  291.9 0.0 copy-done.1
  291.9 1.0 fusion
Async XLA Ops:
  7.2 3.1 %copy-start.2 = (bf16[64,12288]{1,0:T(8,128)(2,1)S(1)}, bf16[64,12288]{1,0:T(8,128)(2,1)}, u32[]{:S(2)}) copy-start(bf16[64,12288]{1,0:T(8,128)(2,1)} %param.6) | copy-start | bytes 4718596
  7.2 87.9 %all-gather.11.cloned.1.call-start = ((), (), s32[]{:S(2)}) async-start(), calls=%async_computation.3 | async-start | bytes 10027008 | tf_op jit(solution)/shard_map/all_gather | solution.py:165
  10.2 156.8 %all-gather.9.cloned.1.call-start = ((), (), s32[]{:S(2)}) async-start(), calls=%async_computation.2 | async-start | bytes 8355840 | tf_op jit(solution)/shard_map/all_gather | solution.py:165
  12.8 4.2 %copy-start.3 = (bf16[512,768]{1,0:T(8,128)(2,1)S(1)}, bf16[512,768]{1,0:T(8,128)(2,1)}, u32[]{:S(2)}) copy-start(bf16[512,768]{1,0:T(8,128)(2,1)} %param.4) | copy-start | bytes 2359300
  12.8 208.1 %all-gather.7.cloned.1.call-start = ((), (), s32[]{:S(2)}) async-start(), calls=%async_computation.1 | async-start | bytes 5013504 | tf_op jit(solution)/shard_map/all_gather | solution.py:165
  15.0 251.8 %all-gather.5.cloned.1.call-start = ((), (), s32[]{:S(2)}) async-start(), calls=%async_computation | async-start | bytes 3342336 | tf_op jit(solution)/shard_map/all_gather | solution.py:165
  17.3 20.6 %collective-permute-start = (bf16[768,512]{1,0:T(8,128)(2,1)S(1)}, bf16[768,512]{1,0:T(8,128)(2,1)S(1)}, u32[]{:S(2)}, u32[]{:S(2)}) collective-permute-start(bf16[768,512]{1,0:T(8,128)(2,1)S(1)} %bitcast.8), channel_id=1, source_target_pairs={{0,1},{1,0},{2,3},{3,2},{4,5},{5,4},{6,7},{7,6},{8,9},{9,8},{10,11... | collective-permute-start | bytes 2359304 | tf_op jit(solution)/shard_map/ppermute | solution.py:171
  38.0 57.1 %copy-start = (bf16[768,1024]{1,0:T(8,128)(2,1)}, bf16[768,1024]{1,0:T(8,128)(2,1)S(1)}, u32[]{:S(2)}) copy-start(bf16[768,1024]{1,0:T(8,128)(2,1)S(1)} %constant_dynamic-update-slice_fusion.refs_0_) | copy-start | bytes 4718596
  272.0 19.9 %collective-permute-start.1 = (bf16[512,768]{1,0:T(8,128)(2,1)}, bf16[512,768]{1,0:T(8,128)(2,1)S(1)}, u32[]{:S(2)}, u32[]{:S(2)}) collective-permute-start(bf16[512,768]{1,0:T(8,128)(2,1)} %bitcast.9), channel_id=1, source_target_pairs={{0,1},{1,0},{2,3},{3,2},{4,5},{5,4},{6,7},{7,6},{8,9},{9,8},{10,11... | collective-permute-start | bytes 2359304 | tf_op jit(solution)/shard_map/ppermute | solution.py:183
  278.8 13.1 %copy-start.1 = (f32[1,512,768]{2,1,0:T(8,128)S(1)}, f32[1,512,768]{2,1,0:T(8,128)}, u32[]{:S(2)}) copy-start(f32[1,512,768]{2,1,0:T(8,128)} %share.2) | copy-start | bytes 4718596
Sparse Core Ops, SparseCore 0:
  10.9 84.1 all-gather.10
  97.3 69.6 all-gather.8
  169.4 51.5 all-gather.6
  223.1 43.7 all-gather.4

commit v2 on v0

v2 whole, which is shorter than its diff:
```python
import functools
import math

import jax
import jax.numpy as jnp
import numpy as np
from jax import lax
from jax.experimental import pallas as pl
from jax.experimental.pallas import tpu as pltpu
from jax.sharding import PartitionSpec as P

BLOCK = 384
STEP = 2 * BLOCK
CHUNKS = (1, 2, 2, 2, 1)
VMEM_LIMIT = 60 * 1024 * 1024
ANYWHERE = pl.BlockSpec(memory_space=pltpu.HBM)
TICK = jax.ShapeDtypeStruct((8, 128), jnp.float32)
NT = (((1,), (1,)), ((), ()))
TN = (((0,), (0,)), ((), ()))


def gelu_slope(value):
    coeff = math.sqrt(2.0 / math.pi)
    inner = coeff * (value + 0.044715 * value * value * value)
    tanh_u = jnp.tanh(inner)
    return 0.5 * (1.0 + tanh_u) + 0.5 * value * (1.0 - tanh_u * tanh_u) * coeff * (
        1.0 + 3.0 * 0.044715 * value * value
    )


def plan(steps):
    pairs, total = steps // 2, sum(CHUNKS)
    bounds, done = [0], 0
    for share in CHUNKS:
        done += share
        bounds.append(round(pairs * done / total))
    return [(2 * a, 2 * (b - a)) for a, b in zip(bounds, bounds[1:]) if b > a]


def gate_kernel(*refs):
    del refs


def gate_call(pieces, ticks):
    count = len(pieces)
    result = pl.pallas_call(
        gate_kernel,
        in_specs=[ANYWHERE] * (count + len(ticks)),
        out_specs=[ANYWHERE] * (count + 1),
        out_shape=[jax.ShapeDtypeStruct(p.shape, p.dtype) for p in pieces] + [TICK],
        input_output_aliases={i: i for i in range(count)},
        name="gate",
    )(*pieces, *ticks)
    return result[:count], result[count]


def merge_kernel(count, place_ref, *refs):
    pieces, (out_ref, sems) = refs[:count], refs[-2:]
    copies = []
    for k, piece in enumerate(pieces):
        rows = piece.shape[0]
        at = pl.multiple_of(place_ref[k], rows)
        copies.append(pltpu.make_async_copy(piece, out_ref.at[pl.ds(at, rows), :], sems.at[k]))
        copies[-1].start()
    for copy in copies:
        copy.wait()


def merge_call(places, pieces, ticks):
    count = len(pieces)
    tokens = sum(piece.shape[0] for piece in pieces)
    width = pieces[0].shape[1]
    return pl.pallas_call(
        functools.partial(merge_kernel, count),
        grid_spec=pltpu.PrefetchScalarGridSpec(
            num_scalar_prefetch=1,
            grid=(1,),
            in_specs=[ANYWHERE] * (count + len(ticks)),
            out_specs=ANYWHERE,
            scratch_shapes=[pltpu.SemaphoreType.DMA((count,))],
        ),
        out_shape=jax.ShapeDtypeStruct((tokens, width), pieces[0].dtype),
        cost_estimate=pl.CostEstimate(
            flops=0, bytes_accessed=4 * tokens * width, transcendentals=0
        ),
        name="merge",
    )(places, *pieces, *ticks)


def chunk_kernel(scale, halves, half_steps, with_share, first, n_ticks, off_ref, *refs):
    refs = list(refs)
    xt_ref = refs.pop(0)
    hg_refs = [refs.pop(0) for _ in range(halves)]
    w_ref = refs.pop(0) if with_share else None
    acc_in = refs.pop(0) if with_share and not first else None
    del refs[:n_ticks]
    if not first:
        del refs[:3]
    wg_ref, left_ref, right_ref, tick_ref = refs[:4]
    refs = refs[4:]
    step, steps = pl.program_id(0), halves * half_steps
    if with_share:
        acc_out, acc_ref, in_sem, out_sem = refs

    @pl.when(step == 0)
    def _():
        tick_ref[...] = jnp.zeros_like(tick_ref)
        if with_share:
            if first:
                acc_ref[...] = jnp.zeros_like(acc_ref)
            else:
                pltpu.make_async_copy(acc_in, acc_ref, in_sem).start()

    def work(hg_ref):
        grad = jnp.dot(xt_ref[...], hg_ref[...], preferred_element_type=jnp.float32)
        wg_ref[...] = grad.astype(wg_ref.dtype)

        if with_share:
            if not first:

                @pl.when(step == 0)
                def _():
                    pltpu.make_async_copy(acc_in, acc_ref, in_sem).wait()

            acc_ref[...] += lax.dot_general(
                hg_ref[...], w_ref[...], NT, preferred_element_type=jnp.float32
            )

            @pl.when(step == steps - 1)
            def _():
                pltpu.make_async_copy(acc_ref, acc_out, out_sem).start()

    if halves == 1:
        work(hg_refs[0])
    else:
        for k in range(halves):
            pl.when(step // half_steps == k)(functools.partial(work, hg_refs[k]))

    rows, cols = wg_ref.shape
    for i in range(rows // BLOCK):
        for j in range(cols // BLOCK):
            at = (pl.ds(i * BLOCK, BLOCK), pl.ds(j * BLOCK, BLOCK))
            tile = wg_ref[at]
            left = lax.dot_general(tile, tile, NT, preferred_element_type=jnp.float32)
            left_ref[at] = (left * scale).astype(left_ref.dtype)
            right = lax.dot_general(tile, tile, TN, preferred_element_type=jnp.float32)
            right_ref[at] = (right * scale).astype(right_ref.dtype)

    if with_share:

        @pl.when(step == steps - 1)
        def _():
            pltpu.make_async_copy(acc_ref, acc_out, out_sem).wait()


def chunk_call(scale, offs, x_t, hgs, weight, acc, outs, ticks, with_share):
    rows, tokens = x_t.shape
    halves, half_steps = len(hgs), hgs[0].shape[1] // STEP
    first = outs is None

    def at(s, off):
        return (0, off[s // half_steps] + s % half_steps)

    def part(k):
        return lambda s, off: (0, jnp.clip(s - k * half_steps, 0, half_steps - 1))

    args = [x_t] + hgs
    in_specs = [pl.BlockSpec((rows, tokens), lambda s, off: (0, 0))]
    in_specs += [pl.BlockSpec((tokens, STEP), part(k)) for k in range(halves)]
    out_shape = [jax.ShapeDtypeStruct(weight.shape, jnp.bfloat16)] * 3 + [TICK]
    out_specs = [pl.BlockSpec((rows, STEP), at)] * 3
    out_specs.append(pl.BlockSpec(TICK.shape, lambda s, off: (0, 0)))
    scratch = []
    aliases = {}
    if with_share:
        args.append(weight)
        in_specs.append(pl.BlockSpec((rows, STEP), at))
        out_shape.append(jax.ShapeDtypeStruct((tokens, rows), jnp.float32))
        out_specs.append(ANYWHERE)
        scratch += [
            pltpu.VMEM((tokens, rows), jnp.float32),
            pltpu.SemaphoreType.DMA,
            pltpu.SemaphoreType.DMA,
        ]
        if not first:
            args.append(acc)
            in_specs.append(ANYWHERE)
    args += ticks
    in_specs += [ANYWHERE] * len(ticks)
    if not first:
        aliases = {1 + len(args) + i: i for i in range(3)}
        args += list(outs)
        in_specs += [ANYWHERE] * 3
    cells = halves * half_steps * STEP * rows
    return pl.pallas_call(
        functools.partial(
            chunk_kernel, scale, halves, half_steps, with_share, first, len(ticks)
        ),
        grid_spec=pltpu.PrefetchScalarGridSpec(
            num_scalar_prefetch=1,
            grid=(halves * half_steps,),
            in_specs=in_specs,
            out_specs=out_specs,
            scratch_shapes=scratch,
        ),
        out_shape=out_shape,
        input_output_aliases=aliases,
        compiler_params=pltpu.CompilerParams(vmem_limit_bytes=VMEM_LIMIT),
        cost_estimate=pl.CostEstimate(
            flops=cells * (2 * tokens * (2 if with_share else 1) + 4 * BLOCK),
            bytes_accessed=8 * cells + 2 * halves * half_steps * STEP * tokens,
            transcendentals=0,
        ),
        name="chunk",
    )(offs, *args)


def share_kernel(groups, group, half_steps, who_ref, off_ref, *refs):
    own_hg, other_hg, w_ref, acc_ref, away_ref, own_ref, sum_ref = refs
    step = pl.program_id(0)

    @pl.when(step == 0)
    def _():
        sum_ref[...] = acc_ref[...]

    for k, hg_ref in enumerate((own_hg, other_hg)):

        @pl.when(step // half_steps == k)
        def _(hg_ref=hg_ref):
            sum_ref[...] += lax.dot_general(
                hg_ref[...], w_ref[...], NT, preferred_element_type=jnp.float32
            )

    @pl.when(step == 2 * half_steps - 1)
    def _():
        for k in range(groups):
            at = pl.multiple_of(who_ref[k] * group, group)
            part = sum_ref[pl.ds(at, group), :]
            if k:
                away_ref[k - 1] = part.astype(away_ref.dtype)
            else:
                own_ref[...] = part


def share_call(who, offs, hgs, weight, acc, groups):
    tokens, rows = acc.shape
    group = tokens // groups
    half_steps = hgs[0].shape[1] // STEP

    def part(k):
        return lambda s, who, off: (0, jnp.clip(s - k * half_steps, 0, half_steps - 1))

    return pl.pallas_call(
        functools.partial(share_kernel, groups, group, half_steps),
        grid_spec=pltpu.PrefetchScalarGridSpec(
            num_scalar_prefetch=2,
            grid=(2 * half_steps,),
            in_specs=[
                pl.BlockSpec((tokens, STEP), part(0)),
                pl.BlockSpec((tokens, STEP), part(1)),
                pl.BlockSpec(
                    (rows, STEP),
                    lambda s, who, off: (0, off[s // half_steps] + s % half_steps),
                ),
                pl.BlockSpec((tokens, rows), lambda s, *_: (0, 0)),
            ],
            out_specs=[
                pl.BlockSpec((groups - 1, group, rows), lambda s, *_: (0, 0, 0)),
                pl.BlockSpec((group, rows), lambda s, *_: (0, 0)),
            ],
            scratch_shapes=[pltpu.VMEM((tokens, rows), jnp.float32)],
        ),
        out_shape=[
            jax.ShapeDtypeStruct((groups - 1, group, rows), jnp.bfloat16),
            jax.ShapeDtypeStruct((group, rows), jnp.float32),
        ],
        compiler_params=pltpu.CompilerParams(vmem_limit_bytes=VMEM_LIMIT),
        cost_estimate=pl.CostEstimate(
            flops=4 * tokens * half_steps * STEP * rows,
            bytes_accessed=4 * half_steps * STEP * (rows + tokens) + 8 * tokens * rows,
            transcendentals=0,
        ),
        name="share",
    )(who, offs, *hgs, weight, acc)


class Ring:
    def __init__(self, size):
        self.chips = size // 2
        self.order = list(range(0, self.chips, 2)) + list(range(1, self.chips, 2))[::-1]
        self.hops = self.chips // 2

    def shift(self, value, by):
        pairs = []
        for k, chip in enumerate(self.order):
            to = self.order[(k + by) % self.chips]
            pairs += [(2 * chip + core, 2 * to + core) for core in range(2)]
        return lax.ppermute(value, "row", pairs)

    def swap(self, value):
        return lax.ppermute(value, "row", [(i, i ^ 1) for i in range(2 * self.chips)])

    def places(self, rows_each):
        table = []
        for row in range(2 * self.chips):
            pos = self.order.index(row // 2)
            base = lambda by: self.order[(pos + by) % self.chips] * rows_each
            line = [base(0)]
            for hop in range(1, self.hops):
                line += [base(-hop), base(hop)]
            line += [base(-self.hops), base(self.hops) + rows_each // 2]
            table.append(line)
        return jnp.asarray(np.array(table, np.int32))[lax.axis_index("row")]


class Stream:
    def __init__(self, ring, piece):
        self.ring, self.fresh, self.kept, self.hop = ring, [piece], [], 0

    def advance(self):
        ring = self.ring
        self.kept += self.fresh
        ahead, behind = (self.fresh * 2)[:2]
        self.hop += 1
        if self.hop == ring.hops:
            half = ahead.shape[0] // 2
            ahead, behind = ahead[:half], behind[half:]
        self.fresh = [ring.shift(ahead, 1), ring.shift(behind, -1)]

    def gate(self, ticks):
        self.fresh, tick = gate_call(self.fresh, ticks)
        return tick

    def pieces(self):
        return self.kept + self.fresh


def on_device(row_size, cols, tokens, weight, pre_act, out_grad):
    me, core = lax.axis_index("col"), lax.axis_index("row") % 2
    group, rows = tokens.shape
    num_tokens = group * cols
    scale = 1.0 / (BLOCK * num_tokens)
    chunks = plan(weight.shape[1] // STEP)
    ring = Ring(row_size)
    places = ring.places(2 * pre_act.shape[0])

    def hidden_of(start, width):
        h = lax.dynamic_slice_in_dim(pre_act, start, width, 1).astype(jnp.float32)
        g = lax.dynamic_slice_in_dim(out_grad, start, width, 1).astype(jnp.float32)
        return (g * gelu_slope(h)).astype(jnp.bfloat16)

    def stream_of(chunk):
        first, half = chunk[0] * STEP, chunk[1] * STEP // 2
        got = ring.swap(hidden_of(first + (1 - core) * half, half))
        mine = hidden_of(first + core * half, half)
        upper, lower = jnp.where(core == 0, mine, got), jnp.where(core == 0, got, mine)
        return Stream(ring, jnp.concatenate([upper, lower], axis=0))

    streams = [stream_of(chunk) for chunk in chunks]
    offsets = [
        jnp.stack([a + core * (n // 2), a + (1 - core) * (n // 2)]).astype(jnp.int32)
        for a, n in chunks
    ]

    own_t = tokens.T
    x_t = jnp.zeros((rows, num_tokens), jnp.bfloat16)
    x_t = lax.dynamic_update_slice(x_t, own_t, (0, me * group))
    for s in range(1, cols):
        piece = lax.ppermute(own_t, "col", [(i, (i + s) % cols) for i in range(cols)])
        x_t = lax.dynamic_update_slice(x_t, piece, (0, (me - s) % cols * group))

    def advance(k, upto, ticks):
        out = []
        if k < len(streams):
            while streams[k].hop < upto:
                if ticks:
                    out = [streams[k].gate(ticks)]
                streams[k].advance()
        return out

    half, last = ring.hops // 2, len(chunks) - 1
    advance(0, half, [])
    if last:
        advance(0, half + 1, [streams[1].fresh[0]])
    advance(1, half, [])
    advance(0, ring.hops, [])
    acc, outs, ticks = None, None, []
    for k in range(len(chunks)):
        seen = advance(k + 1, half + 1, ticks) + advance(k + 2, 1, ticks)
        own = merge_call(places, streams[k].pieces(), seen)
        other = ring.swap(own)
        offs = offsets[k]
        if k < last:
            *outs, tick, acc = chunk_call(
                scale, offs[:1], x_t, [own], weight, acc, outs, seen, True
            )
            seen = advance(k + 1, ring.hops, [tick]) + advance(k + 2, half, [tick])
            *outs, tick, acc = chunk_call(
                scale, offs[1:], x_t, [other], weight, acc, outs, seen, True
            )
            ticks = [tick]
    who = (me + jnp.arange(cols, dtype=jnp.int32)) % cols
    away, share = share_call(who, offs, [own, other], weight, acc, cols)
    arrived = [
        lax.ppermute(away[s - 1], "col", [(i, (i + s) % cols) for i in range(cols)])
        for s in range(1, cols)
    ]
    *outs, tick = chunk_call(
        scale, offs, x_t, [own, other], weight, None, outs, [share], False
    )
    for piece in arrived:
        share = share + piece.astype(jnp.float32)
    return (share.astype(jnp.bfloat16), *outs)


def solution(mesh):
    in_specs = (P("col", "row"), P("row", "col"), P("row", "col"), P("row", "col"))
    out_specs = (P("col", "row"), P("row", "col"), P("row", "col"), P("row", "col"))
    return jax.shard_map(
        functools.partial(on_device, mesh.shape["row"], mesh.shape["col"]),
        mesh=mesh,
        in_specs=in_specs,
        out_specs=out_specs,
        check_vma=False,
    )
```

time: 567 us -> 657 us (1.16)
  Pallas kernels: 0 us -> 516 us
  matrix products: 250 us -> 0 us
  local copies, waits for them, and re-layouts: 159 us -> 29.3 us
  waiting for transfers between devices: 134 us -> 39.2 us
  starting transfers between devices: 0.12 us -> 47.1 us
  between operations: 13.7 us -> 1.51 us
  other arithmetic: 6.82 us -> 15.6 us
    pallas_call x0 -> x28, Pallas kernels: none -> 516 us  [the longest x5 391 us: merge_call(): pl.pallas_call(functools.partial(merge_kernel, count), grid_spec=pltpu.Pr...]
    dot_general x4 -> x0, matrix products: 250 us -> none  [the longest x1 99.8 us: on_device(): jnp.einsum('ipjq,irjq->ipjr', tiles, tiles, precision=lax.Precision.HIGHEST)]
    all_gather x2 -> x0, waiting for transfers between devices: 133 us -> none  [the longest x1 131 us: on_device(): grad_all = lax.all_gather(hidden_grad, 'row', axis=0, tiled=True)]
    convert_element_type x2 -> x0, local copies, waits for them, and re-layouts: 49 us -> none  [the longest x1 24.5 us: on_device(): left_stats = left.reshape(rows_here, cols_here).astype(jnp.bfloat16)]
    unnamed x3 -> x75, local copies, waits for them, and re-layouts: 65.2 us -> 16.3 us
    ppermute x0 -> x52, starting transfers between devices: none -> 47.1 us  [the longest x40 42 us: shift(): return lax.ppermute(value, 'row', pairs)]
    reshape x1 -> x0, local copies, waits for them, and re-layouts: 45 us -> none  [on_device(): weight_sum.reshape(rows_here // BLOCK, BLOCK, cols_here // BLOCK, BLOCK)]
    ppermute x0 -> x52, waiting for transfers between devices: none -> 39.2 us  [the longest x40 30.3 us: shift(): return lax.ppermute(value, 'row', pairs)]
  transfers between devices with their start and end apart: 3 -> 52, of which waited for: 2 -> 10; matrix products, arithmetic and copies ran while one was open for 73% -> 4% of each run, Pallas kernels for 0% -> 33%
where the time goes in v2:
time: 657 us; the launch traced here: 649 us
  Pallas kernels  516 us (79%)
  starting transfers between devices  47.1 us (7%)
  waiting for transfers between devices  39.2 us (6%)
  local copies, waits for them, and re-layouts  29.3 us (4%)
  other arithmetic  15.6 us (2%)
    pallas_call x5, Pallas kernels, merge_call(): pl.pallas_call(functools.partial(merge_kernel, count), grid_spec=pltpu.Pr...  391 us
    pallas_call x9, Pallas kernels, chunk_call(): pl.pallas_call(functools.partial(chunk_kernel, scale, halves, half_steps,...  117 us
    ppermute x40, starting transfers between devices, shift(): return lax.ppermute(value, 'row', pairs)  42 us
    ppermute x40, waiting for transfers between devices, shift(): return lax.ppermute(value, 'row', pairs)  30.3 us
    unnamed x75, local copies, waits for them, and re-layouts  16.3 us
  transfers between devices with their start and end apart: 52, of which 10 were waited for; matrix products, arithmetic and copies ran while one was open for 4% of the time, Pallas kernels for 33%

profile of v2, /device:TPU:0, one launch (start us, length us, event | category | flops | bytes accessed | tf_op | source)
XLA Modules:
  0.0 648.9 jit_solution(17674447315218269474)
XLA Ops:
  0.7 1.4 fusion.88
  2.7 2.9 fusion.52
  6.5 1.4 copy.57
  8.0 2.7 collective-permute-start.1
  10.6 1.9 broadcast_select_fusion.7
  12.6 1.6 collective-permute-start.10
  14.7 2.8 broadcast_select_fusion.1
  17.5 2.1 collective-permute-done.10.refs_1_
  19.7 1.6 collective-permute-start.12
  22.5 3.4 collective-permute-done.12.refs_0_
  25.9 1.3 collective-permute-done.13.refs_1_
  27.9 1.6 collective-permute-start.14
  30.3 3.6 collective-permute-done.14.refs_5_
  33.9 1.6 collective-permute-start.16
  36.0 1.2 fusion.91.place_ref
  37.3 1.6 collective-permute-start.3
  40.2 1.1 collective-permute-done.17.refs_8_
  41.4 49.5 %merge.5.refs_1_ = bf16[1024,768]{1,0:T(8,128)(2,1)} custom-call(s32[9]{0:T(128)} %fusion.91.place_ref, bf16[128,768]{1,0:T(8,128)(2,1)} %copy-done.22, bf16[128,768]{1,0:T(8,128)(2,1)} %copy-done.32, bf16[128,768]{1,0:T(8,128)(2,1)} %copy-done.33, bf16[128,768]{1,0:T(8,128)(2,1)} %get-tuple-element.84.refs_3_, bf16[128,768]{1,0:T(8,128)(2,1)} %get-tuple-element.85.refs_4_, ...), custom_call_target="tpu_custom_call" | custom-call | bytes 3145728 | tf_op jit(solution)/shard_map/merge/pallas_call | solution.py:73
  91.1 1.6 collective-permute-start.21
  92.7 1.5 collective-permute-start.5
  95.9 1.2 constant_dynamic-update-slice_fusion.refs_0_
  97.1 14.2 %collective-permute-done.5.refs_3_ = bf16[128,1536]{1,0:T(8,128)(2,1)} collective-permute-done((bf16[128,1536]{1,0:T(8,128)(2,1)}, bf16[128,1536]{1,0:T(8,128)(2,1)}, u32[]{:S(2)}, u32[]{:S(2)}) %collective-permute-start.5) | collective-permute-done | bytes 393248 | tf_op jit(solution)/shard_map/ppermute | solution.py:298
  111.3 1.6 collective-permute-start.7
  113.3 8.3 %chunk.9 = (bf16[768,12288]{1,0:T(8,128)(2,1)}, bf16[768,12288]{1,0:T(8,128)(2,1)}, bf16[768,12288]{1,0:T(8,128)(2,1)}, f32[8,128]{1,0:T(8,128)}, f32[1024,768]{1,0:T(8,128)}) custom-call(s32[1]{0:T(128)} %bitcast.5.off_ref, bf16[768,1024]{1,0:T(8,128)(2,1)} %copy-done, bf16[1024,768]{1,0:T(8,128)(2,1)} %merge.5.refs_1_, bf16[768,12288]{1,0:T(8,128)(2,1)} %refs_2_.17), custom_call_target="tpu_custom_call" | custom-call | flops 3321888768 | bytes 6291456 | tf_op jit(solution)/shard_map/chunk/pallas_call | solution.py:195
  122.6 1.6 collective-permute-start.23
  127.0 0.9 slice.32
  127.9 1.6 collective-permute-start.18
  129.5 0.9 slice.33
  131.2 9.4 %chunk.10 = (bf16[768,12288]{1,0:T(8,128)(2,1)}, bf16[768,12288]{1,0:T(8,128)(2,1)}, bf16[768,12288]{1,0:T(8,128)(2,1)}, f32[8,128]{1,0:T(8,128)}, f32[1024,768]{1,0:T(8,128)}) custom-call(s32[1]{0:T(128)} %bitcast.6.off_ref, bf16[768,1024]{1,0:T(8,128)(2,1)} %copy-done, ...), custom_call_target="tpu_custom_call", output_to_operand_aliasing={{0}: (7, {}), {1}: (8, {}), {2}: (9, {})} | custom-call | flops 3321888768 | bytes 6291456 | tf_op jit(solution)/shard_map/chunk/pallas_call | solution.py:195
  142.9 97.3 %merge.6.refs_1_ = bf16[1024,1536]{1,0:T(8,128)(2,1)} custom-call(s32[9]{0:T(128)} %fusion.91.place_ref, bf16[128,1536]{1,0:T(8,128)(2,1)} %pad_maximum_fusion.refs_2_.refs_0_, bf16[128,1536]{1,0:T(8,128)(2,1)} %collective-permute-done.3.refs_1_, bf16[128,1536]{1,0:T(8,128)(2,1)} %collective-permute-done.4.refs_2_, ...), custom_call_target="tpu_custom_call" | custom-call | bytes 6291456 | tf_op jit(solution)/shard_map/merge/pallas_call | solution.py:73
  240.3 0.9 broadcast_select_fusion.8
  241.2 1.6 pad_maximum_fusion.3.refs_0_
  242.8 1.6 collective-permute-start.30
  244.8 1.6 collective-permute-start.28
  246.8 14.8 %chunk.11 = (bf16[768,12288]{1,0:T(8,128)(2,1)}, bf16[768,12288]{1,0:T(8,128)(2,1)}, bf16[768,12288]{1,0:T(8,128)(2,1)}, f32[8,128]{1,0:T(8,128)}, f32[1024,768]{1,0:T(8,128)}) custom-call(s32[1]{0:T(128)} %bitcast.7.off_ref, bf16[768,1024]{1,0:T(8,128)(2,1)} %copy-done, ...), custom_call_target="tpu_custom_call", output_to_operand_aliasing={{0}: (7, {}), {1}: (8, {}), {2}: (9, {})} | custom-call | flops 6643777536 | bytes 12582912 | tf_op jit(solution)/shard_map/chunk/pallas_call | solution.py:195
  262.4 1.6 collective-permute-start.36
  264.5 1.6 slice.34
  266.1 1.6 collective-permute-start.34
  267.7 1.6 slice.35
  270.0 1.6 copy-done.5
  271.6 14.7 %chunk.12 = (bf16[768,12288]{1,0:T(8,128)(2,1)}, bf16[768,12288]{1,0:T(8,128)(2,1)}, bf16[768,12288]{1,0:T(8,128)(2,1)}, f32[8,128]{1,0:T(8,128)}, f32[1024,768]{1,0:T(8,128)}) custom-call(s32[1]{0:T(128)} %bitcast.3.off_ref, bf16[768,1024]{1,0:T(8,128)(2,1)} %copy-done, ...), custom_call_target="tpu_custom_call", output_to_operand_aliasing={{0}: (7, {}), {1}: (8, {}), {2}: (9, {})} | custom-call | flops 6643777536 | bytes 12582912 | tf_op jit(solution)/shard_map/chunk/pallas_call | solution.py:195
  287.1 97.1 %merge.7.refs_1_ = bf16[1024,1536]{1,0:T(8,128)(2,1)} custom-call(s32[9]{0:T(128)} %fusion.91.place_ref, bf16[128,1536]{1,0:T(8,128)(2,1)} %copy-done.11, bf16[128,1536]{1,0:T(8,128)(2,1)} %get-tuple-element.89.refs_1_, bf16[128,1536]{1,0:T(8,128)(2,1)} %get-tuple-element.90.refs_2_, bf16[128,1536]{1,0:T(8,128)(2,1)} %get-tuple-element.105.refs_3_, ...), custom_call_target="tpu_custom_call" | custom-call | bytes 6291456 | tf_op jit(solution)/shard_map/merge/pallas_call | solution.py:73
  384.4 1.6 collective-permute-start.32
  386.4 1.6 collective-permute-start.41
  388.5 14.8 %chunk.13 = (bf16[768,12288]{1,0:T(8,128)(2,1)}, bf16[768,12288]{1,0:T(8,128)(2,1)}, bf16[768,12288]{1,0:T(8,128)(2,1)}, f32[8,128]{1,0:T(8,128)}, f32[1024,768]{1,0:T(8,128)}) custom-call(s32[1]{0:T(128)} %bitcast.8.off_ref, bf16[768,1024]{1,0:T(8,128)(2,1)} %copy-done, ...), custom_call_target="tpu_custom_call", output_to_operand_aliasing={{0}: (7, {}), {1}: (8, {}), {2}: (9, {})} | custom-call | flops 6643777536 | bytes 12582912 | tf_op jit(solution)/shard_map/chunk/pallas_call | solution.py:195
  403.4 1.6 collective-permute-start.38
  406.2 1.6 slice.36
  407.8 1.6 collective-permute-start.45
  409.4 1.6 slice.37
  411.9 1.6 copy-done.6
  413.6 14.8 %chunk.14 = (bf16[768,12288]{1,0:T(8,128)(2,1)}, bf16[768,12288]{1,0:T(8,128)(2,1)}, bf16[768,12288]{1,0:T(8,128)(2,1)}, f32[8,128]{1,0:T(8,128)}, f32[1024,768]{1,0:T(8,128)}) custom-call(s32[1]{0:T(128)} %bitcast.9.off_ref, bf16[768,1024]{1,0:T(8,128)(2,1)} %copy-done, ...), custom_call_target="tpu_custom_call", output_to_operand_aliasing={{0}: (7, {}), {1}: (8, {}), {2}: (9, {})} | custom-call | flops 6643777536 | bytes 12582912 | tf_op jit(solution)/shard_map/chunk/pallas_call | solution.py:195
  429.2 97.1 %merge.8.refs_1_ = bf16[1024,1536]{1,0:T(8,128)(2,1)} custom-call(s32[9]{0:T(128)} %fusion.91.place_ref, bf16[128,1536]{1,0:T(8,128)(2,1)} %get-tuple-element.109.refs_0_, bf16[128,1536]{1,0:T(8,128)(2,1)} %get-tuple-element.118.refs_1_, bf16[128,1536]{1,0:T(8,128)(2,1)} %get-tuple-element.119.refs_2_, bf16[128,1536]{1,0:T(8,128)(2,1)} %get-tuple-element.130.refs_3_, ...), custom_call_target="tpu_custom_call" | custom-call | bytes 6291456 | tf_op jit(solution)/shard_map/merge/pallas_call | solution.py:73
  526.5 1.6 collective-permute-start.43
  528.5 14.8 %chunk.15 = (bf16[768,12288]{1,0:T(8,128)(2,1)}, bf16[768,12288]{1,0:T(8,128)(2,1)}, bf16[768,12288]{1,0:T(8,128)(2,1)}, f32[8,128]{1,0:T(8,128)}, f32[1024,768]{1,0:T(8,128)}) custom-call(s32[1]{0:T(128)} %bitcast.10.off_ref, bf16[768,1024]{1,0:T(8,128)(2,1)} %copy-done, ...), custom_call_target="tpu_custom_call", output_to_operand_aliasing={{0}: (6, {}), {1}: (7, {}), {2}: (8, {})} | custom-call | flops 6643777536 | bytes 12582912 | tf_op jit(solution)/shard_map/chunk/pallas_call | solution.py:195
  545.1 1.6 collective-permute-start.47
  548.2 1.5 collective-permute-done.47.refs_7_
  549.7 2.6 collective-permute-done.48.refs_8_
  553.0 49.5 %merge.9.refs_0_.refs_1_ = bf16[1024,768]{1,0:T(8,128)(2,1)} custom-call(s32[9]{0:T(128)} %fusion.91.place_ref, bf16[128,768]{1,0:T(8,128)(2,1)} %get-tuple-element.115.refs_0_, bf16[128,768]{1,0:T(8,128)(2,1)} %get-tuple-element.127.refs_1_, bf16[128,768]{1,0:T(8,128)(2,1)} %get-tuple-element.128.refs_2_, bf16[128,768]{1,0:T(8,128)(2,1)} %get-tuple-element.138.refs_3_, ...), custom_call_target="tpu_custom_call" | custom-call | bytes 3145728 | tf_op jit(solution)/shard_map/merge/pallas_call | solution.py:73
  603.2 14.8 %chunk.16 = (bf16[768,12288]{1,0:T(8,128)(2,1)}, bf16[768,12288]{1,0:T(8,128)(2,1)}, bf16[768,12288]{1,0:T(8,128)(2,1)}, f32[8,128]{1,0:T(8,128)}, f32[1024,768]{1,0:T(8,128)}) custom-call(s32[1]{0:T(128)} %bitcast.11.off_ref, bf16[768,1024]{1,0:T(8,128)(2,1)} %copy-done, ...), custom_call_target="tpu_custom_call", output_to_operand_aliasing={{0}: (6, {}), {1}: (7, {}), {2}: (8, {})} | custom-call | flops 6643777536 | bytes 12582912 | tf_op jit(solution)/shard_map/chunk/pallas_call | solution.py:195
  618.0 1.2 copy-done.1
  619.2 8.4 %share.1 = (bf16[1,512,768]{2,1,0:T(8,128)(2,1)}, f32[512,768]{1,0:T(8,128)}) custom-call(s32[2]{0:T(128)} %get-tuple-element.185.who_ref, s32[2]{0:T(128)} %get-tuple-element.186.off_ref, bf16[1024,768]{1,0:T(8,128)(2,1)} %merge.9.refs_0_.refs_1_, bf16[1024,768]{1,0:T(8,128)(2,1)} %copy-done.1, bf16[768,12288]{1,0:T(8,128)(2,1)} %refs_2_.17, ...), custom_call_target="tpu_custom_call" | custom-call | flops 2415919104 | bytes 11796480 | tf_op jit(solution)/shard_map/share/pallas_call | solution.py:253
  628.1 10.8 %chunk.17 = (bf16[768,12288]{1,0:T(8,128)(2,1)}, bf16[768,12288]{1,0:T(8,128)(2,1)}, bf16[768,12288]{1,0:T(8,128)(2,1)}, f32[8,128]{1,0:T(8,128)}) custom-call(s32[2]{0:T(128)} %get-tuple-element.186.off_ref, bf16[768,1024]{1,0:T(8,128)(2,1)} %copy-done, ...), custom_call_target="tpu_custom_call", output_to_operand_aliasing={{0}: (5, {}), {1}: (6, {}), {2}: (7, {})} | custom-call | flops 4227858432 | bytes 12582912 | tf_op jit(solution)/shard_map/chunk/pallas_call | solution.py:195
  638.9 8.8 %collective-permute-done.51 = bf16[512,768]{1,0:T(8,128)(2,1)S(1)} collective-permute-done((bf16[512,768]{1,0:T(8,128)(2,1)}, bf16[512,768]{1,0:T(8,128)(2,1)S(1)}, u32[]{:S(2)}, u32[]{:S(2)}) %collective-permute-start.51) | collective-permute-done | bytes 786464 | tf_op jit(solution)/shard_map/ppermute | solution.py:405
  647.7 1.0 add_convert_fusion
  (173 shorter events, 28.5 us)
Async XLA Ops:
  0.6 10.0 %copy-start.10 = (bf16[64,12288]{1,0:T(8,128)(2,1)S(1)}, bf16[64,12288]{1,0:T(8,128)(2,1)}, u32[]{:S(2)}) copy-start(bf16[64,12288]{1,0:T(8,128)(2,1)} %param.7) | copy-start | bytes 4718596
  2.1 5.9 collective-permute-start
  2.6 8.0 %collective-permute-start.9 = (bf16[64,768]{1,0:T(8,128)(2,1)S(1)}, bf16[64,768]{1,0:T(8,128)(2,1)S(1)}, u32[]{:S(2)}, u32[]{:S(2)}) collective-permute-start(bf16[64,768]{1,0:T(8,128)(2,1)S(1)} %get-tuple-element.183), channel_id=1, source_target_pairs={{0,2},{2,0},{4,6},{6,4},{8,10},{10,8},{12,14},{14,12},{16,18},{18,... | collective-permute-start | bytes 294920 | tf_op jit(solution)/shard_map/ppermute | solution.py:301
  5.6 8.7 %collective-permute-start.2 = (bf16[64,1536]{1,0:T(8,128)(2,1)}, bf16[64,1536]{1,0:T(8,128)(2,1)S(1)}, u32[]{:S(2)}, u32[]{:S(2)}) collective-permute-start(bf16[64,1536]{1,0:T(8,128)(2,1)} %get-tuple-element.180), channel_id=1, source_target_pairs={{0,2},{2,0},{4,6},{6,4},{8,10},{10,8},{12,14},{14,12},{16,18},{18,... | collective-permute-start | bytes 589832 | tf_op jit(solution)/shard_map/ppermute | solution.py:301
  6.0 8.7 %collective-permute-start.20 = (bf16[64,1536]{1,0:T(8,128)(2,1)}, bf16[64,1536]{1,0:T(8,128)(2,1)S(1)}, u32[]{:S(2)}, u32[]{:S(2)}) collective-permute-start(bf16[64,1536]{1,0:T(8,128)(2,1)} %get-tuple-element.179), channel_id=1, source_target_pairs={{0,2},{2,0},{4,6},{6,4},{8,10},{10,8},{12,14},{14,12},{16,18},{18,... | collective-permute-start | bytes 589832 | tf_op jit(solution)/shard_map/ppermute | solution.py:301
  6.1 8.6 %collective-permute-start.26 = (bf16[64,1536]{1,0:T(8,128)(2,1)S(1)}, bf16[64,1536]{1,0:T(8,128)(2,1)S(1)}, u32[]{:S(2)}, u32[]{:S(2)}) collective-permute-start(bf16[64,1536]{1,0:T(8,128)(2,1)S(1)} %get-tuple-element.178), channel_id=1, source_target_pairs={{0,2},{2,0},{4,6},{6,4},{8,10},{10,8},{12,14},{14,12},{16,18},{18,... | collective-permute-start | bytes 589832 | tf_op jit(solution)/shard_map/ppermute | solution.py:301
  8.0 6.7 %copy-start.27 = (bf16[64,768]{1,0:T(8,128)(2,1)}, bf16[64,768]{1,0:T(8,128)(2,1)S(1)}, u32[]{:S(2)}) copy-start(bf16[64,768]{1,0:T(8,128)(2,1)S(1)} %collective-permute-done) | copy-start | bytes 294916
  8.0 87.4 %collective-permute-start.1 = (bf16[768,512]{1,0:T(8,128)(2,1)S(1)}, bf16[768,512]{1,0:T(8,128)(2,1)}, u32[]{:S(2)}, u32[]{:S(2)}) collective-permute-start(bf16[768,512]{1,0:T(8,128)(2,1)S(1)} %bitcast.15), channel_id=1, source_target_pairs={{0,1},{1,0},{2,3},{3,2},{4,5},{5,4},{6,7},{7,6},{8,9},{9,8},{10,11... | collective-permute-start | bytes 2359304 | tf_op jit(solution)/shard_map/ppermute | solution.py:369
  12.6 9.8 %copy-start.22 = (bf16[128,768]{1,0:T(8,128)(2,1)}, bf16[128,768]{1,0:T(8,128)(2,1)S(1)}, u32[]{:S(2)}) copy-start(bf16[128,768]{1,0:T(8,128)(2,1)S(1)} %pad_maximum_fusion.4.refs_0_) | copy-start | bytes 589828
  12.6 7.0 %collective-permute-start.10 = (bf16[128,768]{1,0:T(8,128)(2,1)S(1)}, bf16[128,768]{1,0:T(8,128)(2,1)S(1)}, u32[]{:S(2)}, u32[]{:S(2)}) collective-permute-start(bf16[128,768]{1,0:T(8,128)(2,1)S(1)} %pad_maximum_fusion.4.refs_0_), channel_id=1, source_target_pairs={{0,8},{2,10},{8,16},{10,18},{16,24},{18,26},{24,28},{26,30},{28,20... | collective-permute-start | bytes 589832 | tf_op jit(solution)/shard_map/ppermute | solution.py:298
  14.3 7.0 %collective-permute-start.11 = (bf16[128,768]{1,0:T(8,128)(2,1)S(1)}, bf16[128,768]{1,0:T(8,128)(2,1)S(1)}, u32[]{:S(2)}, u32[]{:S(2)}) collective-permute-start(bf16[128,768]{1,0:T(8,128)(2,1)S(1)} %pad_maximum_fusion.4.refs_0_), channel_id=1, source_target_pairs={{0,4},{2,6},{8,0},{10,2},{16,8},{18,10},{24,16},{26,18},{28,24},{3... | collective-permute-start | bytes 589832 | tf_op jit(solution)/shard_map/ppermute | solution.py:298
  19.7 6.3 copy-start.32
  19.7 6.2 collective-permute-start.12
  21.2 6.0 collective-permute-start.13
  22.5 14.8 %copy-start.3 = (bf16[128,1536]{1,0:T(8,128)(2,1)S(1)}, bf16[128,1536]{1,0:T(8,128)(2,1)}, u32[]{:S(2)}) copy-start(bf16[128,1536]{1,0:T(8,128)(2,1)} %pad_maximum_fusion.refs_2_.refs_0_) | copy-start | bytes 1179652
  27.9 6.0 collective-permute-start.14
  29.5 6.0 collective-permute-start.15
  30.1 60.9 %copy-start.20 = (bf16[64,1536]{1,0:T(8,128)(2,1)S(1)}, bf16[64,1536]{1,0:T(8,128)(2,1)}, u32[]{:S(2)}) copy-start(bf16[64,1536]{1,0:T(8,128)(2,1)} %get-tuple-element.174) | copy-start | bytes 589828
  33.9 5.4 copy-start.25
  33.9 5.7 collective-permute-start.16
  35.5 5.9 collective-permute-start.17
  37.3 55.4 %collective-permute-start.3 = (bf16[128,1536]{1,0:T(8,128)(2,1)S(1)}, bf16[128,1536]{1,0:T(8,128)(2,1)}, u32[]{:S(2)}, u32[]{:S(2)}) collective-permute-start(bf16[128,1536]{1,0:T(8,128)(2,1)S(1)} %copy-done.3), channel_id=1, source_target_pairs={{0,8},{2,10},{8,16},{10,18},{16,24},{18,26},{24,28},{26,30},{28,20... | collective-permute-start | bytes 1179656 | tf_op jit(solution)/shard_map/ppermute | solution.py:298
  38.8 55.3 %collective-permute-start.4 = (bf16[128,1536]{1,0:T(8,128)(2,1)S(1)}, bf16[128,1536]{1,0:T(8,128)(2,1)}, u32[]{:S(2)}, u32[]{:S(2)}) collective-permute-start(bf16[128,1536]{1,0:T(8,128)(2,1)S(1)} %copy-done.3), channel_id=1, source_target_pairs={{0,4},{2,6},{8,0},{10,2},{16,8},{18,10},{24,16},{26,18},{28,24},{3... | collective-permute-start | bytes 1179656 | tf_op jit(solution)/shard_map/ppermute | solution.py:298
  90.9 40.3 %collective-permute-start.25 = (bf16[1024,768]{1,0:T(8,128)(2,1)}, bf16[1024,768]{1,0:T(8,128)(2,1)}, u32[]{:S(2)}, u32[]{:S(2)}) collective-permute-start(bf16[1024,768]{1,0:T(8,128)(2,1)} %merge.5.refs_1_), channel_id=1, source_target_pairs={{0,2},{2,0},{4,6},{6,4},{8,10},{10,8},{12,14},{14,12},{16,18},{18,... | collective-permute-start | bytes 4718600 | tf_op jit(solution)/shard_map/ppermute | solution.py:301
  91.1 30.6 %copy-start.11 = (bf16[128,1536]{1,0:T(8,128)(2,1)}, bf16[128,1536]{1,0:T(8,128)(2,1)S(1)}, u32[]{:S(2)}) copy-start(bf16[128,1536]{1,0:T(8,128)(2,1)S(1)} %pad_maximum_fusion.1.refs_0_) | copy-start | bytes 1179652
  91.1 30.6 %collective-permute-start.21 = (bf16[128,1536]{1,0:T(8,128)(2,1)S(1)}, bf16[128,1536]{1,0:T(8,128)(2,1)S(1)}, u32[]{:S(2)}, u32[]{:S(2)}) collective-permute-start(bf16[128,1536]{1,0:T(8,128)(2,1)S(1)} %pad_maximum_fusion.1.refs_0_), channel_id=1, source_target_pairs={{0,8},{2,10},{8,16},{10,18},{16,24},{18,26},{24,28},{26,30},{28,20... | collective-permute-start | bytes 1179656 | tf_op jit(solution)/shard_map/ppermute | solution.py:298
  92.7 18.6 %collective-permute-start.5 = (bf16[128,1536]{1,0:T(8,128)(2,1)}, bf16[128,1536]{1,0:T(8,128)(2,1)}, u32[]{:S(2)}, u32[]{:S(2)}) collective-permute-start(bf16[128,1536]{1,0:T(8,128)(2,1)} %collective-permute-done.3.refs_1_), channel_id=1, source_target_pairs={{0,8},{2,10},{8,16},{10,18},{16,24},{18,26},{24,28},{26,30},{28,20... | collective-permute-start | bytes 1179656 | tf_op jit(solution)/shard_map/ppermute | solution.py:298
  94.2 18.7 %collective-permute-start.6 = (bf16[128,1536]{1,0:T(8,128)(2,1)}, bf16[128,1536]{1,0:T(8,128)(2,1)}, u32[]{:S(2)}, u32[]{:S(2)}) collective-permute-start(bf16[128,1536]{1,0:T(8,128)(2,1)} %collective-permute-done.4.refs_2_), channel_id=1, source_target_pairs={{0,4},{2,6},{8,0},{10,2},{16,8},{18,10},{24,16},{26,18},{28,24},{3... | collective-permute-start | bytes 1179656 | tf_op jit(solution)/shard_map/ppermute | solution.py:298
  95.4 26.2 %collective-permute-start.22 = (bf16[128,1536]{1,0:T(8,128)(2,1)S(1)}, bf16[128,1536]{1,0:T(8,128)(2,1)S(1)}, u32[]{:S(2)}, u32[]{:S(2)}) collective-permute-start(bf16[128,1536]{1,0:T(8,128)(2,1)S(1)} %pad_maximum_fusion.1.refs_0_), channel_id=1, source_target_pairs={{0,4},{2,6},{8,0},{10,2},{16,8},{18,10},{24,16},{26,18},{28,24},{3... | collective-permute-start | bytes 1179656 | tf_op jit(solution)/shard_map/ppermute | solution.py:298
  97.1 16.2 %copy-start = (bf16[768,1024]{1,0:T(8,128)(2,1)}, bf16[768,1024]{1,0:T(8,128)(2,1)S(1)}, u32[]{:S(2)}) copy-start(bf16[768,1024]{1,0:T(8,128)(2,1)S(1)} %constant_dynamic-update-slice_fusion.refs_0_) | copy-start | bytes 4718596
  111.3 14.2 %collective-permute-start.7 = (bf16[128,1536]{1,0:T(8,128)(2,1)}, bf16[128,1536]{1,0:T(8,128)(2,1)S(1)}, u32[]{:S(2)}, u32[]{:S(2)}) collective-permute-start(bf16[128,1536]{1,0:T(8,128)(2,1)} %collective-permute-done.5.refs_3_), channel_id=1, source_target_pairs={{0,8},{2,10},{8,16},{10,18},{16,24},{18,26},{24,28},{26,30},{28,20... | collective-permute-start | bytes 1179656 | tf_op jit(solution)/shard_map/ppermute | solution.py:298
  112.9 12.6 %collective-permute-start.8 = (bf16[128,1536]{1,0:T(8,128)(2,1)}, bf16[128,1536]{1,0:T(8,128)(2,1)S(1)}, u32[]{:S(2)}, u32[]{:S(2)}) collective-permute-start(bf16[128,1536]{1,0:T(8,128)(2,1)} %collective-permute-done.6.refs_4_), channel_id=1, source_target_pairs={{0,4},{2,6},{8,0},{10,2},{16,8},{18,10},{24,16},{26,18},{28,24},{3... | collective-permute-start | bytes 1179656 | tf_op jit(solution)/shard_map/ppermute | solution.py:298
  113.3 11.3 %copy-start.21 = (bf16[64,1536]{1,0:T(8,128)(2,1)S(1)}, bf16[64,1536]{1,0:T(8,128)(2,1)}, u32[]{:S(2)}) copy-start(bf16[64,1536]{1,0:T(8,128)(2,1)} %broadcast_select_fusion) | copy-start | bytes 589828
  122.6 18.0 %collective-permute-start.23 = (bf16[128,1536]{1,0:T(8,128)(2,1)}, bf16[128,1536]{1,0:T(8,128)(2,1)S(1)}, u32[]{:S(2)}, u32[]{:S(2)}) collective-permute-start(bf16[128,1536]{1,0:T(8,128)(2,1)} %get-tuple-element.89.refs_1_), channel_id=1, source_target_pairs={{0,8},{2,10},{8,16},{10,18},{16,24},{18,26},{24,28},{26,30},{28,20... | collective-permute-start | bytes 1179656 | tf_op jit(solution)/shard_map/ppermute | solution.py:298
  124.2 16.4 %collective-permute-start.24 = (bf16[128,1536]{1,0:T(8,128)(2,1)}, bf16[128,1536]{1,0:T(8,128)(2,1)S(1)}, u32[]{:S(2)}, u32[]{:S(2)}) collective-permute-start(bf16[128,1536]{1,0:T(8,128)(2,1)} %get-tuple-element.90.refs_2_), channel_id=1, source_target_pairs={{0,4},{2,6},{8,0},{10,2},{16,8},{18,10},{24,16},{26,18},{28,24},{3... | collective-permute-start | bytes 1179656 | tf_op jit(solution)/shard_map/ppermute | solution.py:298
  127.9 14.2 %collective-permute-start.18 = (bf16[64,1536]{1,0:T(8,128)(2,1)S(1)}, bf16[64,1536]{1,0:T(8,128)(2,1)S(1)}, u32[]{:S(2)}, u32[]{:S(2)}) collective-permute-start(bf16[64,1536]{1,0:T(8,128)(2,1)S(1)} %slice.32), channel_id=1, source_target_pairs={{0,8},{2,10},{8,16},{10,18},{16,24},{18,26},{24,28},{26,30},{28,20... | collective-permute-start | bytes 589832 | tf_op jit(solution)/shard_map/ppermute | solution.py:298
  130.5 11.7 %collective-permute-start.19 = (bf16[64,1536]{1,0:T(8,128)(2,1)S(1)}, bf16[64,1536]{1,0:T(8,128)(2,1)S(1)}, u32[]{:S(2)}, u32[]{:S(2)}) collective-permute-start(bf16[64,1536]{1,0:T(8,128)(2,1)S(1)} %slice.33), channel_id=1, source_target_pairs={{0,4},{2,6},{8,0},{10,2},{16,8},{18,10},{24,16},{26,18},{28,24},{3... | collective-permute-start | bytes 589832 | tf_op jit(solution)/shard_map/ppermute | solution.py:298
  142.9 99.9 %copy-start.4 = (bf16[128,1536]{1,0:T(8,128)(2,1)S(1)}, bf16[128,1536]{1,0:T(8,128)(2,1)}, u32[]{:S(2)}) copy-start(bf16[128,1536]{1,0:T(8,128)(2,1)} %get-tuple-element.109.refs_0_) | copy-start | bytes 1179652
  240.2 29.8 %collective-permute-start.27 = (bf16[1024,1536]{1,0:T(8,128)(2,1)}, bf16[1024,1536]{1,0:T(8,128)(2,1)S(1)}, u32[]{:S(2)}, u32[]{:S(2)}) collective-permute-start(bf16[1024,1536]{1,0:T(8,128)(2,1)} %merge.6.refs_1_), channel_id=1, source_target_pairs={{0,2},{2,0},{4,6},{6,4},{8,10},{10,8},{12,14},{14,12},{16,18},{18,... | collective-permute-start | bytes 9437192 | tf_op jit(solution)/shard_map/ppermute | solution.py:301
  242.8 18.9 %collective-permute-start.30 = (bf16[128,1536]{1,0:T(8,128)(2,1)S(1)}, bf16[128,1536]{1,0:T(8,128)(2,1)S(1)}, u32[]{:S(2)}, u32[]{:S(2)}) collective-permute-start(bf16[128,1536]{1,0:T(8,128)(2,1)S(1)} %copy-done.4), channel_id=1, source_target_pairs={{0,8},{2,10},{8,16},{10,18},{16,24},{18,26},{24,28},{26,30},{28,20... | collective-permute-start | bytes 1179656 | tf_op jit(solution)/shard_map/ppermute | solution.py:298
  244.3 17.4 %collective-permute-start.31 = (bf16[128,1536]{1,0:T(8,128)(2,1)S(1)}, bf16[128,1536]{1,0:T(8,128)(2,1)}, u32[]{:S(2)}, u32[]{:S(2)}) collective-permute-start(bf16[128,1536]{1,0:T(8,128)(2,1)S(1)} %copy-done.4), channel_id=1, source_target_pairs={{0,4},{2,6},{8,0},{10,2},{16,8},{18,10},{24,16},{26,18},{28,24},{3... | collective-permute-start | bytes 1179656 | tf_op jit(solution)/shard_map/ppermute | solution.py:298
  244.8 19.7 %collective-permute-start.28 = (bf16[128,1536]{1,0:T(8,128)(2,1)}, bf16[128,1536]{1,0:T(8,128)(2,1)}, u32[]{:S(2)}, u32[]{:S(2)}) collective-permute-start(bf16[128,1536]{1,0:T(8,128)(2,1)} %get-tuple-element.105.refs_3_), channel_id=1, source_target_pairs={{0,8},{2,10},{8,16},{10,18},{16,24},{18,26},{24,28},{26,30},{28,20... | collective-permute-start | bytes 1179656 | tf_op jit(solution)/shard_map/ppermute | solution.py:298
  246.4 18.1 %collective-permute-start.29 = (bf16[128,1536]{1,0:T(8,128)(2,1)}, bf16[128,1536]{1,0:T(8,128)(2,1)}, u32[]{:S(2)}, u32[]{:S(2)}) collective-permute-start(bf16[128,1536]{1,0:T(8,128)(2,1)} %get-tuple-element.106.refs_4_), channel_id=1, source_target_pairs={{0,4},{2,6},{8,0},{10,2},{16,8},{18,10},{24,16},{26,18},{28,24},{3... | collective-permute-start | bytes 1179656 | tf_op jit(solution)/shard_map/ppermute | solution.py:298
  262.4 23.9 %collective-permute-start.36 = (bf16[128,1536]{1,0:T(8,128)(2,1)}, bf16[128,1536]{1,0:T(8,128)(2,1)S(1)}, u32[]{:S(2)}, u32[]{:S(2)}) collective-permute-start(bf16[128,1536]{1,0:T(8,128)(2,1)} %get-tuple-element.118.refs_1_), channel_id=1, source_target_pairs={{0,8},{2,10},{8,16},{10,18},{16,24},{18,26},{24,28},{26,30},{28,20... | collective-permute-start | bytes 1179656 | tf_op jit(solution)/shard_map/ppermute | solution.py:298
  264.0 22.4 %collective-permute-start.37 = (bf16[128,1536]{1,0:T(8,128)(2,1)}, bf16[128,1536]{1,0:T(8,128)(2,1)}, u32[]{:S(2)}, u32[]{:S(2)}) collective-permute-start(bf16[128,1536]{1,0:T(8,128)(2,1)} %get-tuple-element.119.refs_2_), channel_id=1, source_target_pairs={{0,4},{2,6},{8,0},{10,2},{16,8},{18,10},{24,16},{26,18},{28,24},{3... | collective-permute-start | bytes 1179656 | tf_op jit(solution)/shard_map/ppermute | solution.py:298
  266.1 21.0 %collective-permute-start.34 = (bf16[64,1536]{1,0:T(8,128)(2,1)}, bf16[64,1536]{1,0:T(8,128)(2,1)}, u32[]{:S(2)}, u32[]{:S(2)}) collective-permute-start(bf16[64,1536]{1,0:T(8,128)(2,1)} %slice.34), channel_id=1, source_target_pairs={{0,8},{2,10},{8,16},{10,18},{16,24},{18,26},{24,28},{26,30},{28,20... | collective-permute-start | bytes 589832 | tf_op jit(solution)/shard_map/ppermute | solution.py:298
  269.3 17.8 %collective-permute-start.35 = (bf16[64,1536]{1,0:T(8,128)(2,1)}, bf16[64,1536]{1,0:T(8,128)(2,1)}, u32[]{:S(2)}, u32[]{:S(2)}) collective-permute-start(bf16[64,1536]{1,0:T(8,128)(2,1)} %slice.35), channel_id=1, source_target_pairs={{0,4},{2,6},{8,0},{10,2},{16,8},{18,10},{24,16},{26,18},{28,24},{3... | collective-permute-start | bytes 589832 | tf_op jit(solution)/shard_map/ppermute | solution.py:298
  384.3 27.6 %collective-permute-start.40 = (bf16[1024,1536]{1,0:T(8,128)(2,1)}, bf16[1024,1536]{1,0:T(8,128)(2,1)S(1)}, u32[]{:S(2)}, u32[]{:S(2)}) collective-permute-start(bf16[1024,1536]{1,0:T(8,128)(2,1)} %merge.7.refs_1_), channel_id=1, source_target_pairs={{0,2},{2,0},{4,6},{6,4},{8,10},{10,8},{12,14},{14,12},{16,18},{18,... | collective-permute-start | bytes 9437192 | tf_op jit(solution)/shard_map/ppermute | solution.py:301
  384.4 19.0 %collective-permute-start.32 = (bf16[128,768]{1,0:T(8,128)(2,1)}, bf16[128,768]{1,0:T(8,128)(2,1)}, u32[]{:S(2)}, u32[]{:S(2)}) collective-permute-start(bf16[128,768]{1,0:T(8,128)(2,1)} %get-tuple-element.115.refs_0_), channel_id=1, source_target_pairs={{0,8},{2,10},{8,16},{10,18},{16,24},{18,26},{24,28},{26,30},{28,20... | collective-permute-start | bytes 589832 | tf_op jit(solution)/shard_map/ppermute | solution.py:298
  386.0 17.3 %collective-permute-start.33 = (bf16[128,768]{1,0:T(8,128)(2,1)}, bf16[128,768]{1,0:T(8,128)(2,1)}, u32[]{:S(2)}, u32[]{:S(2)}) collective-permute-start(bf16[128,768]{1,0:T(8,128)(2,1)} %get-tuple-element.115.refs_0_), channel_id=1, source_target_pairs={{0,4},{2,6},{8,0},{10,2},{16,8},{18,10},{24,16},{26,18},{28,24},{3... | collective-permute-start | bytes 589832 | tf_op jit(solution)/shard_map/ppermute | solution.py:298
  386.4 19.0 %collective-permute-start.41 = (bf16[128,1536]{1,0:T(8,128)(2,1)}, bf16[128,1536]{1,0:T(8,128)(2,1)S(1)}, u32[]{:S(2)}, u32[]{:S(2)}) collective-permute-start(bf16[128,1536]{1,0:T(8,128)(2,1)} %get-tuple-element.130.refs_3_), channel_id=1, source_target_pairs={{0,8},{2,10},{8,16},{10,18},{16,24},{18,26},{24,28},{26,30},{28,20... | collective-permute-start | bytes 1179656 | tf_op jit(solution)/shard_map/ppermute | solution.py:298
  388.0 17.4 %collective-permute-start.42 = (bf16[128,1536]{1,0:T(8,128)(2,1)}, bf16[128,1536]{1,0:T(8,128)(2,1)}, u32[]{:S(2)}, u32[]{:S(2)}) collective-permute-start(bf16[128,1536]{1,0:T(8,128)(2,1)} %get-tuple-element.131.refs_4_), channel_id=1, source_target_pairs={{0,4},{2,6},{8,0},{10,2},{16,8},{18,10},{24,16},{26,18},{28,24},{3... | collective-permute-start | bytes 1179656 | tf_op jit(solution)/shard_map/ppermute | solution.py:298
  403.4 25.1 %collective-permute-start.38 = (bf16[128,768]{1,0:T(8,128)(2,1)}, bf16[128,768]{1,0:T(8,128)(2,1)}, u32[]{:S(2)}, u32[]{:S(2)}) collective-permute-start(bf16[128,768]{1,0:T(8,128)(2,1)} %get-tuple-element.127.refs_1_), channel_id=1, source_target_pairs={{0,8},{2,10},{8,16},{10,18},{16,24},{18,26},{24,28},{26,30},{28,20... | collective-permute-start | bytes 589832 | tf_op jit(solution)/shard_map/ppermute | solution.py:298
  405.0 23.4 %collective-permute-start.39 = (bf16[128,768]{1,0:T(8,128)(2,1)}, bf16[128,768]{1,0:T(8,128)(2,1)}, u32[]{:S(2)}, u32[]{:S(2)}) collective-permute-start(bf16[128,768]{1,0:T(8,128)(2,1)} %get-tuple-element.128.refs_2_), channel_id=1, source_target_pairs={{0,4},{2,6},{8,0},{10,2},{16,8},{18,10},{24,16},{26,18},{28,24},{3... | collective-permute-start | bytes 589832 | tf_op jit(solution)/shard_map/ppermute | solution.py:298
  407.8 20.6 %collective-permute-start.45 = (bf16[64,1536]{1,0:T(8,128)(2,1)}, bf16[64,1536]{1,0:T(8,128)(2,1)S(1)}, u32[]{:S(2)}, u32[]{:S(2)}) collective-permute-start(bf16[64,1536]{1,0:T(8,128)(2,1)} %slice.36), channel_id=1, source_target_pairs={{0,8},{2,10},{8,16},{10,18},{16,24},{18,26},{24,28},{26,30},{28,20... | collective-permute-start | bytes 589832 | tf_op jit(solution)/shard_map/ppermute | solution.py:298
  411.0 17.4 %collective-permute-start.46 = (bf16[64,1536]{1,0:T(8,128)(2,1)}, bf16[64,1536]{1,0:T(8,128)(2,1)S(1)}, u32[]{:S(2)}, u32[]{:S(2)}) collective-permute-start(bf16[64,1536]{1,0:T(8,128)(2,1)} %slice.37), channel_id=1, source_target_pairs={{0,4},{2,6},{8,0},{10,2},{16,8},{18,10},{24,16},{26,18},{28,24},{3... | collective-permute-start | bytes 589832 | tf_op jit(solution)/shard_map/ppermute | solution.py:298
  526.4 76.8 %collective-permute-start.50 = (bf16[1024,1536]{1,0:T(8,128)(2,1)}, bf16[1024,1536]{1,0:T(8,128)(2,1)}, u32[]{:S(2)}, u32[]{:S(2)}) collective-permute-start(bf16[1024,1536]{1,0:T(8,128)(2,1)} %merge.8.refs_1_), channel_id=1, source_target_pairs={{0,2},{2,0},{4,6},{6,4},{8,10},{10,8},{12,14},{14,12},{16,18},{18,... | collective-permute-start | bytes 9437192 | tf_op jit(solution)/shard_map/ppermute | solution.py:301
  526.5 16.9 %collective-permute-start.43 = (bf16[128,768]{1,0:T(8,128)(2,1)}, bf16[128,768]{1,0:T(8,128)(2,1)S(1)}, u32[]{:S(2)}, u32[]{:S(2)}) collective-permute-start(bf16[128,768]{1,0:T(8,128)(2,1)} %get-tuple-element.138.refs_3_), channel_id=1, source_target_pairs={{0,8},{2,10},{8,16},{10,18},{16,24},{18,26},{24,28},{26,30},{28,20... | collective-permute-start | bytes 589832 | tf_op jit(solution)/shard_map/ppermute | solution.py:298
  528.1 15.3 %collective-permute-start.44 = (bf16[128,768]{1,0:T(8,128)(2,1)}, bf16[128,768]{1,0:T(8,128)(2,1)S(1)}, u32[]{:S(2)}, u32[]{:S(2)}) collective-permute-start(bf16[128,768]{1,0:T(8,128)(2,1)} %get-tuple-element.139.refs_4_), channel_id=1, source_target_pairs={{0,4},{2,6},{8,0},{10,2},{16,8},{18,10},{24,16},{26,18},{28,24},{3... | collective-permute-start | bytes 589832 | tf_op jit(solution)/shard_map/ppermute | solution.py:298
  545.1 4.6 collective-permute-start.47
  547.6 4.8 collective-permute-start.48
  602.5 15.5 %collective-permute-start.49 = (bf16[1024,768]{1,0:T(8,128)(2,1)}, bf16[1024,768]{1,0:T(8,128)(2,1)S(1)}, u32[]{:S(2)}, u32[]{:S(2)}) collective-permute-start(bf16[1024,768]{1,0:T(8,128)(2,1)} %merge.9.refs_0_.refs_1_), channel_id=1, source_target_pairs={{0,2},{2,0},{4,6},{6,4},{8,10},{10,8},{12,14},{14,12},{16,18},{18,... | collective-permute-start | bytes 4718600 | tf_op jit(solution)/shard_map/ppermute | solution.py:301
  627.6 20.1 %collective-permute-start.51 = (bf16[512,768]{1,0:T(8,128)(2,1)}, bf16[512,768]{1,0:T(8,128)(2,1)S(1)}, u32[]{:S(2)}, u32[]{:S(2)}) collective-permute-start(bf16[512,768]{1,0:T(8,128)(2,1)} %bitcast.16), channel_id=1, source_target_pairs={{0,1},{1,0},{2,3},{3,2},{4,5},{5,4},{6,7},{7,6},{8,9},{9,8},{10,11... | collective-permute-start | bytes 2359304 | tf_op jit(solution)/shard_map/ppermute | solution.py:405
  628.1 19.7 %copy-start.2 = (f32[512,768]{1,0:T(8,128)S(1)}, f32[512,768]{1,0:T(8,128)}, u32[]{:S(2)}) copy-start(f32[512,768]{1,0:T(8,128)} %get-tuple-element.156.refs_3_) | copy-start | bytes 4718596
  (25 other events, 30.4 us)

commit v3 on v1

--- a/solution.py
+++ b/solution.py
@@ -10,7 +10,7 @@
 
 BLOCK = 384
 STEP = 2 * BLOCK
-SHARES = (6, 5, 3, 2)
+SHARES = (1, 1)
 VMEM_LIMIT = 56 * 1024 * 1024
 
 
@@ -112,42 +112,59 @@
     )(*args)
 
 
-def share_kernel(_, hg_ref, w_ref, acc_ref, out_ref):
-    total = acc_ref[...] + lax.dot_general(
+def share_kernel(groups, group, steps, who_ref, hg_ref, w_ref, acc_ref, away_ref, own_ref, sum_ref):
+    step = pl.program_id(0)
+
+    @pl.when(step == 0)
+    def _():
+        sum_ref[...] = acc_ref[...]
+
+    sum_ref[...] += lax.dot_general(
         hg_ref[...], w_ref[...], (((1,), (1,)), ((), ())), preferred_element_type=jnp.float32
     )
-    out_ref[...] = total[None].astype(out_ref.dtype)
-
-
-def share_call(which, hg, weight, acc, count, offset, dtype):
-    tokens, width = hg.shape
-    rows = weight.shape[0]
-    group = tokens // count
-    tile = 256 if rows % 256 == 0 else BLOCK
-    pieces = which.shape[0]
-    grid_spec = pltpu.PrefetchScalarGridSpec(
-        num_scalar_prefetch=1,
-        grid=(pieces, rows // tile),
-        in_specs=[
-            pl.BlockSpec((group, width), lambda p, d, w: (w[p], 0)),
-            pl.BlockSpec((tile, width), lambda p, d, w: (d, 0)),
-            pl.BlockSpec((group, tile), lambda p, d, w: (w[p], d)),
+
+    @pl.when(step == steps - 1)
+    def _():
+        for k in range(groups):
+            at = pl.multiple_of(who_ref[k] * group, group)
+            part = sum_ref[pl.ds(at, group), :]
+            if k:
+                away_ref[k - 1] = part.astype(away_ref.dtype)
+            else:
+                own_ref[...] = part
+
+
+def share_call(who, hg, weight, acc, groups, offset, steps):
+    tokens, rows = acc.shape
+    group = tokens // groups
+    return pl.pallas_call(
+        functools.partial(share_kernel, groups, group, steps),
+        grid_spec=pltpu.PrefetchScalarGridSpec(
+            num_scalar_prefetch=1,
+            grid=(steps,),
+            in_specs=[
+                pl.BlockSpec((tokens, STEP), lambda s, _: (0, s)),
+                pl.BlockSpec((rows, STEP), lambda s, _: (0, s + offset)),
+                pl.BlockSpec((tokens, rows), lambda s, _: (0, 0)),
+            ],
+            out_specs=[
+                pl.BlockSpec((groups - 1, group, rows), lambda s, _: (0, 0, 0)),
+                pl.BlockSpec((group, rows), lambda s, _: (0, 0)),
+            ],
+            scratch_shapes=[pltpu.VMEM((tokens, rows), jnp.float32)],
+        ),
+        out_shape=[
+            jax.ShapeDtypeStruct((groups - 1, group, rows), jnp.bfloat16),
+            jax.ShapeDtypeStruct((group, rows), jnp.float32),
         ],
-        out_specs=pl.BlockSpec((1, group, tile), lambda p, d, w: (p, 0, d)),
-    )
-    w_last = weight[:, offset * STEP:]
-    return pl.pallas_call(
-        share_kernel,
-        grid_spec=grid_spec,
-        out_shape=jax.ShapeDtypeStruct((pieces, group, rows), dtype),
         compiler_params=pltpu.CompilerParams(vmem_limit_bytes=VMEM_LIMIT),
         cost_estimate=pl.CostEstimate(
-            flops=2 * pieces * group * width * rows,
-            bytes_accessed=2 * rows * width + pieces * group * (2 * width + 6 * rows),
+            flops=2 * tokens * steps * STEP * rows,
+            bytes_accessed=2 * steps * STEP * (rows + tokens) + 8 * tokens * rows,
             transcendentals=0,
         ),
         name="share",
-    )(which, hg, w_last, acc)
+    )(who, hg, weight, acc)
 
 
 def on_device(cols, tokens, weight, pre_act, out_grad):
@@ -177,13 +194,12 @@
 
     offset, steps = chunks[-1]
     hg = gathered[-1]
-    others = (me + jnp.arange(1, cols, dtype=jnp.int32)) % cols
-    shares = share_call(others, hg, weight, acc, cols, offset, jnp.bfloat16)
+    who = (me + jnp.arange(cols, dtype=jnp.int32)) % cols
+    shares, own = share_call(who, hg, weight, acc, cols, offset, steps)
     arrived = [
         lax.ppermute(shares[s - 1], "col", [(i, (i + s) % cols) for i in range(cols)])
         for s in range(1, cols)
     ]
-    own = share_call(me[None], hg, weight, acc, cols, offset, jnp.float32)[0]
     outs = chunk_call(scale, x_t, hg, weight, None, outs, offset, steps, False)
     for piece in arrived:
         own = own + piece.astype(jnp.float32)

time: 300 us -> 271 us (0.903)
  Pallas kernels: 94.8 us -> 83 us
  waiting for transfers between devices: 171 us -> 162 us
  other arithmetic: 10.6 us -> 6.05 us
  local copies, waits for them, and re-layouts: 4.22 us -> 1.04 us
    pallas_call x4 -> x2, Pallas kernels: 84.3 us -> 65.1 us  [chunk_call(): pl.pallas_call(functools.partial(chunk_kernel, scale, with_share, first),...]
    all_gather x4 -> x2, waiting for transfers between devices: 154 us -> 145 us  [on_device(): gathered.append(lax.all_gather(hidden, 'row', axis=0, tiled=True))]
    pallas_call x2 -> x1, Pallas kernels: 10.5 us -> 17.9 us  [share_call(): pl.pallas_call(functools.partial(share_kernel, groups, group, steps), gri...]
    convert_element_type x4 -> x1, other arithmetic: 9.52 us -> 4.43 us  [on_device(): hidden = (out_grad[:, at].astype(jnp.float32) * slope).astype(jnp.bfloat16)]
    ppermute x1, waiting for transfers between devices: 3.63 us -> 0.01 us  [on_device(): lax.ppermute(shares[s - 1], 'col', [(i, (i + s) % cols) for i in range(co...]
    slice x1 -> x0, local copies, waits for them, and re-layouts: 3.53 us -> none  [share_call(): w_last = weight[:, offset * STEP:]]
  transfers between devices with their start and end apart: 6 -> 4, of which waited for: 6 -> 3; matrix products, arithmetic and copies ran while one was open for 4% -> 0% of each run, Pallas kernels for 30% -> 24%
where the time goes in v3:
time: 271 us
  waiting for transfers between devices  162 us (60%)
  Pallas kernels  83 us (31%)
  between operations  14.1 us (5%)
  other arithmetic  6.05 us (2%)
  starting transfers between devices  4.59 us (2%)
    all_gather x2, waiting for transfers between devices, on_device(): gathered.append(lax.all_gather(hidden, 'row', axis=0, tiled=True))  145 us
    pallas_call x2, Pallas kernels, chunk_call(): pl.pallas_call(functools.partial(chunk_kernel, scale, with_share, first),...  65.1 us
    pallas_call x1, Pallas kernels, share_call(): pl.pallas_call(functools.partial(share_kernel, groups, group, steps), gri...  17.9 us
    ppermute x1, waiting for transfers between devices, on_device(): lax.ppermute(own_t, 'col', [(i, (i + s) % cols) for i in range(cols)])  16.6 us
  transfers between devices with their start and end apart: 4, of which 3 were waited for; matrix products, arithmetic and copies ran while one was open for 0% of the time, Pallas kernels for 24%

profile of v3, /device:TPU:0, one launch (start us, length us, event | category | flops | bytes accessed | tf_op | source)
XLA Modules:
  0.0 271.0 jit_solution(15257791973350260338)
XLA Ops:
  7.2 0.0 all-gather.5.cloned.1.call-start
  7.2 4.4 %fusion.16 = (bf16[64,6144]{1,0:T(8,128)(2,1)}, bf16[64,6144]{1,0:T(8,128)(2,1)}) fusion(bf16[64,12288]{1,0:T(8,128)(2,1)} %param.6, bf16[64,12288]{1,0:T(8,128)(2,1)} %param.7), kind=kLoop, calls=%fused_computation.30 | loop fusion | flops 16515072 | bytes 4718592 | tf_op jit(solution)/shard_map/convert_element_type | solution.py:181
  11.6 0.0 copy-start.2
  11.6 0.0 all-gather.5.cloned.1.call-update
  11.7 0.0 all-gather.3.cloned.1.call-start
  11.7 0.7 all-gather.3.cloned.1.call-update
  12.4 0.4 copy-done.2
  12.8 0.3 copy.11
  13.1 3.0 %collective-permute-start = (bf16[768,512]{1,0:T(8,128)(2,1)S(1)}, bf16[768,512]{1,0:T(8,128)(2,1)S(1)}, u32[]{:S(2)}, u32[]{:S(2)}) collective-permute-start(bf16[768,512]{1,0:T(8,128)(2,1)S(1)} %bitcast.3), channel_id=1, source_target_pairs={{0,1},{1,0},{2,3},{3,2},{4,5},{5,4},{6,7},{7,6},{8,9},{9,8},{10,11... | collective-permute-start | bytes 2359304 | tf_op jit(solution)/shard_map/ppermute | solution.py:188
  16.1 0.6 and_select_fusion.who_ref
  16.7 0.2 broadcast_in_dim.3
  16.9 0.1 constant_dynamic-update-slice_fusion.1
  17.0 16.6 %collective-permute-done = bf16[768,512]{1,0:T(8,128)(2,1)S(1)} collective-permute-done((bf16[768,512]{1,0:T(8,128)(2,1)S(1)}, bf16[768,512]{1,0:T(8,128)(2,1)S(1)}, u32[]{:S(2)}, u32[]{:S(2)}) %collective-permute-start) | collective-permute-done | bytes 786464 | tf_op jit(solution)/shard_map/ppermute | solution.py:188
  33.6 0.1 constant_dynamic-update-slice_fusion.refs_0_
  33.7 0.0 copy-start
  33.8 81.5 %all-gather.5.cloned.1.call-done.refs_1_ = bf16[1024,6144]{1,0:T(8,128)(2,1)} async-done(((bf16[64,6144]{1,0:T(8,128)(2,1)}), bf16[1024,6144]{1,0:T(8,128)(2,1)}) %all-gather.5.cloned.1.call-update) | async-done | bytes 12582928 | tf_op jit(solution)/shard_map/all_gather | solution.py:182
  115.3 0.0 copy-done
  115.3 37.8 %chunk.2 = (bf16[768,12288]{1,0:T(8,128)(2,1)}, bf16[768,12288]{1,0:T(8,128)(2,1)}, bf16[768,12288]{1,0:T(8,128)(2,1)}, f32[1024,768]{1,0:T(8,128)}) custom-call(bf16[768,1024]{1,0:T(8,128)(2,1)} %copy-done, bf16[1024,6144]{1,0:T(8,128)(2,1)} %all-gather.5.cloned.1.call-done.refs_1_, bf16[768,12288]{1,0:T(8,128)(2,1)} %w_ref.1), custom_call_target="tpu_custom_call" | custom-call | flops 26575110144 | bytes 50331648 | tf_op jit(solution)/shard_map/chunk/pallas_call | solution.py:98
  153.1 63.4 %all-gather.3.cloned.1.call-done.hg_ref.refs_1_ = bf16[1024,6144]{1,0:T(8,128)(2,1)} async-done(((bf16[64,6144]{1,0:T(8,128)(2,1)}), bf16[1024,6144]{1,0:T(8,128)(2,1)}) %all-gather.3.cloned.1.call-update) | async-done | bytes 12582928 | tf_op jit(solution)/shard_map/all_gather | solution.py:182
  216.5 17.9 %share.1 = (bf16[1,512,768]{2,1,0:T(8,128)(2,1)}, f32[512,768]{1,0:T(8,128)}) custom-call(s32[2]{0:T(128)} %and_select_fusion.who_ref, bf16[1024,6144]{1,0:T(8,128)(2,1)} %all-gather.3.cloned.1.call-done.hg_ref.refs_1_, bf16[768,12288]{1,0:T(8,128)(2,1)} %w_ref.1, f32[1024,768]{1,0:T(8,128)} %get-tuple-element.13.acc_ref), custom_call_target="tpu_custom_call" | custom-call | flops 9663676416 | bytes 28311552 | tf_op jit(solution)/shard_map/share/pallas_call | solution.py:140
  234.4 1.5 collective-permute-start.1
  235.9 0.0 copy-start.1
  235.9 27.2 %chunk.3 = (bf16[768,12288]{1,0:T(8,128)(2,1)}, bf16[768,12288]{1,0:T(8,128)(2,1)}, bf16[768,12288]{1,0:T(8,128)(2,1)}) custom-call(bf16[768,1024]{1,0:T(8,128)(2,1)} %copy-done, bf16[1024,6144]{1,0:T(8,128)(2,1)} %all-gather.3.cloned.1.call-done.hg_ref.refs_1_, ...), custom_call_target="tpu_custom_call", output_to_operand_aliasing={{0}: (2, {}), {1}: (3, {}), {2}: (4, {})} | custom-call | flops 16911433728 | bytes 50331648 | tf_op jit(solution)/shard_map/chunk/pallas_call | solution.py:98
  263.1 0.0 collective-permute-done.1
  263.1 0.0 copy-done.1
  263.1 1.0 add_convert_fusion
Async XLA Ops:
  7.2 108.1 %all-gather.5.cloned.1.call-start = ((), (), s32[]{:S(2)}) async-start(), calls=%async_computation.1 | async-start | bytes 13369344 | tf_op jit(solution)/shard_map/all_gather | solution.py:182
  11.6 1.1 copy-start.2
  11.7 204.9 %all-gather.3.cloned.1.call-start = ((), (), s32[]{:S(2)}) async-start(), calls=%async_computation | async-start | bytes 13369344 | tf_op jit(solution)/shard_map/all_gather | solution.py:182
  13.1 20.6 %collective-permute-start = (bf16[768,512]{1,0:T(8,128)(2,1)S(1)}, bf16[768,512]{1,0:T(8,128)(2,1)S(1)}, u32[]{:S(2)}, u32[]{:S(2)}) collective-permute-start(bf16[768,512]{1,0:T(8,128)(2,1)S(1)} %bitcast.3), channel_id=1, source_target_pairs={{0,1},{1,0},{2,3},{3,2},{4,5},{5,4},{6,7},{7,6},{8,9},{9,8},{10,11... | collective-permute-start | bytes 2359304 | tf_op jit(solution)/shard_map/ppermute | solution.py:188
  33.7 81.5 %copy-start = (bf16[768,1024]{1,0:T(8,128)(2,1)}, bf16[768,1024]{1,0:T(8,128)(2,1)S(1)}, u32[]{:S(2)}) copy-start(bf16[768,1024]{1,0:T(8,128)(2,1)S(1)} %constant_dynamic-update-slice_fusion.refs_0_) | copy-start | bytes 4718596
  234.4 28.7 %collective-permute-start.1 = (bf16[512,768]{1,0:T(8,128)(2,1)}, bf16[512,768]{1,0:T(8,128)(2,1)S(1)}, u32[]{:S(2)}, u32[]{:S(2)}) collective-permute-start(bf16[512,768]{1,0:T(8,128)(2,1)} %bitcast.4), channel_id=1, source_target_pairs={{0,1},{1,0},{2,3},{3,2},{4,5},{5,4},{6,7},{7,6},{8,9},{9,8},{10,11... | collective-permute-start | bytes 2359304 | tf_op jit(solution)/shard_map/ppermute | solution.py:200
  235.9 27.2 %copy-start.1 = (f32[512,768]{1,0:T(8,128)S(1)}, f32[512,768]{1,0:T(8,128)}, u32[]{:S(2)}) copy-start(f32[512,768]{1,0:T(8,128)} %get-tuple-element.14) | copy-start | bytes 4718596
Sparse Core Ops, SparseCore 0:
  11.8 103.4 all-gather.4
  117.6 98.9 all-gather.2

commit v4 on v2

--- a/solution.py
+++ b/solution.py
@@ -11,12 +11,11 @@
 
 BLOCK = 384
 STEP = 2 * BLOCK
-CHUNKS = (1, 2, 2, 2, 1)
+RING, GATHER = 0, 1
+CHUNKS = ((RING, 2), (GATHER, 3), (RING, 3))
 VMEM_LIMIT = 60 * 1024 * 1024
 ANYWHERE = pl.BlockSpec(memory_space=pltpu.HBM)
 TICK = jax.ShapeDtypeStruct((8, 128), jnp.float32)
-NT = (((1,), (1,)), ((), ()))
-TN = (((0,), (0,)), ((), ()))
 
 
 def gelu_slope(value):
@@ -29,12 +28,15 @@
 
 
 def plan(steps):
-    pairs, total = steps // 2, sum(CHUNKS)
-    bounds, done = [0], 0
-    for share in CHUNKS:
+    pairs, total = steps // 2, sum(share for _, share in CHUNKS)
+    out, done, at = [], 0, 0
+    for kind, share in CHUNKS:
         done += share
-        bounds.append(round(pairs * done / total))
-    return [(2 * a, 2 * (b - a)) for a, b in zip(bounds, bounds[1:]) if b > a]
+        to = round(pairs * done / total)
+        if to > at:
+            out.append((kind, 2 * at, 2 * (to - at)))
+        at = to
+    return out
 
 
 def gate_kernel(*refs):
@@ -54,37 +56,31 @@
     return result[:count], result[count]
 
 
-def merge_kernel(count, place_ref, *refs):
-    pieces, (out_ref, sems) = refs[:count], refs[-2:]
-    copies = []
-    for k, piece in enumerate(pieces):
+def merge_kernel(place_ref, *refs):
+    for k, piece in enumerate(refs[:-1]):
         rows = piece.shape[0]
         at = pl.multiple_of(place_ref[k], rows)
-        copies.append(pltpu.make_async_copy(piece, out_ref.at[pl.ds(at, rows), :], sems.at[k]))
-        copies[-1].start()
-    for copy in copies:
-        copy.wait()
-
-
-def merge_call(places, pieces, ticks):
-    count = len(pieces)
+        refs[-1][pl.ds(at, rows), :] = piece[...]
+
+
+def merge_call(places, pieces):
     tokens = sum(piece.shape[0] for piece in pieces)
     width = pieces[0].shape[1]
     return pl.pallas_call(
-        functools.partial(merge_kernel, count),
+        merge_kernel,
         grid_spec=pltpu.PrefetchScalarGridSpec(
             num_scalar_prefetch=1,
-            grid=(1,),
-            in_specs=[ANYWHERE] * (count + len(ticks)),
-            out_specs=ANYWHERE,
-            scratch_shapes=[pltpu.SemaphoreType.DMA((count,))],
+            grid=(width // STEP,),
+            in_specs=[pl.BlockSpec((p.shape[0], STEP), lambda s, _: (0, s)) for p in pieces],
+            out_specs=pl.BlockSpec((tokens, STEP), lambda s, _: (0, s)),
         ),
         out_shape=jax.ShapeDtypeStruct((tokens, width), pieces[0].dtype),
+        compiler_params=pltpu.CompilerParams(vmem_limit_bytes=VMEM_LIMIT),
         cost_estimate=pl.CostEstimate(
             flops=0, bytes_accessed=4 * tokens * width, transcendentals=0
         ),
         name="merge",
-    )(places, *pieces, *ticks)
+    )(places, *pieces)
 
 
 def chunk_kernel(scale, halves, half_steps, with_share, first, n_ticks, off_ref, *refs):
@@ -122,9 +118,7 @@
                 def _():
                     pltpu.make_async_copy(acc_in, acc_ref, in_sem).wait()
 
-            acc_ref[...] += lax.dot_general(
-                hg_ref[...], w_ref[...], NT, preferred_element_type=jnp.float32
-            )
+            acc_ref[...] += jnp.dot(hg_ref[...], w_ref[...], preferred_element_type=jnp.float32)
 
             @pl.when(step == steps - 1)
             def _():
@@ -141,9 +135,10 @@
         for j in range(cols // BLOCK):
             at = (pl.ds(i * BLOCK, BLOCK), pl.ds(j * BLOCK, BLOCK))
             tile = wg_ref[at]
-            left = lax.dot_general(tile, tile, NT, preferred_element_type=jnp.float32)
+            flipped = tile.T
+            left = jnp.dot(tile, flipped, preferred_element_type=jnp.float32)
             left_ref[at] = (left * scale).astype(left_ref.dtype)
-            right = lax.dot_general(tile, tile, TN, preferred_element_type=jnp.float32)
+            right = jnp.dot(flipped, tile, preferred_element_type=jnp.float32)
             right_ref[at] = (right * scale).astype(right_ref.dtype)
 
     if with_share:
@@ -153,8 +148,9 @@
             pltpu.make_async_copy(acc_ref, acc_out, out_sem).wait()
 
 
-def chunk_call(scale, offs, x_t, hgs, weight, acc, outs, ticks, with_share):
+def chunk_call(scale, offs, x_t, hgs, weight_t, acc, outs, ticks, with_share):
     rows, tokens = x_t.shape
+    columns = weight_t.shape[0]
     halves, half_steps = len(hgs), hgs[0].shape[1] // STEP
     first = outs is None
 
@@ -167,14 +163,14 @@
     args = [x_t] + hgs
     in_specs = [pl.BlockSpec((rows, tokens), lambda s, off: (0, 0))]
     in_specs += [pl.BlockSpec((tokens, STEP), part(k)) for k in range(halves)]
-    out_shape = [jax.ShapeDtypeStruct(weight.shape, jnp.bfloat16)] * 3 + [TICK]
+    out_shape = [jax.ShapeDtypeStruct((rows, columns), jnp.bfloat16)] * 3 + [TICK]
     out_specs = [pl.BlockSpec((rows, STEP), at)] * 3
     out_specs.append(pl.BlockSpec(TICK.shape, lambda s, off: (0, 0)))
     scratch = []
     aliases = {}
     if with_share:
-        args.append(weight)
-        in_specs.append(pl.BlockSpec((rows, STEP), at))
+        args.append(weight_t)
+        in_specs.append(pl.BlockSpec((STEP, rows), lambda s, off: at(s, off)[::-1]))
         out_shape.append(jax.ShapeDtypeStruct((tokens, rows), jnp.float32))
         out_specs.append(ANYWHERE)
         scratch += [
@@ -215,23 +211,21 @@
     )(offs, *args)
 
 
-def share_kernel(groups, group, half_steps, who_ref, off_ref, *refs):
-    own_hg, other_hg, w_ref, acc_ref, away_ref, own_ref, sum_ref = refs
+def share_kernel(groups, group, halves, half_steps, who_ref, off_ref, *refs):
+    w_ref, acc_ref, away_ref, own_ref, sum_ref = refs[halves:]
     step = pl.program_id(0)
 
     @pl.when(step == 0)
     def _():
         sum_ref[...] = acc_ref[...]
 
-    for k, hg_ref in enumerate((own_hg, other_hg)):
+    for k in range(halves):
 
         @pl.when(step // half_steps == k)
-        def _(hg_ref=hg_ref):
-            sum_ref[...] += lax.dot_general(
-                hg_ref[...], w_ref[...], NT, preferred_element_type=jnp.float32
-            )
-
-    @pl.when(step == 2 * half_steps - 1)
+        def _(hg_ref=refs[k]):
+            sum_ref[...] += jnp.dot(hg_ref[...], w_ref[...], preferred_element_type=jnp.float32)
+
+    @pl.when(step == halves * half_steps - 1)
     def _():
         for k in range(groups):
             at = pl.multiple_of(who_ref[k] * group, group)
@@ -242,25 +236,25 @@
                 own_ref[...] = part
 
 
-def share_call(who, offs, hgs, weight, acc, groups):
+def share_call(who, offs, hgs, weight_t, acc, groups):
     tokens, rows = acc.shape
     group = tokens // groups
-    half_steps = hgs[0].shape[1] // STEP
+    halves, half_steps = len(hgs), hgs[0].shape[1] // STEP
+    steps = halves * half_steps
 
     def part(k):
         return lambda s, who, off: (0, jnp.clip(s - k * half_steps, 0, half_steps - 1))
 
     return pl.pallas_call(
-        functools.partial(share_kernel, groups, group, half_steps),
+        functools.partial(share_kernel, groups, group, halves, half_steps),
         grid_spec=pltpu.PrefetchScalarGridSpec(
             num_scalar_prefetch=2,
-            grid=(2 * half_steps,),
-            in_specs=[
-                pl.BlockSpec((tokens, STEP), part(0)),
-                pl.BlockSpec((tokens, STEP), part(1)),
+            grid=(steps,),
+            in_specs=[pl.BlockSpec((tokens, STEP), part(k)) for k in range(halves)]
+            + [
                 pl.BlockSpec(
-                    (rows, STEP),
-                    lambda s, who, off: (0, off[s // half_steps] + s % half_steps),
+                    (STEP, rows),
+                    lambda s, who, off: (off[s // half_steps] + s % half_steps, 0),
                 ),
                 pl.BlockSpec((tokens, rows), lambda s, *_: (0, 0)),
             ],
@@ -276,12 +270,12 @@
         ],
         compiler_params=pltpu.CompilerParams(vmem_limit_bytes=VMEM_LIMIT),
         cost_estimate=pl.CostEstimate(
-            flops=4 * tokens * half_steps * STEP * rows,
-            bytes_accessed=4 * half_steps * STEP * (rows + tokens) + 8 * tokens * rows,
+            flops=2 * tokens * steps * STEP * rows,
+            bytes_accessed=2 * steps * STEP * (rows + tokens) + 8 * tokens * rows,
             transcendentals=0,
         ),
         name="share",
-    )(who, offs, *hgs, weight, acc)
+    )(who, offs, *hgs, weight_t, acc)
 
 
 class Ring:
@@ -349,18 +343,25 @@
         g = lax.dynamic_slice_in_dim(out_grad, start, width, 1).astype(jnp.float32)
         return (g * gelu_slope(h)).astype(jnp.bfloat16)
 
-    def stream_of(chunk):
-        first, half = chunk[0] * STEP, chunk[1] * STEP // 2
+    def ring_piece(first, half):
         got = ring.swap(hidden_of(first + (1 - core) * half, half))
         mine = hidden_of(first + core * half, half)
         upper, lower = jnp.where(core == 0, mine, got), jnp.where(core == 0, got, mine)
-        return Stream(ring, jnp.concatenate([upper, lower], axis=0))
-
-    streams = [stream_of(chunk) for chunk in chunks]
-    offsets = [
-        jnp.stack([a + core * (n // 2), a + (1 - core) * (n // 2)]).astype(jnp.int32)
-        for a, n in chunks
-    ]
+        return jnp.concatenate([upper, lower], axis=0)
+
+    streams, held, offsets, sent = {}, {}, {}, []
+    for k, (kind, first, steps) in enumerate(chunks):
+        if kind == RING:
+            streams[k] = Stream(ring, ring_piece(first * STEP, steps * STEP // 2))
+            half = steps // 2
+            offsets[k] = jnp.stack([first + core * half, first + (1 - core) * half])
+        else:
+            hidden = hidden_of(first * STEP, steps * STEP)
+            sent.append(hidden)
+            held[k] = [lax.all_gather(hidden, "row", axis=0, tiled=True)]
+            offsets[k] = jnp.full((1,), first)
+        offsets[k] = offsets[k].astype(jnp.int32)
+    weight_t = weight.T
 
     own_t = tokens.T
     x_t = jnp.zeros((rows, num_tokens), jnp.bfloat16)
@@ -369,44 +370,46 @@
         piece = lax.ppermute(own_t, "col", [(i, (i + s) % cols) for i in range(cols)])
         x_t = lax.dynamic_update_slice(x_t, piece, (0, (me - s) % cols * group))
 
-    def advance(k, upto, ticks):
-        out = []
-        if k < len(streams):
-            while streams[k].hop < upto:
-                if ticks:
-                    out = [streams[k].gate(ticks)]
-                streams[k].advance()
-        return out
+    def advance(k, hops, ticks=()):
+        for _ in range(hops):
+            if ticks:
+                streams[k].gate(list(ticks))
+                ticks = ()
+            streams[k].advance()
+
+    def collect(k):
+        own = merge_call(places, streams[k].pieces())
+        held[k] = [own, ring.swap(own)]
 
     half, last = ring.hops // 2, len(chunks) - 1
-    advance(0, half, [])
-    if last:
-        advance(0, half + 1, [streams[1].fresh[0]])
-    advance(1, half, [])
-    advance(0, ring.hops, [])
+    early = [k for k in streams if k < last]
+    for k in early:
+        advance(k, ring.hops - 1, sent)
+    for k in streams:
+        if k not in early:
+            advance(k, half, [streams[e].fresh[0] for e in early])
+    for k in early:
+        advance(k, 1)
+        collect(k)
+
     acc, outs, ticks = None, None, []
-    for k in range(len(chunks)):
-        seen = advance(k + 1, half + 1, ticks) + advance(k + 2, 1, ticks)
-        own = merge_call(places, streams[k].pieces(), seen)
-        other = ring.swap(own)
-        offs = offsets[k]
-        if k < last:
-            *outs, tick, acc = chunk_call(
-                scale, offs[:1], x_t, [own], weight, acc, outs, seen, True
-            )
-            seen = advance(k + 1, ring.hops, [tick]) + advance(k + 2, half, [tick])
-            *outs, tick, acc = chunk_call(
-                scale, offs[1:], x_t, [other], weight, acc, outs, seen, True
-            )
-            ticks = [tick]
+    for k in range(last):
+        if k == last - 1 and last in streams:
+            advance(last, ring.hops - half, ticks)
+            collect(last)
+            ticks = ticks + [held[last][0]]
+        *outs, tick, acc = chunk_call(
+            scale, offsets[k], x_t, held[k], weight_t, acc, outs, ticks, True
+        )
+        ticks = [tick]
     who = (me + jnp.arange(cols, dtype=jnp.int32)) % cols
-    away, share = share_call(who, offs, [own, other], weight, acc, cols)
+    away, share = share_call(who, offsets[last], held[last], weight_t, acc, cols)
     arrived = [
         lax.ppermute(away[s - 1], "col", [(i, (i + s) % cols) for i in range(cols)])
         for s in range(1, cols)
     ]
     *outs, tick = chunk_call(
-        scale, offs, x_t, [own, other], weight, None, outs, [share], False
+        scale, offsets[last], x_t, held[last], weight_t, None, outs, [share], False
     )
     for piece in arrived:
         share = share + piece.astype(jnp.float32)

time: 657 us -> 276 us (0.42); the launches traced: 649 us -> 275 us
  Pallas kernels: 516 us -> 107 us
  waiting for transfers between devices: 39.2 us -> 80.9 us
  starting transfers between devices: 47.1 us -> 29.2 us
  between operations: 1.51 us -> 14.3 us
    pallas_call x6 -> x3, Pallas kernels: 399 us -> 25.1 us  [the longest x1 15 us: share_call(): pl.pallas_call(functools.partial(share_kernel, groups, group, halves, hal...]
    ppermute x40 -> x16, waiting for transfers between devices: 30.3 us -> 77.4 us  [shift(): return lax.ppermute(value, 'row', pairs)]
    pallas_call x9 -> x3, Pallas kernels: 117 us -> 81.9 us  [chunk_call(): pl.pallas_call(functools.partial(chunk_kernel, scale, halves, half_steps,...]
    ppermute x40 -> x16, starting transfers between devices: 42 us -> 24.9 us  [shift(): return lax.ppermute(value, 'row', pairs)]
    unnamed x75 -> x36, local copies, waits for them, and re-layouts: 16.3 us -> 27.4 us
    ppermute x1, waiting for transfers between devices: 8.82 us -> 0.01 us  [on_device(): lax.ppermute(away[s - 1], 'col', [(i, (i + s) % cols) for i in range(cols)])]
    slice x10 -> x4, local copies, waits for them, and re-layouts: 10.2 us -> 1.51 us  [advance(): ahead, behind = (ahead[:half], behind[half:])]
  transfers between devices with their start and end apart: 52 -> 23, of which waited for: 10 -> 9; matrix products, arithmetic and copies ran while one was open for 4% -> 13% of each run, Pallas kernels for 33% -> 33%
where the time goes in v4:
time: 276 us; the launch traced here: 275 us
  Pallas kernels  107 us (39%)
  waiting for transfers between devices  80.9 us (29%)
  local copies, waits for them, and re-layouts  30.5 us (11%)
  starting transfers between devices  29.2 us (11%)
  between operations  14.3 us (5%)
  other arithmetic  13 us (5%)
    pallas_call x3, Pallas kernels, chunk_call(): pl.pallas_call(functools.partial(chunk_kernel, scale, halves, half_steps,...  81.9 us
    ppermute x16, waiting for transfers between devices, shift(): return lax.ppermute(value, 'row', pairs)  77.4 us
    unnamed x36, local copies, waits for them, and re-layouts  27.4 us
    ppermute x16, starting transfers between devices, shift(): return lax.ppermute(value, 'row', pairs)  24.9 us
    pallas_call x1, Pallas kernels, share_call(): pl.pallas_call(functools.partial(share_kernel, groups, group, halves, hal...  15 us
    pallas_call x2, Pallas kernels, merge_call(): pl.pallas_call(merge_kernel, grid_spec=pltpu.PrefetchScalarGridSpec(num_s...  10.1 us
    convert_element_type x3, other arithmetic, hidden_of(): return (g * gelu_slope(h)).astype(jnp.bfloat16)  6.34 us
  transfers between devices with their start and end apart: 23, of which 9 were waited for; matrix products, arithmetic and copies ran while one was open for 13% of the time, Pallas kernels for 33%

profile of v4, /device:TPU:0, one launch (start us, length us, event | category | flops | bytes accessed | tf_op | source)
XLA Modules:
  0.0 274.9 jit_solution(282819236539018154)
XLA Ops:
  7.2 0.0 all-gather.2.cloned.1.call-start
  7.2 3.0 %fusion.7.refs_1_ = bf16[64,4608]{1,0:T(8,128)(2,1)} fusion(bf16[64,12288]{1,0:T(8,128)(2,1)} %param.7, bf16[64,12288]{1,0:T(8,128)(2,1)} %param.8), kind=kLoop, calls=%fused_computation.29 | loop fusion | flops 6193152 | bytes 1769472 | tf_op jit(solution)/shard_map/convert_element_type | solution.py:344
  10.2 0.0 all-gather.2.cloned.1.call-update
  10.3 1.2 fusion.43
  11.5 0.5 collective-permute-start.1
  12.0 1.1 collective-permute-done.1
  13.1 1.2 broadcast_select_fusion.3
  14.4 0.8 pad_maximum_fusion.1.refs_0_
  15.2 2.9 %collective-permute-start.10 = (bf16[128,1536]{1,0:T(8,128)(2,1)}, bf16[128,1536]{1,0:T(8,128)(2,1)S(1)}, u32[]{:S(2)}, u32[]{:S(2)}) collective-permute-start(bf16[128,1536]{1,0:T(8,128)(2,1)} %get-tuple-element.22.refs_0_), channel_id=1, source_target_pairs={{0,4},{2,6},{8,0},{10,2},{16,8},{18,10},{24,16},{26,18},{28,24},{3... | collective-permute-start | bytes 1179656 | tf_op jit(solution)/shard_map/ppermute | solution.py:292
  18.0 0.1 collective-permute-start.2
  18.1 17.2 %collective-permute-done.10.refs_2_ = bf16[128,1536]{1,0:T(8,128)(2,1)S(1)} collective-permute-done((bf16[128,1536]{1,0:T(8,128)(2,1)}, bf16[128,1536]{1,0:T(8,128)(2,1)S(1)}, u32[]{:S(2)}, u32[]{:S(2)}) %collective-permute-start.10) | collective-permute-done | bytes 393248 | tf_op jit(solution)/shard_map/ppermute | solution.py:292
  35.3 0.0 copy-start.11
  35.3 5.1 %collective-permute-start.3 = (bf16[128,1536]{1,0:T(8,128)(2,1)S(1)}, bf16[128,1536]{1,0:T(8,128)(2,1)S(1)}, u32[]{:S(2)}, u32[]{:S(2)}) collective-permute-start(bf16[128,1536]{1,0:T(8,128)(2,1)S(1)} %collective-permute-done.2.refs_1_), channel_id=1, source_target_pairs={{0,8},{2,10},{8,16},{10,18},{16,24},{18,26},{24,28},{26,30},{28,20... | collective-permute-start | bytes 1179656 | tf_op jit(solution)/shard_map/ppermute | solution.py:292
  40.4 14.7 %collective-permute-done.11.refs_4_ = bf16[128,1536]{1,0:T(8,128)(2,1)S(1)} collective-permute-done((bf16[128,1536]{1,0:T(8,128)(2,1)S(1)}, bf16[128,1536]{1,0:T(8,128)(2,1)S(1)}, u32[]{:S(2)}, u32[]{:S(2)}) %collective-permute-start.11) | collective-permute-done | bytes 393248 | tf_op jit(solution)/shard_map/ppermute | solution.py:292
  55.1 0.8 collective-permute-start.12
  55.9 1.3 collective-permute-start.4
  57.2 16.0 %collective-permute-done.12.refs_6_ = bf16[128,1536]{1,0:T(8,128)(2,1)S(1)} collective-permute-done((bf16[128,1536]{1,0:T(8,128)(2,1)S(1)}, bf16[128,1536]{1,0:T(8,128)(2,1)S(1)}, u32[]{:S(2)}, u32[]{:S(2)}) %collective-permute-start.12) | collective-permute-done | bytes 393248 | tf_op jit(solution)/shard_map/ppermute | solution.py:292
  73.3 0.7 slice.17
  74.0 0.0 collective-permute-start.14
  74.0 0.0 collective-permute-done.4.refs_1_.refs_5_
  74.0 0.0 copy-start.2
  74.0 0.7 slice.16
  74.8 2.4 collective-permute-start.13
  77.2 1.2 fusion.46.place_ref
  78.4 11.2 %collective-permute-done.14.refs_8_ = bf16[64,1536]{1,0:T(8,128)(2,1)S(1)} collective-permute-done((bf16[64,1536]{1,0:T(8,128)(2,1)}, bf16[64,1536]{1,0:T(8,128)(2,1)S(1)}, u32[]{:S(2)}, u32[]{:S(2)}) %collective-permute-start.14) | collective-permute-done | bytes 196640 | tf_op jit(solution)/shard_map/ppermute | solution.py:292
  89.6 0.0 collective-permute-done.13.refs_7_
  89.6 0.7 copy-done.16
  90.3 4.0 %merge.2.refs_1_ = bf16[1024,1536]{1,0:T(8,128)(2,1)} custom-call(s32[9]{0:T(128)} %fusion.46.place_ref, bf16[128,1536]{1,0:T(8,128)(2,1)} %get-tuple-element.22.refs_0_, bf16[128,1536]{1,0:T(8,128)(2,1)} %copy-done.11, bf16[128,1536]{1,0:T(8,128)(2,1)} %copy-done.10, bf16[128,1536]{1,0:T(8,128)(2,1)} %copy-done.13, bf16[128,1536]{1,0:T(8,128)(2,1)} %copy-done.12, ...), custom_call_target="tpu_custom_call" | custom-call | bytes 6291456 | tf_op jit(solution)/shard_map/merge/pallas_call | solution.py:69
  94.3 2.1 fusion.25
  96.4 0.5 collective-permute-start
  96.9 0.3 copy.19
  97.2 1.4 collective-permute-start.9
  98.6 2.4 collective-permute-done
  101.0 1.4 broadcast_select_fusion.1
  102.5 0.9 pad_maximum_fusion.refs_0_
  103.3 5.9 %collective-permute-start.6 = (bf16[128,2304]{1,0:T(8,128)(2,1)}, bf16[128,2304]{1,0:T(8,128)(2,1)}, u32[]{:S(2)}, u32[]{:S(2)}) collective-permute-start(bf16[128,2304]{1,0:T(8,128)(2,1)} %get-tuple-element.23.refs_0_), channel_id=1, source_target_pairs={{0,4},{2,6},{8,0},{10,2},{16,8},{18,10},{24,16},{26,18},{28,24},{3... | collective-permute-start | bytes 1769480 | tf_op jit(solution)/shard_map/ppermute | solution.py:292
  109.3 24.5 %copy.20 = bf16[768,12288]{0,1:T(8,128)(2,1)} copy(bf16[768,12288]{1,0:T(8,128)(2,1)} %param.6) | data formatting | bytes 37748736 | tf_op args[1]
  133.8 0.7 pad_add_fusion.1.off_ref
  134.4 0.2 broadcast_in_dim.3
  134.6 0.1 constant_dynamic-update-slice_fusion.1
  134.7 0.1 constant_dynamic-update-slice_fusion.refs_0_
  134.9 0.0 collective-permute-done.6.refs_2_
  134.9 2.0 collective-permute-start.8
  136.8 0.1 collective-permute-start.7
  137.0 0.0 collective-permute-done.15.refs_2_
  137.0 23.0 %chunk.3 = (bf16[768,12288]{1,0:T(8,128)(2,1)}, bf16[768,12288]{1,0:T(8,128)(2,1)}, bf16[768,12288]{1,0:T(8,128)(2,1)}, f32[8,128]{1,0:T(8,128)}, f32[1024,768]{1,0:T(8,128)}) custom-call(s32[2]{0:T(128)} %pad_add_fusion.1.off_ref, bf16[768,1024]{1,0:T(8,128)(2,1)} %copy-done, bf16[1024,1536]{1,0:T(8,128)(2,1)} %merge.2.refs_1_, ...), custom_call_target="tpu_custom_call" | custom-call | flops 13287555072 | bytes 25165824 | tf_op jit(solution)/shard_map/chunk/pallas_call | solution.py:191
  160.0 0.8 copy-done.3
  160.8 0.2 copy-done.4
  161.0 0.0 collective-permute-start.16
  161.0 2.0 collective-permute-start.17
  163.0 12.7 %collective-permute-done.16.refs_5_ = bf16[128,2304]{1,0:T(8,128)(2,1)S(1)} collective-permute-done((bf16[128,2304]{1,0:T(8,128)(2,1)}, bf16[128,2304]{1,0:T(8,128)(2,1)S(1)}, u32[]{:S(2)}, u32[]{:S(2)}) %collective-permute-start.16) | collective-permute-done | bytes 589856 | tf_op jit(solution)/shard_map/ppermute | solution.py:292
  175.7 0.3 collective-permute-start.18
  176.1 2.0 collective-permute-start.19
  178.0 5.0 %collective-permute-done.18.refs_7_ = bf16[64,2304]{1,0:T(8,128)(2,1)S(1)} collective-permute-done((bf16[64,2304]{1,0:T(8,128)(2,1)S(1)}, bf16[64,2304]{1,0:T(8,128)(2,1)S(1)}, u32[]{:S(2)}, u32[]{:S(2)}) %collective-permute-start.18) | collective-permute-done | bytes 294944 | tf_op jit(solution)/shard_map/ppermute | solution.py:292
  183.0 0.5 collective-permute-done.19.refs_8_
  183.5 0.2 copy-done.14
  183.7 0.7 copy-done.15
  184.4 6.1 %merge.3.refs_5_.refs_0_.refs_1_ = bf16[1024,2304]{1,0:T(8,128)(2,1)} custom-call(s32[9]{0:T(128)} %fusion.46.place_ref, bf16[128,2304]{1,0:T(8,128)(2,1)} %get-tuple-element.23.refs_0_, bf16[128,2304]{1,0:T(8,128)(2,1)} %collective-permute-done.5.refs_1_, bf16[128,2304]{1,0:T(8,128)(2,1)} %collective-permute-done.6.refs_2_, ...), custom_call_target="tpu_custom_call" | custom-call | bytes 9437184 | tf_op jit(solution)/shard_map/merge/pallas_call | solution.py:69
  190.6 0.6 and_select_fusion
  191.1 35.2 %chunk.4 = (bf16[768,12288]{1,0:T(8,128)(2,1)}, bf16[768,12288]{1,0:T(8,128)(2,1)}, bf16[768,12288]{1,0:T(8,128)(2,1)}, f32[8,128]{1,0:T(8,128)}, f32[1024,768]{1,0:T(8,128)}) custom-call(s32[1]{0:T(128)} %constant.83.clone.1.off_ref, bf16[768,1024]{1,0:T(8,128)(2,1)} %copy-done, ...), custom_call_target="tpu_custom_call", output_to_operand_aliasing={{0}: (7, {}), {1}: (8, {}), {2}: (9, {})} | custom-call | flops 19931332608 | bytes 37748736 | tf_op jit(solution)/shard_map/chunk/pallas_call | solution.py:191
  226.3 15.0 %share.1 = (bf16[1,512,768]{2,1,0:T(8,128)(2,1)}, f32[512,768]{1,0:T(8,128)}) custom-call(s32[2]{0:T(128)} %get-tuple-element.44.who_ref, s32[2]{0:T(128)} %get-tuple-element.45.off_ref, bf16[1024,2304]{1,0:T(8,128)(2,1)} %merge.3.refs_5_.refs_0_.refs_1_, bf16[1024,2304]{1,0:T(8,128)(2,1)} %collective-permute-done.20.refs_1_.refs_2_, ...), custom_call_target="tpu_custom_call" | custom-call | flops 7247757312 | bytes 22806528 | tf_op jit(solution)/shard_map/share/pallas_call | solution.py:248
  241.3 1.8 collective-permute-start.21
  243.2 23.8 %chunk.5 = (bf16[768,12288]{1,0:T(8,128)(2,1)}, bf16[768,12288]{1,0:T(8,128)(2,1)}, bf16[768,12288]{1,0:T(8,128)(2,1)}, f32[8,128]{1,0:T(8,128)}) custom-call(s32[2]{0:T(128)} %get-tuple-element.45.off_ref, bf16[768,1024]{1,0:T(8,128)(2,1)} %copy-done, ...), custom_call_target="tpu_custom_call", output_to_operand_aliasing={{0}: (5, {}), {1}: (6, {}), {2}: (7, {})} | custom-call | flops 12683575296 | bytes 37748736 | tf_op jit(solution)/shard_map/chunk/pallas_call | solution.py:191
  267.0 1.0 add_convert_fusion
  (48 shorter events, 0.2 us)
Async XLA Ops:
  7.2 3.1 %copy-start.5 = (bf16[64,12288]{1,0:T(8,128)(2,1)S(1)}, bf16[64,12288]{1,0:T(8,128)(2,1)}, u32[]{:S(2)}) copy-start(bf16[64,12288]{1,0:T(8,128)(2,1)} %param.7) | copy-start | bytes 4718596
  7.2 184.0 %all-gather.2.cloned.1.call-start = ((), (), s32[]{:S(2)}) async-start(), calls=%async_computation | async-start | bytes 10027008 | tf_op jit(solution)/shard_map/all_gather | solution.py:361
  11.5 1.6 collective-permute-start.1
  15.2 20.1 %collective-permute-start.10 = (bf16[128,1536]{1,0:T(8,128)(2,1)}, bf16[128,1536]{1,0:T(8,128)(2,1)S(1)}, u32[]{:S(2)}, u32[]{:S(2)}) collective-permute-start(bf16[128,1536]{1,0:T(8,128)(2,1)} %get-tuple-element.22.refs_0_), channel_id=1, source_target_pairs={{0,4},{2,6},{8,0},{10,2},{16,8},{18,10},{24,16},{26,18},{28,24},{3... | collective-permute-start | bytes 1179656 | tf_op jit(solution)/shard_map/ppermute | solution.py:292
  18.0 17.3 %collective-permute-start.2 = (bf16[128,1536]{1,0:T(8,128)(2,1)}, bf16[128,1536]{1,0:T(8,128)(2,1)S(1)}, u32[]{:S(2)}, u32[]{:S(2)}) collective-permute-start(bf16[128,1536]{1,0:T(8,128)(2,1)} %get-tuple-element.22.refs_0_), channel_id=1, source_target_pairs={{0,8},{2,10},{8,16},{10,18},{16,24},{18,26},{24,28},{26,30},{28,20... | collective-permute-start | bytes 1179656 | tf_op jit(solution)/shard_map/ppermute | solution.py:292
  35.3 20.6 %copy-start.10 = (bf16[128,1536]{1,0:T(8,128)(2,1)}, bf16[128,1536]{1,0:T(8,128)(2,1)S(1)}, u32[]{:S(2)}) copy-start(bf16[128,1536]{1,0:T(8,128)(2,1)S(1)} %collective-permute-done.10.refs_2_) | copy-start | bytes 1179652
  35.3 19.8 %collective-permute-start.11 = (bf16[128,1536]{1,0:T(8,128)(2,1)S(1)}, bf16[128,1536]{1,0:T(8,128)(2,1)S(1)}, u32[]{:S(2)}, u32[]{:S(2)}) collective-permute-start(bf16[128,1536]{1,0:T(8,128)(2,1)S(1)} %collective-permute-done.10.refs_2_), channel_id=1, source_target_pairs={{0,4},{2,6},{8,0},{10,2},{16,8},{18,10},{24,16},{26,18},{28,24},{3... | collective-permute-start | bytes 1179656 | tf_op jit(solution)/shard_map/ppermute | solution.py:292
  35.3 20.6 %copy-start.11 = (bf16[128,1536]{1,0:T(8,128)(2,1)}, bf16[128,1536]{1,0:T(8,128)(2,1)S(1)}, u32[]{:S(2)}) copy-start(bf16[128,1536]{1,0:T(8,128)(2,1)S(1)} %collective-permute-done.2.refs_1_) | copy-start | bytes 1179652
  35.3 20.6 %collective-permute-start.3 = (bf16[128,1536]{1,0:T(8,128)(2,1)S(1)}, bf16[128,1536]{1,0:T(8,128)(2,1)S(1)}, u32[]{:S(2)}, u32[]{:S(2)}) collective-permute-start(bf16[128,1536]{1,0:T(8,128)(2,1)S(1)} %collective-permute-done.2.refs_1_), channel_id=1, source_target_pairs={{0,8},{2,10},{8,16},{10,18},{16,24},{18,26},{24,28},{26,30},{28,20... | collective-permute-start | bytes 1179656 | tf_op jit(solution)/shard_map/ppermute | solution.py:292
  55.1 2.1 copy-start.12
  55.1 18.1 %collective-permute-start.12 = (bf16[128,1536]{1,0:T(8,128)(2,1)S(1)}, bf16[128,1536]{1,0:T(8,128)(2,1)S(1)}, u32[]{:S(2)}, u32[]{:S(2)}) collective-permute-start(bf16[128,1536]{1,0:T(8,128)(2,1)S(1)} %collective-permute-done.11.refs_4_), channel_id=1, source_target_pairs={{0,4},{2,6},{8,0},{10,2},{16,8},{18,10},{24,16},{26,18},{28,24},{3... | collective-permute-start | bytes 1179656 | tf_op jit(solution)/shard_map/ppermute | solution.py:292
  55.9 18.1 %copy-start.13 = (bf16[128,1536]{1,0:T(8,128)(2,1)}, bf16[128,1536]{1,0:T(8,128)(2,1)S(1)}, u32[]{:S(2)}) copy-start(bf16[128,1536]{1,0:T(8,128)(2,1)S(1)} %collective-permute-done.3.refs_3_) | copy-start | bytes 1179652
  55.9 18.1 %collective-permute-start.4 = (bf16[128,1536]{1,0:T(8,128)(2,1)S(1)}, bf16[128,1536]{1,0:T(8,128)(2,1)S(1)}, u32[]{:S(2)}, u32[]{:S(2)}) collective-permute-start(bf16[128,1536]{1,0:T(8,128)(2,1)S(1)} %collective-permute-done.3.refs_3_), channel_id=1, source_target_pairs={{0,8},{2,10},{8,16},{10,18},{16,24},{18,26},{24,28},{26,30},{28,20... | collective-permute-start | bytes 1179656 | tf_op jit(solution)/shard_map/ppermute | solution.py:292
  73.3 16.4 %copy-start.8 = (bf16[128,1536]{1,0:T(8,128)(2,1)}, bf16[128,1536]{1,0:T(8,128)(2,1)S(1)}, u32[]{:S(2)}) copy-start(bf16[128,1536]{1,0:T(8,128)(2,1)S(1)} %collective-permute-done.12.refs_6_) | copy-start | bytes 1179652
  74.0 15.6 %collective-permute-start.14 = (bf16[64,1536]{1,0:T(8,128)(2,1)}, bf16[64,1536]{1,0:T(8,128)(2,1)S(1)}, u32[]{:S(2)}, u32[]{:S(2)}) collective-permute-start(bf16[64,1536]{1,0:T(8,128)(2,1)} %slice.17), channel_id=1, source_target_pairs={{0,4},{2,6},{8,0},{10,2},{16,8},{18,10},{24,16},{26,18},{28,24},{3... | collective-permute-start | bytes 589832 | tf_op jit(solution)/shard_map/ppermute | solution.py:292
  74.0 15.6 %copy-start.2 = (bf16[128,1536]{1,0:T(8,128)(2,1)}, bf16[128,1536]{1,0:T(8,128)(2,1)S(1)}, u32[]{:S(2)}) copy-start(bf16[128,1536]{1,0:T(8,128)(2,1)S(1)} %collective-permute-done.4.refs_1_.refs_5_) | copy-start | bytes 1179652
  74.8 14.9 %collective-permute-start.13 = (bf16[64,1536]{1,0:T(8,128)(2,1)}, bf16[64,1536]{1,0:T(8,128)(2,1)}, u32[]{:S(2)}, u32[]{:S(2)}) collective-permute-start(bf16[64,1536]{1,0:T(8,128)(2,1)} %slice.16), channel_id=1, source_target_pairs={{0,8},{2,10},{8,16},{10,18},{16,24},{18,26},{24,28},{26,30},{28,20... | collective-permute-start | bytes 589832 | tf_op jit(solution)/shard_map/ppermute | solution.py:292
  78.4 18.5 %copy-start.9 = (bf16[512,768]{1,0:T(8,128)(2,1)S(1)}, bf16[512,768]{1,0:T(8,128)(2,1)}, u32[]{:S(2)}) copy-start(bf16[512,768]{1,0:T(8,128)(2,1)} %param.5) | copy-start | bytes 2359300
  89.6 0.7 copy-start.16
  94.3 42.7 %collective-permute-start.15 = (bf16[1024,1536]{1,0:T(8,128)(2,1)}, bf16[1024,1536]{1,0:T(8,128)(2,1)}, u32[]{:S(2)}, u32[]{:S(2)}) collective-permute-start(bf16[1024,1536]{1,0:T(8,128)(2,1)} %merge.2.refs_1_), channel_id=1, source_target_pairs={{0,2},{2,0},{4,6},{6,4},{8,10},{10,8},{12,14},{14,12},{16,18},{18,... | collective-permute-start | bytes 9437192 | tf_op jit(solution)/shard_map/ppermute | solution.py:295
  96.4 4.6 %collective-permute-start = (bf16[64,2304]{1,0:T(8,128)(2,1)}, bf16[64,2304]{1,0:T(8,128)(2,1)S(1)}, u32[]{:S(2)}, u32[]{:S(2)}) collective-permute-start(bf16[64,2304]{1,0:T(8,128)(2,1)} %fusion.25), channel_id=1, source_target_pairs={{0,2},{2,0},{4,6},{6,4},{8,10},{10,8},{12,14},{14,12},{16,18},{18,... | collective-permute-start | bytes 884744 | tf_op jit(solution)/shard_map/ppermute | solution.py:295
  97.2 37.6 %collective-permute-start.9 = (bf16[768,512]{1,0:T(8,128)(2,1)S(1)}, bf16[768,512]{1,0:T(8,128)(2,1)S(1)}, u32[]{:S(2)}, u32[]{:S(2)}) collective-permute-start(bf16[768,512]{1,0:T(8,128)(2,1)S(1)} %bitcast.13), channel_id=1, source_target_pairs={{0,1},{1,0},{2,3},{3,2},{4,5},{5,4},{6,7},{7,6},{8,9},{9,8},{10,11... | collective-permute-start | bytes 2359304 | tf_op jit(solution)/shard_map/ppermute | solution.py:370
  103.3 31.5 %collective-permute-start.6 = (bf16[128,2304]{1,0:T(8,128)(2,1)}, bf16[128,2304]{1,0:T(8,128)(2,1)}, u32[]{:S(2)}, u32[]{:S(2)}) collective-permute-start(bf16[128,2304]{1,0:T(8,128)(2,1)} %get-tuple-element.23.refs_0_), channel_id=1, source_target_pairs={{0,4},{2,6},{8,0},{10,2},{16,8},{18,10},{24,16},{26,18},{28,24},{3... | collective-permute-start | bytes 1769480 | tf_op jit(solution)/shard_map/ppermute | solution.py:292
  109.3 27.6 %collective-permute-start.5 = (bf16[128,2304]{1,0:T(8,128)(2,1)}, bf16[128,2304]{1,0:T(8,128)(2,1)}, u32[]{:S(2)}, u32[]{:S(2)}) collective-permute-start(bf16[128,2304]{1,0:T(8,128)(2,1)} %get-tuple-element.23.refs_0_), channel_id=1, source_target_pairs={{0,8},{2,10},{8,16},{10,18},{16,24},{18,26},{24,28},{26,30},{28,20... | collective-permute-start | bytes 1769480 | tf_op jit(solution)/shard_map/ppermute | solution.py:292
  134.9 2.1 copy-start
  134.9 25.1 %collective-permute-start.8 = (bf16[128,2304]{1,0:T(8,128)(2,1)}, bf16[128,2304]{1,0:T(8,128)(2,1)S(1)}, u32[]{:S(2)}, u32[]{:S(2)}) collective-permute-start(bf16[128,2304]{1,0:T(8,128)(2,1)} %collective-permute-done.6.refs_2_), channel_id=1, source_target_pairs={{0,4},{2,6},{8,0},{10,2},{16,8},{18,10},{24,16},{26,18},{28,24},{3... | collective-permute-start | bytes 1769480 | tf_op jit(solution)/shard_map/ppermute | solution.py:292
  136.8 23.1 %collective-permute-start.7 = (bf16[128,2304]{1,0:T(8,128)(2,1)}, bf16[128,2304]{1,0:T(8,128)(2,1)S(1)}, u32[]{:S(2)}, u32[]{:S(2)}) collective-permute-start(bf16[128,2304]{1,0:T(8,128)(2,1)} %collective-permute-done.5.refs_1_), channel_id=1, source_target_pairs={{0,8},{2,10},{8,16},{10,18},{16,24},{18,26},{24,28},{26,30},{28,20... | collective-permute-start | bytes 1769480 | tf_op jit(solution)/shard_map/ppermute | solution.py:292
  160.0 0.8 copy-start.3
  160.0 1.0 copy-start.4
  161.0 14.7 %collective-permute-start.16 = (bf16[128,2304]{1,0:T(8,128)(2,1)}, bf16[128,2304]{1,0:T(8,128)(2,1)S(1)}, u32[]{:S(2)}, u32[]{:S(2)}) collective-permute-start(bf16[128,2304]{1,0:T(8,128)(2,1)} %get-tuple-element.25.refs_3_), channel_id=1, source_target_pairs={{0,8},{2,10},{8,16},{10,18},{16,24},{18,26},{24,28},{26,30},{28,20... | collective-permute-start | bytes 1769480 | tf_op jit(solution)/shard_map/ppermute | solution.py:292
  161.0 15.0 %collective-permute-start.17 = (bf16[128,2304]{1,0:T(8,128)(2,1)}, bf16[128,2304]{1,0:T(8,128)(2,1)S(1)}, u32[]{:S(2)}, u32[]{:S(2)}) collective-permute-start(bf16[128,2304]{1,0:T(8,128)(2,1)} %get-tuple-element.26.refs_4_), channel_id=1, source_target_pairs={{0,4},{2,6},{8,0},{10,2},{16,8},{18,10},{24,16},{26,18},{28,24},{3... | collective-permute-start | bytes 1769480 | tf_op jit(solution)/shard_map/ppermute | solution.py:292
  175.7 7.9 %copy-start.6 = (bf16[128,2304]{1,0:T(8,128)(2,1)}, bf16[128,2304]{1,0:T(8,128)(2,1)S(1)}, u32[]{:S(2)}) copy-start(bf16[128,2304]{1,0:T(8,128)(2,1)S(1)} %collective-permute-done.16.refs_5_) | copy-start | bytes 1769476
  175.7 7.3 %collective-permute-start.18 = (bf16[64,2304]{1,0:T(8,128)(2,1)S(1)}, bf16[64,2304]{1,0:T(8,128)(2,1)S(1)}, u32[]{:S(2)}, u32[]{:S(2)}) collective-permute-start(bf16[64,2304]{1,0:T(8,128)(2,1)S(1)} %slice.18), channel_id=1, source_target_pairs={{0,8},{2,10},{8,16},{10,18},{16,24},{18,26},{24,28},{26,30},{28,20... | collective-permute-start | bytes 884744 | tf_op jit(solution)/shard_map/ppermute | solution.py:292
  176.0 7.5 %copy-start.7 = (bf16[128,2304]{1,0:T(8,128)(2,1)}, bf16[128,2304]{1,0:T(8,128)(2,1)S(1)}, u32[]{:S(2)}) copy-start(bf16[128,2304]{1,0:T(8,128)(2,1)S(1)} %collective-permute-done.17.refs_6_) | copy-start | bytes 1769476
  176.1 7.5 %collective-permute-start.19 = (bf16[64,2304]{1,0:T(8,128)(2,1)S(1)}, bf16[64,2304]{1,0:T(8,128)(2,1)S(1)}, u32[]{:S(2)}, u32[]{:S(2)}) collective-permute-start(bf16[64,2304]{1,0:T(8,128)(2,1)S(1)} %slice.19), channel_id=1, source_target_pairs={{0,4},{2,6},{8,0},{10,2},{16,8},{18,10},{24,16},{26,18},{28,24},{3... | collective-permute-start | bytes 884744 | tf_op jit(solution)/shard_map/ppermute | solution.py:292
  183.0 0.7 copy-start.14
  183.7 0.7 copy-start.15
  190.5 35.8 %collective-permute-start.20 = (bf16[1024,2304]{1,0:T(8,128)(2,1)}, bf16[1024,2304]{1,0:T(8,128)(2,1)}, u32[]{:S(2)}, u32[]{:S(2)}) collective-permute-start(bf16[1024,2304]{1,0:T(8,128)(2,1)} %merge.3.refs_5_.refs_0_.refs_1_), channel_id=1, source_target_pairs={{0,2},{2,0},{4,6},{6,4},{8,10},{10,8},{12,14},{14,12},{16,18},{18,... | collective-permute-start | bytes 14155784 | tf_op jit(solution)/shard_map/ppermute | solution.py:295
  241.3 25.6 %collective-permute-start.21 = (bf16[512,768]{1,0:T(8,128)(2,1)}, bf16[512,768]{1,0:T(8,128)(2,1)S(1)}, u32[]{:S(2)}, u32[]{:S(2)}) collective-permute-start(bf16[512,768]{1,0:T(8,128)(2,1)} %bitcast.14), channel_id=1, source_target_pairs={{0,1},{1,0},{2,3},{3,2},{4,5},{5,4},{6,7},{7,6},{8,9},{9,8},{10,11... | collective-permute-start | bytes 2359304 | tf_op jit(solution)/shard_map/ppermute | solution.py:408
  243.2 23.8 %copy-start.1 = (f32[512,768]{1,0:T(8,128)S(1)}, f32[512,768]{1,0:T(8,128)}, u32[]{:S(2)}) copy-start(f32[512,768]{1,0:T(8,128)} %get-tuple-element.32.refs_3_) | copy-start | bytes 4718596
Sparse Core Ops, SparseCore 0:
  10.4 100.6 all-gather.1

commit v5 on v3

--- a/solution.py
+++ b/solution.py
@@ -3,6 +3,7 @@
 
 import jax
 import jax.numpy as jnp
+import numpy as np
 from jax import lax
 from jax.experimental import pallas as pl
 from jax.experimental.pallas import tpu as pltpu
@@ -10,7 +11,7 @@
 
 BLOCK = 384
 STEP = 2 * BLOCK
-SHARES = (1, 1)
+SHARES = (10, 6)
 VMEM_LIMIT = 56 * 1024 * 1024
 
 
@@ -29,6 +30,23 @@
         done += share
         bounds.append(round(steps * done / sum(SHARES)))
     return [(a, b - a) for a, b in zip(bounds, bounds[1:]) if b > a]
+
+
+def ring_order(size):
+    chips = list(range(0, size // 2, 2)) + list(range(1, size // 2, 2))[::-1]
+    return [2 * chip + core for chip in chips for core in range(2)]
+
+
+def add_share(acc_ref, hg_ref, w_ref):
+    rows = w_ref.shape[0]
+    tile = 256 if rows % 256 == 0 else rows
+    for d in range(0, rows, tile):
+        acc_ref[:, d : d + tile] += lax.dot_general(
+            hg_ref[...],
+            w_ref[d : d + tile, :],
+            (((1,), (1,)), ((), ())),
+            preferred_element_type=jnp.float32,
+        )
 
 
 def block_stats(scale, grad_f32, wg_ref, left_ref, right_ref):
@@ -63,9 +81,7 @@
             else:
                 acc_ref[...] = ins[3][...]
 
-        acc_ref[...] += lax.dot_general(
-            hg_ref[...], w_ref[...], (((1,), (1,)), ((), ())), preferred_element_type=jnp.float32
-        )
+        add_share(acc_ref, hg_ref, w_ref)
     grad = jnp.dot(xt_ref[...], hg_ref[...], preferred_element_type=jnp.float32)
     block_stats(scale, grad, wg_ref, left_ref, right_ref)
 
@@ -112,33 +128,35 @@
     )(*args)
 
 
-def share_kernel(groups, group, steps, who_ref, hg_ref, w_ref, acc_ref, away_ref, own_ref, sum_ref):
+def share_kernel(groups, group, each, steps, from_ref, hg_ref, w_ref, acc_ref, away_ref, own_ref, sum_ref):
     step = pl.program_id(0)
 
     @pl.when(step == 0)
     def _():
         sum_ref[...] = acc_ref[...]
 
-    sum_ref[...] += lax.dot_general(
-        hg_ref[...], w_ref[...], (((1,), (1,)), ((), ())), preferred_element_type=jnp.float32
-    )
+    add_share(sum_ref, hg_ref, w_ref)
 
     @pl.when(step == steps - 1)
     def _():
         for k in range(groups):
-            at = pl.multiple_of(who_ref[k] * group, group)
-            part = sum_ref[pl.ds(at, group), :]
-            if k:
-                away_ref[k - 1] = part.astype(away_ref.dtype)
-            else:
-                own_ref[...] = part
-
-
-def share_call(who, hg, weight, acc, groups, offset, steps):
+            for j in range(group // each):
+                at = pl.multiple_of(from_ref[k * (group // each) + j], each)
+                part = sum_ref[pl.ds(at, each), :]
+                to = pl.ds(j * each, each)
+                if k:
+                    away_ref[k - 1, to, :] = part.astype(away_ref.dtype)
+                else:
+                    own_ref[to, :] = part
+
+
+def share_call(source, hg, weight, acc, groups, offset, steps):
     tokens, rows = acc.shape
     group = tokens // groups
     return pl.pallas_call(
-        functools.partial(share_kernel, groups, group, steps),
+        functools.partial(
+            share_kernel, groups, group, tokens // source.shape[0], steps
+        ),
         grid_spec=pltpu.PrefetchScalarGridSpec(
             num_scalar_prefetch=1,
             grid=(steps,),
@@ -164,29 +182,33 @@
             transcendentals=0,
         ),
         name="share",
-    )(who, hg, weight, acc)
-
-
-def on_device(cols, tokens, weight, pre_act, out_grad):
+    )(source, hg, weight, acc)
+
+
+def on_device(row_size, cols, tokens, weight, pre_act, out_grad):
     me = lax.axis_index("col")
     group, rows = tokens.shape
     num_tokens = group * cols
     scale = 1.0 / (BLOCK * num_tokens)
     chunks = chunk_steps(weight.shape[1] // STEP)
 
+    order, each = ring_order(row_size), pre_act.shape[0]
+
     gathered = []
     for offset, steps in chunks:
         at = slice(offset * STEP, (offset + steps) * STEP)
         slope = gelu_slope(pre_act[:, at].astype(jnp.float32))
         hidden = (out_grad[:, at].astype(jnp.float32) * slope).astype(jnp.bfloat16)
-        gathered.append(lax.all_gather(hidden, "row", axis=0, tiled=True))
-
-    own_t = tokens.T
-    x_t = jnp.zeros((rows, num_tokens), jnp.bfloat16)
-    x_t = lax.dynamic_update_slice(x_t, own_t, (0, me * group))
+        gathered.append(
+            lax.all_gather(hidden, "row", axis=0, tiled=True, axis_index_groups=[order])
+        )
+
+    x_all = jnp.zeros((num_tokens, rows), jnp.bfloat16)
+    x_all = lax.dynamic_update_slice(x_all, tokens, (me * group, 0))
     for s in range(1, cols):
-        piece = lax.ppermute(own_t, "col", [(i, (i + s) % cols) for i in range(cols)])
-        x_t = lax.dynamic_update_slice(x_t, piece, (0, (me - s) % cols * group))
+        piece = lax.ppermute(tokens, "col", [(i, (i + s) % cols) for i in range(cols)])
+        x_all = lax.dynamic_update_slice(x_all, piece, ((me - s) % cols * group, 0))
+    x_t = jnp.concatenate([x_all[r * each : (r + 1) * each] for r in order], axis=0).T
 
     acc, outs = None, None
     for (offset, steps), hg in zip(chunks[:-1], gathered[:-1]):
@@ -194,8 +216,9 @@
 
     offset, steps = chunks[-1]
     hg = gathered[-1]
-    who = (me + jnp.arange(cols, dtype=jnp.int32)) % cols
-    shares, own = share_call(who, hg, weight, acc, cols, offset, steps)
+    places = np.argsort(np.array(order)).astype(np.int32).reshape(cols, row_size // cols) * each
+    source = jnp.asarray(places)[(me + jnp.arange(cols)) % cols].reshape(-1)
+    shares, own = share_call(source, hg, weight, acc, cols, offset, steps)
     arrived = [
         lax.ppermute(shares[s - 1], "col", [(i, (i + s) % cols) for i in range(cols)])
         for s in range(1, cols)
@@ -210,7 +233,7 @@
     in_specs = (P("col", "row"), P("row", "col"), P("row", "col"), P("row", "col"))
     out_specs = (P("col", "row"), P("row", "col"), P("row", "col"), P("row", "col"))
     return jax.shard_map(
-        functools.partial(on_device, mesh.shape["col"]),
+        functools.partial(on_device, mesh.shape["row"], mesh.shape["col"]),
         mesh=mesh,
         in_specs=in_specs,
         out_specs=out_specs,

time: 271 us -> 200 us (0.74)
  waiting for transfers between devices: 162 us -> 89 us
    all_gather x2, waiting for transfers between devices: 145 us -> 73 us  [on_device(): lax.all_gather(hidden, 'row', axis=0, tiled=True, axis_index_groups=[order])]
    pallas_call x1, Pallas kernels: 17.9 us -> 14.6 us  [share_call(): pl.pallas_call(functools.partial(share_kernel, groups, group, tokens // s...]
    convert_element_type x1 -> x2, other arithmetic: 4.43 us -> 6.75 us  [on_device(): hidden = (out_grad[:, at].astype(jnp.float32) * slope).astype(jnp.bfloat16)]
  transfers between devices with their start and end apart: 4 -> 4, of which waited for: 3 -> 3; matrix products, arithmetic and copies ran while one was open for 0% -> 3% of each run, Pallas kernels for 24% -> 34%
where the time goes in v5:
time: 200 us
  waiting for transfers between devices  89 us (44%)
  Pallas kernels  82 us (41%)
  between operations  14.2 us (7%)
  other arithmetic  7.8 us (4%)
  starting transfers between devices  4.59 us (2%)
  local copies, waits for them, and re-layouts  2.44 us (1%)
    all_gather x2, waiting for transfers between devices, on_device(): lax.all_gather(hidden, 'row', axis=0, tiled=True, axis_index_groups=[order])  73 us
    pallas_call x2, Pallas kernels, chunk_call(): pl.pallas_call(functools.partial(chunk_kernel, scale, with_share, first),...  67.4 us
    ppermute x1, waiting for transfers between devices, on_device(): lax.ppermute(tokens, 'col', [(i, (i + s) % cols) for i in range(cols)])  16 us
    pallas_call x1, Pallas kernels, share_call(): pl.pallas_call(functools.partial(share_kernel, groups, group, tokens // s...  14.6 us
    convert_element_type x2, other arithmetic, on_device(): hidden = (out_grad[:, at].astype(jnp.float32) * slope).astype(jnp.bfloat16)  6.75 us
  transfers between devices with their start and end apart: 4, of which 3 were waited for; matrix products, arithmetic and copies ran while one was open for 3% of the time, Pallas kernels for 34%

profile of v5, /device:TPU:0, one launch (start us, length us, event | category | flops | bytes accessed | tf_op | source)
XLA Modules:
  0.0 200.0 jit_solution(2784797258731679924)
XLA Ops:
  7.2 0.0 all-gather.5.cloned.1.call-start
  7.2 3.8 %fusion.7 = bf16[64,7680]{1,0:T(8,128)(2,1)} fusion(bf16[64,12288]{1,0:T(8,128)(2,1)} %param.7, bf16[64,12288]{1,0:T(8,128)(2,1)} %param.8), kind=kLoop, calls=%fused_computation.22 | loop fusion | flops 10321920 | bytes 2949120 | tf_op jit(solution)/shard_map/convert_element_type | solution.py:201
  11.0 0.0 copy-start.2
  11.0 0.0 all-gather.5.cloned.1.call-update
  11.0 0.0 copy-start.3
  11.1 0.0 all-gather.3.cloned.1.call-start
  11.1 2.9 %fusion.16 = bf16[64,4608]{1,0:T(8,128)(2,1)} fusion(bf16[64,12288]{1,0:T(8,128)(2,1)} %param.7, bf16[64,12288]{1,0:T(8,128)(2,1)} %param.8), kind=kLoop, calls=%fused_computation.32 | loop fusion | flops 6193152 | bytes 1769472 | tf_op jit(solution)/shard_map/convert_element_type | solution.py:201
  14.0 0.0 all-gather.3.cloned.1.call-update
  14.1 0.0 copy-done.2
  14.1 0.3 copy.12
  14.4 3.0 %collective-permute-start = (bf16[512,768]{0,1:T(8,128)(2,1)S(1)}, bf16[512,768]{0,1:T(8,128)(2,1)S(1)}, u32[]{:S(2)}, u32[]{:S(2)}) collective-permute-start(bf16[512,768]{0,1:T(8,128)(2,1)S(1)} %copy.12), channel_id=1, source_target_pairs={{0,1},{1,0},{2,3},{3,2},{4,5},{5,4},{6,7},{7,6},{8,9},{9,8},{10,11... | collective-permute-start | bytes 2359304 | tf_op jit(solution)/shard_map/ppermute | solution.py:209
  17.4 0.0 copy-done.3
  17.4 0.6 gather_fusion
  18.0 0.7 reshape.60.from_ref
  18.6 0.2 broadcast_in_dim.4
  18.8 0.1 constant_dynamic-update-slice_fusion.1
  19.0 16.0 %collective-permute-done = bf16[512,768]{0,1:T(8,128)(2,1)S(1)} collective-permute-done((bf16[512,768]{0,1:T(8,128)(2,1)S(1)}, bf16[512,768]{0,1:T(8,128)(2,1)S(1)}, u32[]{:S(2)}, u32[]{:S(2)}) %collective-permute-start) | collective-permute-done | bytes 786464 | tf_op jit(solution)/shard_map/ppermute | solution.py:209
  34.9 0.1 constant_dynamic-update-slice_fusion
  35.0 0.1 slice_dynamic-update-slice_fusion.6
  35.1 0.1 slice_dynamic-update-slice_fusion.5
  35.2 0.1 slice_dynamic-update-slice_fusion.4
  35.3 0.1 slice_dynamic-update-slice_fusion
  35.4 0.1 slice_dynamic-update-slice_fusion.3
  35.5 0.1 slice_dynamic-update-slice_fusion.2
  35.5 0.1 slice_dynamic-update-slice_fusion.1
  35.6 0.0 copy-start
  35.6 62.4 %all-gather.5.cloned.1.call-done.refs_1_ = bf16[1024,7680]{1,0:T(8,128)(2,1)} async-done(((bf16[64,7680]{1,0:T(8,128)(2,1)}), bf16[1024,7680]{1,0:T(8,128)(2,1)}) %all-gather.5.cloned.1.call-update) | async-done | bytes 15728656 | tf_op jit(solution)/shard_map/all_gather | solution.py:203
  98.0 0.0 copy-done
  98.0 46.1 %chunk.2 = (bf16[768,12288]{1,0:T(8,128)(2,1)}, bf16[768,12288]{1,0:T(8,128)(2,1)}, bf16[768,12288]{1,0:T(8,128)(2,1)}, f32[1024,768]{1,0:T(8,128)}) custom-call(bf16[768,1024]{1,0:T(8,128)(2,1)} %bitcast.4, bf16[1024,7680]{1,0:T(8,128)(2,1)} %all-gather.5.cloned.1.call-done.refs_1_, bf16[768,12288]{1,0:T(8,128)(2,1)} %w_ref.1), custom_call_target="tpu_custom_call" | custom-call | flops 33218887680 | bytes 62914560 | tf_op jit(solution)/shard_map/chunk/pallas_call | solution.py:114
  144.2 10.6 %all-gather.3.cloned.1.call-done.hg_ref.refs_1_ = bf16[1024,4608]{1,0:T(8,128)(2,1)} async-done(((bf16[64,4608]{1,0:T(8,128)(2,1)}), bf16[1024,4608]{1,0:T(8,128)(2,1)}) %all-gather.3.cloned.1.call-update) | async-done | bytes 9437200 | tf_op jit(solution)/shard_map/all_gather | solution.py:203
  154.7 14.6 %share.1 = (bf16[1,512,768]{2,1,0:T(8,128)(2,1)}, f32[512,768]{1,0:T(8,128)}) custom-call(s32[16]{0:T(128)} %reshape.60.from_ref, bf16[1024,4608]{1,0:T(8,128)(2,1)} %all-gather.3.cloned.1.call-done.hg_ref.refs_1_, bf16[768,12288]{1,0:T(8,128)(2,1)} %w_ref.1, f32[1024,768]{1,0:T(8,128)} %get-tuple-element.13.acc_ref), custom_call_target="tpu_custom_call" | custom-call | flops 7247757312 | bytes 22806528 | tf_op jit(solution)/shard_map/share/pallas_call | solution.py:156
  169.4 1.5 collective-permute-start.1
  170.8 0.0 copy-start.1
  170.8 21.2 %chunk.3 = (bf16[768,12288]{1,0:T(8,128)(2,1)}, bf16[768,12288]{1,0:T(8,128)(2,1)}, bf16[768,12288]{1,0:T(8,128)(2,1)}) custom-call(bf16[768,1024]{1,0:T(8,128)(2,1)} %bitcast.5, bf16[1024,4608]{1,0:T(8,128)(2,1)} %all-gather.3.cloned.1.call-done.hg_ref.refs_1_, ...), custom_call_target="tpu_custom_call", output_to_operand_aliasing={{0}: (2, {}), {1}: (3, {}), {2}: (4, {})} | custom-call | flops 12683575296 | bytes 37748736 | tf_op jit(solution)/shard_map/chunk/pallas_call | solution.py:114
  192.1 0.0 collective-permute-done.1
  192.1 0.0 copy-done.1
  192.1 1.0 add_convert_fusion
  (2 shorter events, 0.0 us)
Async XLA Ops:
  7.2 90.9 %all-gather.5.cloned.1.call-start = ((), (), s32[]{:S(2)}) async-start(), calls=%async_computation.1 | async-start | bytes 16711680 | tf_op jit(solution)/shard_map/all_gather | solution.py:203
  11.0 3.1 %copy-start.2 = (bf16[512,768]{1,0:T(8,128)(2,1)S(1)}, bf16[512,768]{1,0:T(8,128)(2,1)}, u32[]{:S(2)}) copy-start(bf16[512,768]{1,0:T(8,128)(2,1)} %param.5) | copy-start | bytes 2359300
  11.0 6.4 %copy-start.3 = (s32[2,8]{1,0:T(2,128)S(1)}, s32[2,8]{1,0:T(2,128)}, u32[]{:S(2)}) copy-start(s32[2,8]{1,0:T(2,128)} %constant.54.clone) | copy-start | bytes 196
  11.1 143.7 %all-gather.3.cloned.1.call-start = ((), (), s32[]{:S(2)}) async-start(), calls=%async_computation | async-start | bytes 10027008 | tf_op jit(solution)/shard_map/all_gather | solution.py:203
  14.4 20.6 %collective-permute-start = (bf16[512,768]{0,1:T(8,128)(2,1)S(1)}, bf16[512,768]{0,1:T(8,128)(2,1)S(1)}, u32[]{:S(2)}, u32[]{:S(2)}) collective-permute-start(bf16[512,768]{0,1:T(8,128)(2,1)S(1)} %copy.12), channel_id=1, source_target_pairs={{0,1},{1,0},{2,3},{3,2},{4,5},{5,4},{6,7},{7,6},{8,9},{9,8},{10,11... | collective-permute-start | bytes 2359304 | tf_op jit(solution)/shard_map/ppermute | solution.py:209
  35.6 62.4 %copy-start = (bf16[1024,768]{0,1:T(8,128)(2,1)}, bf16[1024,768]{0,1:T(8,128)(2,1)S(1)}, u32[]{:S(2)}) copy-start(bf16[1024,768]{0,1:T(8,128)(2,1)S(1)} %slice_dynamic-update-slice_fusion.1) | copy-start | bytes 4718596
  169.4 22.7 %collective-permute-start.1 = (bf16[512,768]{1,0:T(8,128)(2,1)}, bf16[512,768]{1,0:T(8,128)(2,1)S(1)}, u32[]{:S(2)}, u32[]{:S(2)}) collective-permute-start(bf16[512,768]{1,0:T(8,128)(2,1)} %bitcast.6), channel_id=1, source_target_pairs={{0,1},{1,0},{2,3},{3,2},{4,5},{5,4},{6,7},{7,6},{8,9},{9,8},{10,11... | collective-permute-start | bytes 2359304 | tf_op jit(solution)/shard_map/ppermute | solution.py:223
  170.8 21.2 %copy-start.1 = (f32[512,768]{1,0:T(8,128)S(1)}, f32[512,768]{1,0:T(8,128)}, u32[]{:S(2)}) copy-start(f32[512,768]{1,0:T(8,128)} %get-tuple-element.14) | copy-start | bytes 4718596
Sparse Core Ops, SparseCore 0:
  11.2 86.8 all-gather.4
  100.2 54.4 all-gather.2

commit v6 on v5

v6 whole, which is shorter than its diff:
```python
import functools
import math

import jax
import jax.numpy as jnp
from jax import lax
from jax.experimental import pallas as pl
from jax.experimental.pallas import tpu as pltpu
from jax.sharding import PartitionSpec as P

BLOCK = 384
STEP = 2 * BLOCK
SHARES = (11, 5)
VMEM_LIMIT = 56 * 1024 * 1024


def gelu_slope(value):
    coeff = math.sqrt(2.0 / math.pi)
    inner = coeff * (value + 0.044715 * value * value * value)
    tanh_u = jnp.tanh(inner)
    return 0.5 * (1.0 + tanh_u) + 0.5 * value * (1.0 - tanh_u * tanh_u) * coeff * (
        1.0 + 3.0 * 0.044715 * value * value
    )


def chunk_steps(steps):
    bounds, done = [0], 0
    for share in SHARES:
        done += share
        bounds.append(round(steps * done / sum(SHARES)))
    return [(a, b - a) for a, b in zip(bounds, bounds[1:]) if b > a]


def gather_order(size):
    return [2, 3, 0, 1] + list(range(4, size))


def in_order(ref, base, group, index, each):
    turn = jnp.where(index == 0, 2 * each, 0)
    parts = [
        ref[pl.ds(pl.multiple_of(base + turn, each), 2 * each), :],
        ref[pl.ds(pl.multiple_of(base + 2 * each - turn, each), 2 * each), :],
    ]
    if group > 4 * each:
        parts.append(ref[pl.ds(pl.multiple_of(base + 4 * each, each), group - 4 * each), :])
    return jnp.concatenate(parts, axis=0)


def add_share(acc_ref, hg, w_ref):
    rows = w_ref.shape[0]
    tile = 256 if rows % 256 == 0 else rows
    for d in range(0, rows, tile):
        acc_ref[:, d : d + tile] += lax.dot_general(
            hg,
            w_ref[d : d + tile, :],
            (((1,), (1,)), ((), ())),
            preferred_element_type=jnp.float32,
        )


def block_stats(scale, grad_f32, wg_ref, left_ref, right_ref):
    rows, cols = grad_f32.shape
    wg_ref[...] = grad_f32.astype(wg_ref.dtype)
    for i in range(rows // BLOCK):
        for j in range(cols // BLOCK):
            at = (pl.ds(i * BLOCK, BLOCK), pl.ds(j * BLOCK, BLOCK))
            tile = wg_ref[at]
            left = lax.dot_general(
                tile, tile, (((1,), (1,)), ((), ())), preferred_element_type=jnp.float32
            )
            left_ref[at] = (left * scale).astype(left_ref.dtype)
            right = lax.dot_general(
                tile, tile, (((0,), (0,)), ((), ())), preferred_element_type=jnp.float32
            )
            right_ref[at] = (right * scale).astype(right_ref.dtype)


def chunk_kernel(scale, each, own_only, first, who_ref, *refs):
    refs = list(refs)
    xt_ref, hg_ref, w_ref = refs[:3]
    acc_in = None if first else refs[3]
    wg_ref, left_ref, right_ref, acc_ref = refs[-4:]

    group = acc_ref.shape[0]

    @pl.when(pl.program_id(0) == 0)
    def _():
        if first:
            acc_ref[...] = jnp.zeros_like(acc_ref)
        elif own_only:
            acc_ref[...] = in_order(acc_in, 0, group, who_ref[0], each)
        else:
            acc_ref[...] = acc_in[...]

    grad = jnp.dot(xt_ref[...], hg_ref[...], preferred_element_type=jnp.float32)
    if own_only:
        me = who_ref[0]
        add_share(acc_ref, in_order(hg_ref, me * group, group, me, each), w_ref)
    else:
        add_share(acc_ref, hg_ref[...], w_ref)
    block_stats(scale, grad, wg_ref, left_ref, right_ref)


def chunk_call(scale, each, who, x_t, hg, weight, acc, outs, offset, steps, own_only):
    rows, tokens = x_t.shape
    first = outs is None
    kept = tokens // who.shape[0] if own_only else tokens
    at = lambda s, who: (0, s + offset)
    args = [x_t, hg, weight]
    in_specs = [
        pl.BlockSpec((rows, tokens), lambda s, who: (0, 0)),
        pl.BlockSpec((tokens, STEP), lambda s, who: (0, s)),
        pl.BlockSpec((rows, STEP), at),
    ]
    aliases = {}
    if not first:
        place = (lambda s, who: (who[0], 0)) if own_only else (lambda s, who: (0, 0))
        args.append(acc)
        in_specs.append(pl.BlockSpec((kept, rows), place))
        aliases = {1 + len(args) + i: i for i in range(3)}
        args += list(outs)
        in_specs += [pl.BlockSpec(memory_space=pl.ANY)] * 3
    cells = steps * STEP * rows
    return pl.pallas_call(
        functools.partial(chunk_kernel, scale, each, own_only, first),
        grid_spec=pltpu.PrefetchScalarGridSpec(
            num_scalar_prefetch=1,
            grid=(steps,),
            in_specs=in_specs,
            out_specs=[pl.BlockSpec((rows, STEP), at)] * 3
            + [pl.BlockSpec((kept, rows), lambda s, who: (0, 0))],
        ),
        out_shape=[jax.ShapeDtypeStruct(weight.shape, jnp.bfloat16)] * 3
        + [jax.ShapeDtypeStruct((kept, rows), jnp.float32)],
        input_output_aliases=aliases,
        compiler_params=pltpu.CompilerParams(vmem_limit_bytes=VMEM_LIMIT),
        cost_estimate=pl.CostEstimate(
            flops=cells * (2 * tokens + 2 * kept + 4 * BLOCK),
            bytes_accessed=8 * cells + 2 * steps * STEP * tokens,
            transcendentals=0,
        ),
        name="chunk",
    )(who, *args)


def away_kernel(each, steps, who_ref, hg_ref, w_ref, acc_ref, out_ref, sum_ref):
    step = pl.program_id(1)

    @pl.when(step == 0)
    def _():
        sum_ref[...] = acc_ref[...]

    add_share(sum_ref, hg_ref[...], w_ref)

    @pl.when(step == steps - 1)
    def _():
        index = who_ref[pl.program_id(0) + 1]
        total = in_order(sum_ref, 0, sum_ref.shape[0], index, each)
        out_ref[0] = total.astype(out_ref.dtype)


def away_call(each, who, hg, weight, acc, offset, steps):
    tokens, rows = acc.shape
    others = who.shape[0] - 1
    group = tokens // (others + 1)
    return pl.pallas_call(
        functools.partial(away_kernel, each, steps),
        grid_spec=pltpu.PrefetchScalarGridSpec(
            num_scalar_prefetch=1,
            grid=(others, steps),
            in_specs=[
                pl.BlockSpec((group, STEP), lambda p, s, who: (who[p + 1], s)),
                pl.BlockSpec((rows, STEP), lambda p, s, who: (0, s + offset)),
                pl.BlockSpec((group, rows), lambda p, s, who: (who[p + 1], 0)),
            ],
            out_specs=pl.BlockSpec((1, group, rows), lambda p, s, who: (p, 0, 0)),
            scratch_shapes=[pltpu.VMEM((group, rows), jnp.float32)],
        ),
        out_shape=jax.ShapeDtypeStruct((others, group, rows), jnp.bfloat16),
        compiler_params=pltpu.CompilerParams(vmem_limit_bytes=VMEM_LIMIT),
        cost_estimate=pl.CostEstimate(
            flops=2 * others * group * steps * STEP * rows,
            bytes_accessed=2 * steps * STEP * (rows + group) + 8 * group * rows,
            transcendentals=0,
        ),
        name="away",
    )(who, hg, weight, acc)


def on_device(row_size, cols, tokens, weight, pre_act, out_grad):
    me = lax.axis_index("col")
    group, rows = tokens.shape
    num_tokens = group * cols
    scale = 1.0 / (BLOCK * num_tokens)
    chunks = chunk_steps(weight.shape[1] // STEP)

    order, each = gather_order(row_size), pre_act.shape[0]

    gathered = []
    for offset, steps in chunks:
        at = slice(offset * STEP, (offset + steps) * STEP)
        slope = gelu_slope(pre_act[:, at].astype(jnp.float32))
        hidden = (out_grad[:, at].astype(jnp.float32) * slope).astype(jnp.bfloat16)
        gathered.append(
            lax.all_gather(hidden, "row", axis=0, tiled=True, axis_index_groups=[order])
        )

    x_all = jnp.zeros((num_tokens, rows), jnp.bfloat16)
    x_all = lax.dynamic_update_slice(x_all, tokens, (me * group, 0))
    for s in range(1, cols):
        piece = lax.ppermute(tokens, "col", [(i, (i + s) % cols) for i in range(cols)])
        x_all = lax.dynamic_update_slice(x_all, piece, ((me - s) % cols * group, 0))
    x_t = jnp.concatenate([x_all[r * each : (r + 1) * each] for r in order], axis=0).T

    who = ((me + jnp.arange(cols)) % cols).astype(jnp.int32)
    acc, outs = None, None
    for (offset, steps), hg in zip(chunks[:-1], gathered[:-1]):
        *outs, acc = chunk_call(scale, each, who, x_t, hg, weight, acc, outs, offset, steps, False)

    (offset, steps), hg = chunks[-1], gathered[-1]
    shares = away_call(each, who, hg, weight, acc, offset, steps)
    arrived = [
        lax.ppermute(shares[s - 1], "col", [(i, (i + s) % cols) for i in range(cols)])
        for s in range(1, cols)
    ]
    *outs, own = chunk_call(scale, each, who, x_t, hg, weight, acc, outs, offset, steps, True)
    for piece in arrived:
        own = own + piece.astype(jnp.float32)
    return (own.astype(jnp.bfloat16), *outs)


def solution(mesh):
    in_specs = (P("col", "row"), P("row", "col"), P("row", "col"), P("row", "col"))
    out_specs = (P("col", "row"), P("row", "col"), P("row", "col"), P("row", "col"))
    return jax.shard_map(
        functools.partial(on_device, mesh.shape["row"], mesh.shape["col"]),
        mesh=mesh,
        in_specs=in_specs,
        out_specs=out_specs,
        check_vma=False,
    )
```

time: 200 us -> 199 us (level)
  other arithmetic: 7.8 us -> 11.2 us
  waiting for transfers between devices: 89 us -> 85.8 us
    all_gather x2, waiting for transfers between devices: 73 us -> 69 us  [on_device(): lax.all_gather(hidden, 'row', axis=0, tiled=True, axis_index_groups=[order])]
  transfers between devices with their start and end apart: 4 -> 4, of which waited for: 3 -> 2; matrix products, arithmetic and copies ran while one was open for 3% -> 3% of each run, Pallas kernels for 34% -> 37%
where the time goes in v6:
time: 199 us
  waiting for transfers between devices  85.8 us (43%)
  Pallas kernels  82.4 us (41%)
  between operations  14.1 us (7%)
  other arithmetic  11.2 us (6%)
  starting transfers between devices  4.59 us (2%)
    pallas_call x2, Pallas kernels, chunk_call(): pl.pallas_call(functools.partial(chunk_kernel, scale, each, own_only, fir...  73.1 us
    all_gather x2, waiting for transfers between devices, on_device(): lax.all_gather(hidden, 'row', axis=0, tiled=True, axis_index_groups=[order])  69 us
    ppermute x1, waiting for transfers between devices, on_device(): lax.ppermute(tokens, 'col', [(i, (i + s) % cols) for i in range(cols)])  16.7 us
    pallas_call x1, Pallas kernels, away_call(): pl.pallas_call(functools.partial(away_kernel, each, steps), grid_spec=plt...  9.29 us
    convert_element_type x2, other arithmetic, on_device(): hidden = (out_grad[:, at].astype(jnp.float32) * slope).astype(jnp.bfloat16)  6.75 us
  transfers between devices with their start and end apart: 4, of which 2 were waited for; matrix products, arithmetic and copies ran while one was open for 3% of the time, Pallas kernels for 37%

profile of v6, /device:TPU:0, one launch (start us, length us, event | category | flops | bytes accessed | tf_op | source)
XLA Modules:
  0.0 198.9 jit_solution(16049015437274663820)
XLA Ops:
  7.2 0.0 all-gather.5.cloned.1.call-start
  7.2 4.0 %fusion.7 = bf16[64,8448]{1,0:T(8,128)(2,1)} fusion(bf16[64,12288]{1,0:T(8,128)(2,1)} %param.6, bf16[64,12288]{1,0:T(8,128)(2,1)} %param.7), kind=kLoop, calls=%fused_computation.21 | loop fusion | flops 11354112 | bytes 3244032 | tf_op jit(solution)/shard_map/convert_element_type | solution.py:203
  11.3 0.0 copy-start
  11.3 0.0 all-gather.5.cloned.1.call-update
  11.3 0.0 all-gather.3.cloned.1.call-start
  11.3 2.7 %fusion.16 = bf16[64,3840]{1,0:T(8,128)(2,1)} fusion(bf16[64,12288]{1,0:T(8,128)(2,1)} %param.6, bf16[64,12288]{1,0:T(8,128)(2,1)} %param.7), kind=kLoop, calls=%fused_computation.32 | loop fusion | flops 5160960 | bytes 1474560 | tf_op jit(solution)/shard_map/convert_element_type | solution.py:203
  14.0 0.0 all-gather.3.cloned.1.call-update
  14.1 0.0 copy-done
  14.1 0.3 copy.11
  14.4 3.0 %collective-permute-start = (bf16[512,768]{0,1:T(8,128)(2,1)S(1)}, bf16[512,768]{0,1:T(8,128)(2,1)S(1)}, u32[]{:S(2)}, u32[]{:S(2)}) collective-permute-start(bf16[512,768]{0,1:T(8,128)(2,1)S(1)} %copy.11), channel_id=1, source_target_pairs={{0,1},{1,0},{2,3},{3,2},{4,5},{5,4},{6,7},{7,6},{8,9},{9,8},{10,11... | collective-permute-start | bytes 2359304 | tf_op jit(solution)/shard_map/ppermute | solution.py:211
  17.4 0.5 and_select_fusion.who_ref
  17.9 0.2 broadcast_in_dim.3
  18.1 0.1 constant_dynamic-update-slice_fusion.1
  18.2 16.7 %collective-permute-done = bf16[512,768]{0,1:T(8,128)(2,1)S(1)} collective-permute-done((bf16[512,768]{0,1:T(8,128)(2,1)S(1)}, bf16[512,768]{0,1:T(8,128)(2,1)S(1)}, u32[]{:S(2)}, u32[]{:S(2)}) %collective-permute-start) | collective-permute-done | bytes 786464 | tf_op jit(solution)/shard_map/ppermute | solution.py:211
  34.9 0.1 constant_dynamic-update-slice_fusion
  35.0 0.1 slice.46
  35.1 0.1 fusion.19
  35.2 1.4 maximum_bitcast_fusion.refs_0_
  36.6 69.0 %all-gather.5.cloned.1.call-done.refs_1_ = bf16[1024,8448]{1,0:T(8,128)(2,1)} async-done(((bf16[64,8448]{1,0:T(8,128)(2,1)}), bf16[1024,8448]{1,0:T(8,128)(2,1)}) %all-gather.5.cloned.1.call-update) | async-done | bytes 17301520 | tf_op jit(solution)/shard_map/all_gather | solution.py:205
  105.7 50.4 %chunk.2 = (bf16[768,12288]{1,0:T(8,128)(2,1)}, bf16[768,12288]{1,0:T(8,128)(2,1)}, bf16[768,12288]{1,0:T(8,128)(2,1)}, f32[1024,768]{1,0:T(8,128)}) custom-call(s32[2]{0:T(128)} %and_select_fusion.who_ref, bf16[768,1024]{1,0:T(8,128)(2,1)} %maximum_bitcast_fusion.refs_0_, bf16[1024,8448]{1,0:T(8,128)(2,1)} %all-gather.5.cloned.1.call-done.refs_1_, ...), custom_call_target="tpu_custom_call" | custom-call | flops 36540776448 | bytes 69206016 | tf_op jit(solution)/shard_map/chunk/pallas_call | solution.py:124
  156.1 0.0 all-gather.3.cloned.1.call-done.refs_1_.hg_ref
  156.1 9.3 %away.1 = bf16[1,512,768]{2,1,0:T(8,128)(2,1)} custom-call(s32[2]{0:T(128)} %and_select_fusion.who_ref, bf16[1024,3840]{1,0:T(8,128)(2,1)} %all-gather.3.cloned.1.call-done.refs_1_.hg_ref, bf16[768,12288]{1,0:T(8,128)(2,1)} %w_ref.1, f32[1024,768]{1,0:T(8,128)} %get-tuple-element.12.refs_3_.acc_ref), custom_call_target="tpu_custom_call" | custom-call | flops 3019898880 | bytes 12976128 | tf_op jit(solution)/shard_map/away/pallas_call | solution.py:166
  165.4 1.5 collective-permute-start.1
  166.9 22.7 %chunk.3 = (bf16[768,12288]{1,0:T(8,128)(2,1)}, bf16[768,12288]{1,0:T(8,128)(2,1)}, bf16[768,12288]{1,0:T(8,128)(2,1)}, f32[512,768]{1,0:T(8,128)}) custom-call(s32[2]{0:T(128)} %and_select_fusion.who_ref, bf16[768,1024]{1,0:T(8,128)(2,1)} %maximum_bitcast_fusion.refs_0_, ...), custom_call_target="tpu_custom_call", output_to_operand_aliasing={{0}: (5, {}), {1}: (6, {}), {2}: (7, {})} | custom-call | flops 13589544960 | bytes 31457280 | tf_op jit(solution)/shard_map/chunk/pallas_call | solution.py:124
  189.6 0.0 collective-permute-done.1
  189.6 2.4 %add_convert_fusion = bf16[512,768]{1,0:T(8,128)(2,1)} fusion(f32[512,768]{1,0:T(8,128)} %get-tuple-element.16, bf16[512,768]{1,0:T(8,128)(2,1)S(1)} %collective-permute-done.1), kind=kLoop, calls=%fused_computation.24 | loop fusion | flops 1179648 | bytes 3145728 | tf_op jit(solution)/shard_map/convert_element_type | solution.py:229
Async XLA Ops:
  7.2 98.5 %all-gather.5.cloned.1.call-start = ((), (), s32[]{:S(2)}) async-start(), calls=%async_computation.1 | async-start | bytes 18382848 | tf_op jit(solution)/shard_map/all_gather | solution.py:205
  11.3 2.8 %copy-start = (bf16[512,768]{1,0:T(8,128)(2,1)S(1)}, bf16[512,768]{1,0:T(8,128)(2,1)}, u32[]{:S(2)}) copy-start(bf16[512,768]{1,0:T(8,128)(2,1)} %param.4) | copy-start | bytes 2359300
  11.3 144.8 %all-gather.3.cloned.1.call-start = ((), (), s32[]{:S(2)}) async-start(), calls=%async_computation | async-start | bytes 8355840 | tf_op jit(solution)/shard_map/all_gather | solution.py:205
  14.4 20.6 %collective-permute-start = (bf16[512,768]{0,1:T(8,128)(2,1)S(1)}, bf16[512,768]{0,1:T(8,128)(2,1)S(1)}, u32[]{:S(2)}, u32[]{:S(2)}) collective-permute-start(bf16[512,768]{0,1:T(8,128)(2,1)S(1)} %copy.11), channel_id=1, source_target_pairs={{0,1},{1,0},{2,3},{3,2},{4,5},{5,4},{6,7},{7,6},{8,9},{9,8},{10,11... | collective-permute-start | bytes 2359304 | tf_op jit(solution)/shard_map/ppermute | solution.py:211
  165.4 24.2 %collective-permute-start.1 = (bf16[512,768]{1,0:T(8,128)(2,1)}, bf16[512,768]{1,0:T(8,128)(2,1)S(1)}, u32[]{:S(2)}, u32[]{:S(2)}) collective-permute-start(bf16[512,768]{1,0:T(8,128)(2,1)} %bitcast.3), channel_id=1, source_target_pairs={{0,1},{1,0},{2,3},{3,2},{4,5},{5,4},{6,7},{7,6},{8,9},{9,8},{10,11... | collective-permute-start | bytes 2359304 | tf_op jit(solution)/shard_map/ppermute | solution.py:223
Sparse Core Ops, SparseCore 0:
  11.4 94.2 all-gather.4
  107.8 47.0 all-gather.2

commit v7 on v5

--- a/solution.py
+++ b/solution.py
@@ -3,7 +3,6 @@
 
 import jax
 import jax.numpy as jnp
-import numpy as np
 from jax import lax
 from jax.experimental import pallas as pl
 from jax.experimental.pallas import tpu as pltpu
@@ -11,7 +10,7 @@
 
 BLOCK = 384
 STEP = 2 * BLOCK
-SHARES = (10, 6)
+SHARES = (11, 5)
 VMEM_LIMIT = 56 * 1024 * 1024
 
 
@@ -32,17 +31,27 @@
     return [(a, b - a) for a, b in zip(bounds, bounds[1:]) if b > a]
 
 
-def ring_order(size):
-    chips = list(range(0, size // 2, 2)) + list(range(1, size // 2, 2))[::-1]
-    return [2 * chip + core for chip in chips for core in range(2)]
-
-
-def add_share(acc_ref, hg_ref, w_ref):
+def gather_order(size):
+    return [2, 3, 0, 1] + list(range(4, size))
+
+
+def in_order(ref, base, group, index, each):
+    turn = jnp.where(index == 0, 2 * each, 0)
+    parts = [
+        ref[pl.ds(pl.multiple_of(base + turn, each), 2 * each), :],
+        ref[pl.ds(pl.multiple_of(base + 2 * each - turn, each), 2 * each), :],
+    ]
+    if group > 4 * each:
+        parts.append(ref[pl.ds(pl.multiple_of(base + 4 * each, each), group - 4 * each), :])
+    return jnp.concatenate(parts, axis=0)
+
+
+def add_share(acc_ref, hg, w_ref):
     rows = w_ref.shape[0]
     tile = 256 if rows % 256 == 0 else rows
     for d in range(0, rows, tile):
         acc_ref[:, d : d + tile] += lax.dot_general(
-            hg_ref[...],
+            hg,
             w_ref[d : d + tile, :],
             (((1,), (1,)), ((), ())),
             preferred_element_type=jnp.float32,
@@ -67,29 +76,26 @@
 
 
 def chunk_kernel(scale, with_share, first, *refs):
-    n_in = 2 + (1 if with_share else 0) + (1 if with_share and not first else 0)
-    ins, outs = refs[:n_in], refs[n_in + (0 if first else 3):]
-    xt_ref, hg_ref = ins[:2]
-    wg_ref, left_ref, right_ref = outs[:3]
+    refs = list(refs)
+    xt_ref, hg_ref = refs[:2]
     if with_share:
-        w_ref, acc_ref = ins[2], outs[3]
+        w_ref, acc_ref = refs[2], refs.pop()
 
         @pl.when(pl.program_id(0) == 0)
         def _():
-            if first:
-                acc_ref[...] = jnp.zeros_like(acc_ref)
-            else:
-                acc_ref[...] = ins[3][...]
-
-        add_share(acc_ref, hg_ref, w_ref)
+            acc_ref[...] = jnp.zeros_like(acc_ref) if first else refs[3][...]
+
     grad = jnp.dot(xt_ref[...], hg_ref[...], preferred_element_type=jnp.float32)
-    block_stats(scale, grad, wg_ref, left_ref, right_ref)
+    if with_share:
+        add_share(acc_ref, hg_ref[...], w_ref)
+    block_stats(scale, grad, *refs[-3:])
 
 
 def chunk_call(scale, x_t, hg, weight, acc, outs, offset, steps, with_share):
     rows, tokens = x_t.shape
     first = outs is None
     at = lambda s: (0, s + offset)
+    whole = pl.BlockSpec((tokens, rows), lambda s: (0, 0))
     args = [x_t, hg]
     in_specs = [
         pl.BlockSpec((rows, tokens), lambda s: (0, 0)),
@@ -100,11 +106,11 @@
     if with_share:
         args.append(weight)
         in_specs.append(pl.BlockSpec((rows, STEP), at))
-        out_shape = out_shape + [jax.ShapeDtypeStruct((tokens, rows), jnp.float32)]
-        out_specs = out_specs + [pl.BlockSpec((tokens, rows), lambda s: (0, 0))]
+        out_shape.append(jax.ShapeDtypeStruct((tokens, rows), jnp.float32))
+        out_specs.append(whole)
         if not first:
             args.append(acc)
-            in_specs.append(pl.BlockSpec((tokens, rows), lambda s: (0, 0)))
+            in_specs.append(whole)
     aliases = {}
     if not first:
         aliases = {len(args) + i: i for i in range(3)}
@@ -128,48 +134,41 @@
     )(*args)
 
 
-def share_kernel(groups, group, each, steps, from_ref, hg_ref, w_ref, acc_ref, away_ref, own_ref, sum_ref):
-    step = pl.program_id(0)
-
-    @pl.when(step == 0)
-    def _():
-        sum_ref[...] = acc_ref[...]
-
-    add_share(sum_ref, hg_ref, w_ref)
-
-    @pl.when(step == steps - 1)
-    def _():
-        for k in range(groups):
-            for j in range(group // each):
-                at = pl.multiple_of(from_ref[k * (group // each) + j], each)
-                part = sum_ref[pl.ds(at, each), :]
-                to = pl.ds(j * each, each)
-                if k:
-                    away_ref[k - 1, to, :] = part.astype(away_ref.dtype)
-                else:
-                    own_ref[to, :] = part
-
-
-def share_call(source, hg, weight, acc, groups, offset, steps):
+def share_kernel(each, who_ref, hg_ref, w_ref, acc_ref, away_ref, own_ref, sum_ref):
+    sum_ref[...] = acc_ref[...] + lax.dot_general(
+        hg_ref[...], w_ref[...], (((1,), (1,)), ((), ())), preferred_element_type=jnp.float32
+    )
+    group = own_ref.shape[0]
+    for k in range(away_ref.shape[0] + 1):
+        index = who_ref[k]
+        part = in_order(sum_ref, index * group, group, index, each)
+        if k:
+            away_ref[k - 1] = part.astype(away_ref.dtype)
+        else:
+            own_ref[...] = part
+
+
+def share_call(each, who, hg, w_last, acc):
     tokens, rows = acc.shape
+    width = hg.shape[1]
+    groups = who.shape[0]
     group = tokens // groups
+    tile = 256 if rows % 256 == 0 else rows
     return pl.pallas_call(
-        functools.partial(
-            share_kernel, groups, group, tokens // source.shape[0], steps
-        ),
+        functools.partial(share_kernel, each),
         grid_spec=pltpu.PrefetchScalarGridSpec(
             num_scalar_prefetch=1,
-            grid=(steps,),
+            grid=(rows // tile,),
             in_specs=[
-                pl.BlockSpec((tokens, STEP), lambda s, _: (0, s)),
-                pl.BlockSpec((rows, STEP), lambda s, _: (0, s + offset)),
-                pl.BlockSpec((tokens, rows), lambda s, _: (0, 0)),
+                pl.BlockSpec((tokens, width), lambda d, who: (0, 0)),
+                pl.BlockSpec((tile, width), lambda d, who: (d, 0)),
+                pl.BlockSpec((tokens, tile), lambda d, who: (0, d)),
             ],
             out_specs=[
-                pl.BlockSpec((groups - 1, group, rows), lambda s, _: (0, 0, 0)),
-                pl.BlockSpec((group, rows), lambda s, _: (0, 0)),
+                pl.BlockSpec((groups - 1, group, tile), lambda d, who: (0, 0, d)),
+                pl.BlockSpec((group, tile), lambda d, who: (0, d)),
             ],
-            scratch_shapes=[pltpu.VMEM((tokens, rows), jnp.float32)],
+            scratch_shapes=[pltpu.VMEM((tokens, tile), jnp.float32)],
         ),
         out_shape=[
             jax.ShapeDtypeStruct((groups - 1, group, rows), jnp.bfloat16),
@@ -177,12 +176,12 @@
         ],
         compiler_params=pltpu.CompilerParams(vmem_limit_bytes=VMEM_LIMIT),
         cost_estimate=pl.CostEstimate(
-            flops=2 * tokens * steps * STEP * rows,
-            bytes_accessed=2 * steps * STEP * (rows + tokens) + 8 * tokens * rows,
+            flops=2 * tokens * width * rows,
+            bytes_accessed=2 * width * (rows + tokens) + 8 * tokens * rows,
             transcendentals=0,
         ),
         name="share",
-    )(source, hg, weight, acc)
+    )(who, hg, w_last, acc)
 
 
 def on_device(row_size, cols, tokens, weight, pre_act, out_grad):
@@ -192,7 +191,7 @@
     scale = 1.0 / (BLOCK * num_tokens)
     chunks = chunk_steps(weight.shape[1] // STEP)
 
-    order, each = ring_order(row_size), pre_act.shape[0]
+    order, each = gather_order(row_size), pre_act.shape[0]
 
     gathered = []
     for offset, steps in chunks:
@@ -210,15 +209,14 @@
         x_all = lax.dynamic_update_slice(x_all, piece, ((me - s) % cols * group, 0))
     x_t = jnp.concatenate([x_all[r * each : (r + 1) * each] for r in order], axis=0).T
 
+    who = ((me + jnp.arange(cols)) % cols).astype(jnp.int32)
     acc, outs = None, None
+    w_last = weight[:, chunks[-1][0] * STEP :]
     for (offset, steps), hg in zip(chunks[:-1], gathered[:-1]):
         *outs, acc = chunk_call(scale, x_t, hg, weight, acc, outs, offset, steps, True)
 
-    offset, steps = chunks[-1]
-    hg = gathered[-1]
-    places = np.argsort(np.array(order)).astype(np.int32).reshape(cols, row_size // cols) * each
-    source = jnp.asarray(places)[(me + jnp.arange(cols)) % cols].reshape(-1)
-    shares, own = share_call(source, hg, weight, acc, cols, offset, steps)
+    (offset, steps), hg = chunks[-1], gathered[-1]
+    shares, own = share_call(each, who, hg, w_last, acc)
     arrived = [
         lax.ppermute(shares[s - 1], "col", [(i, (i + s) % cols) for i in range(cols)])
         for s in range(1, cols)

time: 200 us -> 197 us (0.985)
  waiting for transfers between devices: 89 us -> 80.4 us
  local copies, waits for them, and re-layouts: 2.44 us -> 6.45 us
    slice x0 -> x3, local copies, waits for them, and re-layouts: none -> 5.8 us  [the longest x1 5.64 us: on_device(): w_last = weight[:, chunks[-1][0] * STEP:]]
    ppermute x1, waiting for transfers between devices: 16 us -> 11.1 us  [on_device(): lax.ppermute(tokens, 'col', [(i, (i + s) % cols) for i in range(cols)])]
    all_gather x2, waiting for transfers between devices: 73 us -> 69.1 us  [on_device(): lax.all_gather(hidden, 'row', axis=0, tiled=True, axis_index_groups=[order])]
  transfers between devices with their start and end apart: 4 -> 4, of which waited for: 3 -> 3; matrix products, arithmetic and copies ran while one was open for 3% -> 6% of each run, Pallas kernels for 34% -> 35%
where the time goes in v7:
time: 197 us; the launch traced here: 196 us
  Pallas kernels  81.2 us (41%)
  waiting for transfers between devices  80.4 us (41%)
  between operations  14.1 us (7%)
  other arithmetic  9.67 us (5%)
  local copies, waits for them, and re-layouts  6.45 us (3%)
  starting transfers between devices  4.59 us (2%)
    all_gather x2, waiting for transfers between devices, on_device(): lax.all_gather(hidden, 'row', axis=0, tiled=True, axis_index_groups=[order])  69.1 us
    pallas_call x2, Pallas kernels, chunk_call(): pl.pallas_call(functools.partial(chunk_kernel, scale, with_share, first),...  68 us
    pallas_call x1, Pallas kernels, share_call(): pl.pallas_call(functools.partial(share_kernel, each), grid_spec=pltpu.Pre...  13.2 us
    ppermute x1, waiting for transfers between devices, on_device(): lax.ppermute(tokens, 'col', [(i, (i + s) % cols) for i in range(cols)])  11.1 us
    convert_element_type x2, other arithmetic, on_device(): hidden = (out_grad[:, at].astype(jnp.float32) * slope).astype(jnp.bfloat16)  6.75 us
    slice x1, local copies, waits for them, and re-layouts, on_device(): w_last = weight[:, chunks[-1][0] * STEP:]  5.64 us
  transfers between devices with their start and end apart: 4, of which 3 were waited for; matrix products, arithmetic and copies ran while one was open for 6% of the time, Pallas kernels for 35%

profile of v7, /device:TPU:0, one launch (start us, length us, event | category | flops | bytes accessed | tf_op | source)
XLA Modules:
  0.0 196.4 jit_solution(11078796514146209234)
XLA Ops:
  7.2 0.0 all-gather.5.cloned.1.call-start
  7.2 4.0 %fusion.7 = bf16[64,8448]{1,0:T(8,128)(2,1)} fusion(bf16[64,12288]{1,0:T(8,128)(2,1)} %param.6, bf16[64,12288]{1,0:T(8,128)(2,1)} %param.7), kind=kLoop, calls=%fused_computation.21 | loop fusion | flops 11354112 | bytes 3244032 | tf_op jit(solution)/shard_map/convert_element_type | solution.py:200
  11.3 0.0 copy-start.1
  11.3 0.0 all-gather.5.cloned.1.call-update
  11.3 0.0 all-gather.3.cloned.1.call-start
  11.3 2.7 %fusion.16 = bf16[64,3840]{1,0:T(8,128)(2,1)} fusion(bf16[64,12288]{1,0:T(8,128)(2,1)} %param.6, bf16[64,12288]{1,0:T(8,128)(2,1)} %param.7), kind=kLoop, calls=%fused_computation.32 | loop fusion | flops 5160960 | bytes 1474560 | tf_op jit(solution)/shard_map/convert_element_type | solution.py:200
  14.0 0.0 all-gather.3.cloned.1.call-update
  14.1 0.0 copy-done.1
  14.1 0.3 copy.11
  14.4 3.0 %collective-permute-start = (bf16[512,768]{0,1:T(8,128)(2,1)S(1)}, bf16[512,768]{0,1:T(8,128)(2,1)S(1)}, u32[]{:S(2)}, u32[]{:S(2)}) collective-permute-start(bf16[512,768]{0,1:T(8,128)(2,1)S(1)} %copy.11), channel_id=1, source_target_pairs={{0,1},{1,0},{2,3},{3,2},{4,5},{5,4},{6,7},{7,6},{8,9},{9,8},{10,11... | collective-permute-start | bytes 2359304 | tf_op jit(solution)/shard_map/ppermute | solution.py:208
  17.4 5.6 %slice.42.w_ref = bf16[768,3840]{1,0:T(8,128)(2,1)} slice(bf16[768,12288]{1,0:T(8,128)(2,1)} %refs_2_.1), slice={[0:768], [8448:12288]} | slice | bytes 11796480 | tf_op jit(solution)/shard_map/slice | solution.py:214
  23.0 0.5 and_select_fusion.who_ref
  23.5 0.2 broadcast_in_dim.3
  23.7 0.1 constant_dynamic-update-slice_fusion.1
  23.8 11.1 %collective-permute-done = bf16[512,768]{0,1:T(8,128)(2,1)S(1)} collective-permute-done((bf16[512,768]{0,1:T(8,128)(2,1)S(1)}, bf16[512,768]{0,1:T(8,128)(2,1)S(1)}, u32[]{:S(2)}, u32[]{:S(2)}) %collective-permute-start) | collective-permute-done | bytes 786464 | tf_op jit(solution)/shard_map/ppermute | solution.py:208
  34.9 0.1 constant_dynamic-update-slice_fusion
  35.0 0.1 slice.50
  35.1 0.1 fusion.19
  35.2 1.4 maximum_bitcast_fusion.refs_0_
  36.6 69.1 %all-gather.5.cloned.1.call-done.refs_1_ = bf16[1024,8448]{1,0:T(8,128)(2,1)} async-done(((bf16[64,8448]{1,0:T(8,128)(2,1)}), bf16[1024,8448]{1,0:T(8,128)(2,1)}) %all-gather.5.cloned.1.call-update) | async-done | bytes 17301520 | tf_op jit(solution)/shard_map/all_gather | solution.py:202
  105.7 49.7 %chunk.2 = (bf16[768,12288]{1,0:T(8,128)(2,1)}, bf16[768,12288]{1,0:T(8,128)(2,1)}, bf16[768,12288]{1,0:T(8,128)(2,1)}, f32[1024,768]{1,0:T(8,128)}) custom-call(bf16[768,1024]{1,0:T(8,128)(2,1)} %maximum_bitcast_fusion.refs_0_, bf16[1024,8448]{1,0:T(8,128)(2,1)} %all-gather.5.cloned.1.call-done.refs_1_, bf16[768,12288]{1,0:T(8,128)(2,1)} %refs_2_.1), custom_call_target="tpu_custom_call" | custom-call | flops 36540776448 | bytes 69206016 | tf_op jit(solution)/shard_map/chunk/pallas_call | solution.py:120
  155.4 0.0 all-gather.3.cloned.1.call-done.hg_ref.refs_1_
  155.4 13.2 %share.1 = (bf16[1,512,768]{2,1,0:T(8,128)(2,1)}, f32[512,768]{1,0:T(8,128)}) custom-call(s32[2]{0:T(128)} %and_select_fusion.who_ref, bf16[1024,3840]{1,0:T(8,128)(2,1)} %all-gather.3.cloned.1.call-done.hg_ref.refs_1_, bf16[768,3840]{1,0:T(8,128)(2,1)} %slice.42.w_ref, f32[1024,768]{1,0:T(8,128)} %get-tuple-element.13.acc_ref), custom_call_target="tpu_custom_call" | custom-call | flops 6039797760 | bytes 20054016 | tf_op jit(solution)/shard_map/share/pallas_call | solution.py:157
  168.6 1.5 collective-permute-start.1
  170.1 0.0 copy-start
  170.1 18.2 %chunk.3 = (bf16[768,12288]{1,0:T(8,128)(2,1)}, bf16[768,12288]{1,0:T(8,128)(2,1)}, bf16[768,12288]{1,0:T(8,128)(2,1)}) custom-call(bf16[768,1024]{1,0:T(8,128)(2,1)} %maximum_bitcast_fusion.refs_0_, bf16[1024,3840]{1,0:T(8,128)(2,1)} %all-gather.3.cloned.1.call-done.hg_ref.refs_1_, ...), custom_call_target="tpu_custom_call", output_to_operand_aliasing={{0}: (2, {}), {1}: (3, {}), {2}: (4, {})} | custom-call | flops 10569646080 | bytes 31457280 | tf_op jit(solution)/shard_map/chunk/pallas_call | solution.py:120
  188.3 0.2 collective-permute-done.1
  188.5 0.0 copy-done
  188.5 1.0 add_convert_fusion
Async XLA Ops:
  7.2 98.5 %all-gather.5.cloned.1.call-start = ((), (), s32[]{:S(2)}) async-start(), calls=%async_computation.1 | async-start | bytes 18382848 | tf_op jit(solution)/shard_map/all_gather | solution.py:202
  11.3 2.8 %copy-start.1 = (bf16[512,768]{1,0:T(8,128)(2,1)S(1)}, bf16[512,768]{1,0:T(8,128)(2,1)}, u32[]{:S(2)}) copy-start(bf16[512,768]{1,0:T(8,128)(2,1)} %param.4) | copy-start | bytes 2359300
  11.3 144.1 %all-gather.3.cloned.1.call-start = ((), (), s32[]{:S(2)}) async-start(), calls=%async_computation | async-start | bytes 8355840 | tf_op jit(solution)/shard_map/all_gather | solution.py:202
  14.4 20.6 %collective-permute-start = (bf16[512,768]{0,1:T(8,128)(2,1)S(1)}, bf16[512,768]{0,1:T(8,128)(2,1)S(1)}, u32[]{:S(2)}, u32[]{:S(2)}) collective-permute-start(bf16[512,768]{0,1:T(8,128)(2,1)S(1)} %copy.11), channel_id=1, source_target_pairs={{0,1},{1,0},{2,3},{3,2},{4,5},{5,4},{6,7},{7,6},{8,9},{9,8},{10,11... | collective-permute-start | bytes 2359304 | tf_op jit(solution)/shard_map/ppermute | solution.py:208
  168.6 19.9 %collective-permute-start.1 = (bf16[512,768]{1,0:T(8,128)(2,1)}, bf16[512,768]{1,0:T(8,128)(2,1)S(1)}, u32[]{:S(2)}, u32[]{:S(2)}) collective-permute-start(bf16[512,768]{1,0:T(8,128)(2,1)} %bitcast.3), channel_id=1, source_target_pairs={{0,1},{1,0},{2,3},{3,2},{4,5},{5,4},{6,7},{7,6},{8,9},{9,8},{10,11... | collective-permute-start | bytes 2359304 | tf_op jit(solution)/shard_map/ppermute | solution.py:221
  170.1 18.4 %copy-start = (f32[512,768]{1,0:T(8,128)S(1)}, f32[512,768]{1,0:T(8,128)}, u32[]{:S(2)}) copy-start(f32[512,768]{1,0:T(8,128)} %get-tuple-element.14) | copy-start | bytes 4718596
Sparse Core Ops, SparseCore 0:
  11.4 94.2 all-gather.4
  107.8 47.0 all-gather.2

commit v8 on v7

--- a/solution.py
+++ b/solution.py
@@ -11,7 +11,7 @@
 BLOCK = 384
 STEP = 2 * BLOCK
 SHARES = (11, 5)
-VMEM_LIMIT = 56 * 1024 * 1024
+VMEM_LIMIT = 36 * 1024 * 1024
 
 
 def gelu_slope(value):

time: 197 us -> 200 us (1.015)
  local copies, waits for them, and re-layouts: 6.45 us -> 13 us
  Pallas kernels: 81.2 us -> 76.6 us
  waiting for transfers between devices: 80.4 us -> 82.9 us
    unnamed x5 -> x13, local copies, waits for them, and re-layouts: 0.29 us -> 6.8 us
    pallas_call x2, Pallas kernels: 68 us -> 65.3 us  [chunk_call(): pl.pallas_call(functools.partial(chunk_kernel, scale, with_share, first),...]
  transfers between devices with their start and end apart: 4 -> 4, of which waited for: 3 -> 3; matrix products, arithmetic and copies ran while one was open for 6% -> 5% of each run, Pallas kernels for 35% -> 33%
where the time goes in v8:
time: 200 us; the launch traced here: 199 us
  waiting for transfers between devices  82.9 us (41%)
  Pallas kernels  76.6 us (38%)
  between operations  14.1 us (7%)
  local copies, waits for them, and re-layouts  13 us (6%)
  other arithmetic  8 us (4%)
  starting transfers between devices  4.65 us (2%)
    all_gather x2, waiting for transfers between devices, on_device(): lax.all_gather(hidden, 'row', axis=0, tiled=True, axis_index_groups=[order])  70.3 us
    pallas_call x2, Pallas kernels, chunk_call(): pl.pallas_call(functools.partial(chunk_kernel, scale, with_share, first),...  65.3 us
    ppermute x1, waiting for transfers between devices, on_device(): lax.ppermute(tokens, 'col', [(i, (i + s) % cols) for i in range(cols)])  11.6 us
    pallas_call x1, Pallas kernels, share_call(): pl.pallas_call(functools.partial(share_kernel, each), grid_spec=pltpu.Pre...  11.3 us
    unnamed x13, local copies, waits for them, and re-layouts  6.8 us
    convert_element_type x2, other arithmetic, on_device(): hidden = (out_grad[:, at].astype(jnp.float32) * slope).astype(jnp.bfloat16)  6.75 us
    slice x1, local copies, waits for them, and re-layouts, on_device(): w_last = weight[:, chunks[-1][0] * STEP:]  5.67 us
  transfers between devices with their start and end apart: 4, of which 3 were waited for; matrix products, arithmetic and copies ran while one was open for 5% of the time, Pallas kernels for 33%

profile of v8, /device:TPU:0, one launch (start us, length us, event | category | flops | bytes accessed | tf_op | source)
XLA Modules:
  0.0 199.3 jit_solution(12510462200731280486)
XLA Ops:
  7.2 0.0 all-gather.5.cloned.1.call-start
  7.2 4.0 %fusion.7 = bf16[64,8448]{1,0:T(8,128)(2,1)} fusion(bf16[64,12288]{1,0:T(8,128)(2,1)} %param.6, bf16[64,12288]{1,0:T(8,128)(2,1)} %param.7), kind=kLoop, calls=%fused_computation.21 | loop fusion | flops 11354112 | bytes 3244032 | tf_op jit(solution)/shard_map/convert_element_type | solution.py:200
  11.3 0.0 copy-start.3
  11.3 0.0 all-gather.5.cloned.1.call-update
  11.3 0.0 all-gather.3.cloned.1.call-start
  11.3 2.7 %fusion.16 = bf16[64,3840]{1,0:T(8,128)(2,1)} fusion(bf16[64,12288]{1,0:T(8,128)(2,1)} %param.6, bf16[64,12288]{1,0:T(8,128)(2,1)} %param.7), kind=kLoop, calls=%fused_computation.32 | loop fusion | flops 5160960 | bytes 1474560 | tf_op jit(solution)/shard_map/convert_element_type | solution.py:200
  14.0 0.0 all-gather.3.cloned.1.call-update
  14.1 0.0 copy-done.3
  14.1 0.3 copy.11
  14.4 3.0 %collective-permute-start = (bf16[512,768]{0,1:T(8,128)(2,1)S(1)}, bf16[512,768]{0,1:T(8,128)(2,1)S(1)}, u32[]{:S(2)}, u32[]{:S(2)}) collective-permute-start(bf16[512,768]{0,1:T(8,128)(2,1)S(1)} %copy.11), channel_id=1, source_target_pairs={{0,1},{1,0},{2,3},{3,2},{4,5},{5,4},{6,7},{7,6},{8,9},{9,8},{10,11... | collective-permute-start | bytes 2359304 | tf_op jit(solution)/shard_map/ppermute | solution.py:208
  17.4 5.7 %slice.42.w_ref = bf16[768,3840]{1,0:T(8,128)(2,1)} slice(bf16[768,12288]{1,0:T(8,128)(2,1)} %refs_2_.1), slice={[0:768], [8448:12288]} | slice | bytes 11796480 | tf_op jit(solution)/shard_map/slice | solution.py:214
  23.1 0.2 broadcast_in_dim.3
  23.3 0.1 constant_dynamic-update-slice_fusion.1
  23.4 11.6 %collective-permute-done = bf16[512,768]{0,1:T(8,128)(2,1)S(1)} collective-permute-done((bf16[512,768]{0,1:T(8,128)(2,1)S(1)}, bf16[512,768]{0,1:T(8,128)(2,1)S(1)}, u32[]{:S(2)}, u32[]{:S(2)}) %collective-permute-start) | collective-permute-done | bytes 786464 | tf_op jit(solution)/shard_map/ppermute | solution.py:208
  34.9 0.1 constant_dynamic-update-slice_fusion
  35.0 0.1 slice.50
  35.2 0.1 fusion.19
  35.2 0.2 maximum_bitcast_fusion.refs_0_
  35.4 70.3 %all-gather.5.cloned.1.call-done.refs_1_ = bf16[1024,8448]{1,0:T(8,128)(2,1)} async-done(((bf16[64,8448]{1,0:T(8,128)(2,1)}), bf16[1024,8448]{1,0:T(8,128)(2,1)}) %all-gather.5.cloned.1.call-update) | async-done | bytes 17301520 | tf_op jit(solution)/shard_map/all_gather | solution.py:202
  105.7 48.1 %chunk.2 = (bf16[768,12288]{1,0:T(8,128)(2,1)}, bf16[768,12288]{1,0:T(8,128)(2,1)}, bf16[768,12288]{1,0:T(8,128)(2,1)}, f32[1024,768]{1,0:T(8,128)S(1)}) custom-call(bf16[768,1024]{1,0:T(8,128)(2,1)S(1)} %maximum_bitcast_fusion.refs_0_, bf16[1024,8448]{1,0:T(8,128)(2,1)} %all-gather.5.cloned.1.call-done.refs_1_, bf16[768,12288]{1,0:T(8,128)(2,1)} %refs_2_.1), custom_call_target="tpu_custom_call" | custom-call | flops 36540776448 | bytes 69206016 | tf_op jit(solution)/shard_map/chunk/pallas_call | solution.py:120
  153.8 0.0 copy-start.1
  153.8 1.6 copy-done.1
  155.5 0.0 all-gather.3.cloned.1.call-done.hg_ref.refs_1_
  155.5 0.0 slice-start
  155.5 0.0 copy-start
  155.5 2.8 %copy-done = bf16[768,3840]{1,0:T(8,128)(2,1)S(1)} copy-done((bf16[768,3840]{1,0:T(8,128)(2,1)S(1)}, bf16[768,3840]{1,0:T(8,128)(2,1)}, u32[]{:S(2)}) %copy-start) | copy-done | bytes 5898264
  158.3 0.0 copy-start.2
  158.3 2.0 %copy-done.2 = f32[1024,768]{1,0:T(8,128)S(1)} copy-done((f32[1024,768]{1,0:T(8,128)S(1)}, f32[1024,768]{1,0:T(8,128)}, u32[]{:S(2)}) %copy-start.2) | copy-done | bytes 3145752
  160.3 0.0 slice-start.1
  160.3 11.3 %share.1 = (bf16[1,512,768]{2,1,0:T(8,128)(2,1)S(1)}, f32[512,768]{1,0:T(8,128)S(1)}) custom-call(s32[2]{0:T(128)S(1)} %and_select_fusion.who_ref, bf16[1024,3840]{1,0:T(8,128)(2,1)} %all-gather.3.cloned.1.call-done.hg_ref.refs_1_, bf16[768,3840]{1,0:T(8,128)(2,1)S(1)} %copy-done, f32[1024,768]{1,0:T(8,128)S(1)} %copy-done.2), custom_call_target="tpu_custom_call" | custom-call | flops 6039797760 | bytes 20054016 | tf_op jit(solution)/shard_map/share/pallas_call | solution.py:157
  171.6 1.5 collective-permute-start.1
  173.2 0.0 slice-done
  173.2 0.0 slice-done.1
  173.2 17.1 %chunk.3 = (bf16[768,12288]{1,0:T(8,128)(2,1)}, bf16[768,12288]{1,0:T(8,128)(2,1)}, bf16[768,12288]{1,0:T(8,128)(2,1)}) custom-call(bf16[768,1024]{1,0:T(8,128)(2,1)S(1)} %maximum_bitcast_fusion.refs_0_, bf16[1024,3840]{1,0:T(8,128)(2,1)S(1)} %bitcast.4, ...), custom_call_target="tpu_custom_call", output_to_operand_aliasing={{0}: (2, {}), {1}: (3, {}), {2}: (4, {})} | custom-call | flops 10569646080 | bytes 31457280 | tf_op jit(solution)/shard_map/chunk/pallas_call | solution.py:120
  190.3 1.1 collective-permute-done.1
  191.4 1.0 add_convert_fusion
  (2 shorter events, 0.0 us)
Async XLA Ops:
  7.2 98.5 %all-gather.5.cloned.1.call-start = ((), (), s32[]{:S(2)}) async-start(), calls=%async_computation.1 | async-start | bytes 18382848 | tf_op jit(solution)/shard_map/all_gather | solution.py:202
  11.3 2.8 %copy-start.3 = (bf16[512,768]{1,0:T(8,128)(2,1)S(1)}, bf16[512,768]{1,0:T(8,128)(2,1)}, u32[]{:S(2)}) copy-start(bf16[512,768]{1,0:T(8,128)(2,1)} %param.4) | copy-start | bytes 2359300
  11.3 144.2 %all-gather.3.cloned.1.call-start = ((), (), s32[]{:S(2)}) async-start(), calls=%async_computation | async-start | bytes 8355840 | tf_op jit(solution)/shard_map/all_gather | solution.py:202
  14.4 20.6 %collective-permute-start = (bf16[512,768]{0,1:T(8,128)(2,1)S(1)}, bf16[512,768]{0,1:T(8,128)(2,1)S(1)}, u32[]{:S(2)}, u32[]{:S(2)}) collective-permute-start(bf16[512,768]{0,1:T(8,128)(2,1)S(1)} %copy.11), channel_id=1, source_target_pairs={{0,1},{1,0},{2,3},{3,2},{4,5},{5,4},{6,7},{7,6},{8,9},{9,8},{10,11... | collective-permute-start | bytes 2359304 | tf_op jit(solution)/shard_map/ppermute | solution.py:208
  153.8 1.6 copy-start.1
  155.5 17.7 %slice-start = ((s8[7864320]{0:T(1024)(128)(4,1)}), s8[4194304]{0:T(1024)(128)(4,1)S(1)}, s32[]{:S(2)}) async-start(s8[7864320]{0:T(1024)(128)(4,1)} %bitcast.3), calls=%async_computation.2 | async-start | bytes 8388608
  155.5 2.8 %copy-start = (bf16[768,3840]{1,0:T(8,128)(2,1)S(1)}, bf16[768,3840]{1,0:T(8,128)(2,1)}, u32[]{:S(2)}) copy-start(bf16[768,3840]{1,0:T(8,128)(2,1)} %slice.42.w_ref) | copy-start | bytes 17694724
  158.3 2.0 %copy-start.2 = (f32[1024,768]{1,0:T(8,128)S(1)}, f32[1024,768]{1,0:T(8,128)}, u32[]{:S(2)}) copy-start(f32[1024,768]{1,0:T(8,128)} %copy-done.1) | copy-start | bytes 9437188
  160.3 12.9 %slice-start.1 = ((s8[7864320]{0:T(1024)(128)(4,1)}), s8[3670016]{0:T(1024)(128)(4,1)S(1)}, s32[]{:S(2)}) async-start(s8[7864320]{0:T(1024)(128)(4,1)} %bitcast.3), calls=%async_computation.3 | async-start | bytes 7340032
  171.6 19.8 %collective-permute-start.1 = (bf16[512,768]{1,0:T(8,128)(2,1)S(1)}, bf16[512,768]{1,0:T(8,128)(2,1)S(1)}, u32[]{:S(2)}, u32[]{:S(2)}) collective-permute-start(bf16[512,768]{1,0:T(8,128)(2,1)S(1)} %bitcast.5), channel_id=1, source_target_pairs={{0,1},{1,0},{2,3},{3,2},{4,5},{5,4},{6,7},{7,6},{8,9},{9,8},{10,11... | collective-permute-start | bytes 2359304 | tf_op jit(solution)/shard_map/ppermute | solution.py:221
Sparse Core Ops, SparseCore 0:
  11.4 94.2 all-gather.4
  107.8 47.0 all-gather.2

commit v9 on v7

--- a/solution.py
+++ b/solution.py
@@ -16,11 +16,10 @@
 
 def gelu_slope(value):
     coeff = math.sqrt(2.0 / math.pi)
-    inner = coeff * (value + 0.044715 * value * value * value)
-    tanh_u = jnp.tanh(inner)
-    return 0.5 * (1.0 + tanh_u) + 0.5 * value * (1.0 - tanh_u * tanh_u) * coeff * (
-        1.0 + 3.0 * 0.044715 * value * value
-    )
+    square = value * value
+    tanh_u = jnp.tanh(value * (coeff + (coeff * 0.044715) * square))
+    slope_u = value * (coeff + (3.0 * coeff * 0.044715) * square)
+    return (0.5 + 0.5 * tanh_u) * (1.0 + (1.0 - tanh_u) * slope_u)
 
 
 def chunk_steps(steps):

time: 197 us -> 196 us (level)
  no operation moved by 1% of the time
where the time goes in v9:
time: 196 us
  Pallas kernels  81.2 us (41%)
  waiting for transfers between devices  80.6 us (41%)
  between operations  14.1 us (7%)
  other arithmetic  9.27 us (5%)
  local copies, waits for them, and re-layouts  6.45 us (3%)
  starting transfers between devices  4.59 us (2%)
    all_gather x2, waiting for transfers between devices, on_device(): lax.all_gather(hidden, 'row', axis=0, tiled=True, axis_index_groups=[order])  69.2 us
    pallas_call x2, Pallas kernels, chunk_call(): pl.pallas_call(functools.partial(chunk_kernel, scale, with_share, first),...  68 us
    pallas_call x1, Pallas kernels, share_call(): pl.pallas_call(functools.partial(share_kernel, each), grid_spec=pltpu.Pre...  13.2 us
    ppermute x1, waiting for transfers between devices, on_device(): lax.ppermute(tokens, 'col', [(i, (i + s) % cols) for i in range(cols)])  11.1 us
    convert_element_type x2, other arithmetic, on_device(): hidden = (out_grad[:, at].astype(jnp.float32) * slope).astype(jnp.bfloat16)  6.34 us
    slice x1, local copies, waits for them, and re-layouts, on_device(): w_last = weight[:, chunks[-1][0] * STEP:]  5.64 us
  transfers between devices with their start and end apart: 4, of which 3 were waited for; matrix products, arithmetic and copies ran while one was open for 6% of the time, Pallas kernels for 35%

profile of v9, /device:TPU:0, one launch (start us, length us, event | category | flops | bytes accessed | tf_op | source)
XLA Modules:
  0.0 196.1 jit_solution(11001304870816343394)
XLA Ops:
  7.2 0.0 all-gather.5.cloned.1.call-start
  7.2 3.8 %fusion.9 = bf16[64,8448]{1,0:T(8,128)(2,1)} fusion(bf16[64,12288]{1,0:T(8,128)(2,1)} %param.6, bf16[64,12288]{1,0:T(8,128)(2,1)} %param.7), kind=kLoop, calls=%fused_computation.12 | loop fusion | flops 9191424 | bytes 3244032 | tf_op jit(solution)/shard_map/convert_element_type | solution.py:199
  11.0 0.0 copy-start.1
  11.0 0.0 all-gather.5.cloned.1.call-update
  11.0 0.0 all-gather.3.cloned.1.call-start
  11.1 2.6 %fusion.19 = bf16[64,3840]{1,0:T(8,128)(2,1)} fusion(bf16[64,12288]{1,0:T(8,128)(2,1)} %param.6, bf16[64,12288]{1,0:T(8,128)(2,1)} %param.7), kind=kLoop, calls=%fused_computation.27 | loop fusion | flops 4177920 | bytes 1474560 | tf_op jit(solution)/shard_map/convert_element_type | solution.py:199
  13.6 0.0 all-gather.3.cloned.1.call-update
  13.7 0.0 copy-done.1
  13.7 0.3 copy.11
  13.9 3.0 %collective-permute-start = (bf16[512,768]{0,1:T(8,128)(2,1)S(1)}, bf16[512,768]{0,1:T(8,128)(2,1)S(1)}, u32[]{:S(2)}, u32[]{:S(2)}) collective-permute-start(bf16[512,768]{0,1:T(8,128)(2,1)S(1)} %copy.11), channel_id=1, source_target_pairs={{0,1},{1,0},{2,3},{3,2},{4,5},{5,4},{6,7},{7,6},{8,9},{9,8},{10,11... | collective-permute-start | bytes 2359304 | tf_op jit(solution)/shard_map/ppermute | solution.py:207
  17.0 5.6 %slice.42.w_ref = bf16[768,3840]{1,0:T(8,128)(2,1)} slice(bf16[768,12288]{1,0:T(8,128)(2,1)} %refs_2_.1), slice={[0:768], [8448:12288]} | slice | bytes 11796480 | tf_op jit(solution)/shard_map/slice | solution.py:213
  22.6 0.5 and_select_fusion.who_ref
  23.1 0.2 broadcast_in_dim.3
  23.3 0.1 constant_dynamic-update-slice_fusion.1
  23.4 11.1 %collective-permute-done = bf16[512,768]{0,1:T(8,128)(2,1)S(1)} collective-permute-done((bf16[512,768]{0,1:T(8,128)(2,1)S(1)}, bf16[512,768]{0,1:T(8,128)(2,1)S(1)}, u32[]{:S(2)}, u32[]{:S(2)}) %collective-permute-start) | collective-permute-done | bytes 786464 | tf_op jit(solution)/shard_map/ppermute | solution.py:207
  34.5 0.1 constant_dynamic-update-slice_fusion
  34.6 0.1 slice.50
  34.7 0.1 fusion.21
  34.8 1.4 maximum_bitcast_fusion.refs_0_
  36.2 69.2 %all-gather.5.cloned.1.call-done.refs_1_ = bf16[1024,8448]{1,0:T(8,128)(2,1)} async-done(((bf16[64,8448]{1,0:T(8,128)(2,1)}), bf16[1024,8448]{1,0:T(8,128)(2,1)}) %all-gather.5.cloned.1.call-update) | async-done | bytes 17301520 | tf_op jit(solution)/shard_map/all_gather | solution.py:201
  105.4 49.7 %chunk.2 = (bf16[768,12288]{1,0:T(8,128)(2,1)}, bf16[768,12288]{1,0:T(8,128)(2,1)}, bf16[768,12288]{1,0:T(8,128)(2,1)}, f32[1024,768]{1,0:T(8,128)}) custom-call(bf16[768,1024]{1,0:T(8,128)(2,1)} %maximum_bitcast_fusion.refs_0_, bf16[1024,8448]{1,0:T(8,128)(2,1)} %all-gather.5.cloned.1.call-done.refs_1_, bf16[768,12288]{1,0:T(8,128)(2,1)} %refs_2_.1), custom_call_target="tpu_custom_call" | custom-call | flops 36540776448 | bytes 69206016 | tf_op jit(solution)/shard_map/chunk/pallas_call | solution.py:119
  155.1 0.0 all-gather.3.cloned.1.call-done.hg_ref.refs_1_
  155.1 13.2 %share.1 = (bf16[1,512,768]{2,1,0:T(8,128)(2,1)}, f32[512,768]{1,0:T(8,128)}) custom-call(s32[2]{0:T(128)} %and_select_fusion.who_ref, bf16[1024,3840]{1,0:T(8,128)(2,1)} %all-gather.3.cloned.1.call-done.hg_ref.refs_1_, bf16[768,3840]{1,0:T(8,128)(2,1)} %slice.42.w_ref, f32[1024,768]{1,0:T(8,128)} %get-tuple-element.13.acc_ref), custom_call_target="tpu_custom_call" | custom-call | flops 6039797760 | bytes 20054016 | tf_op jit(solution)/shard_map/share/pallas_call | solution.py:156
  168.4 1.5 collective-permute-start.1
  169.8 0.0 copy-start
  169.8 18.2 %chunk.3 = (bf16[768,12288]{1,0:T(8,128)(2,1)}, bf16[768,12288]{1,0:T(8,128)(2,1)}, bf16[768,12288]{1,0:T(8,128)(2,1)}) custom-call(bf16[768,1024]{1,0:T(8,128)(2,1)} %maximum_bitcast_fusion.refs_0_, bf16[1024,3840]{1,0:T(8,128)(2,1)} %all-gather.3.cloned.1.call-done.hg_ref.refs_1_, ...), custom_call_target="tpu_custom_call", output_to_operand_aliasing={{0}: (2, {}), {1}: (3, {}), {2}: (4, {})} | custom-call | flops 10569646080 | bytes 31457280 | tf_op jit(solution)/shard_map/chunk/pallas_call | solution.py:119
  188.1 0.2 collective-permute-done.1
  188.3 0.0 copy-done
  188.3 1.0 add_convert_fusion
Async XLA Ops:
  7.2 98.2 %all-gather.5.cloned.1.call-start = ((), (), s32[]{:S(2)}) async-start(), calls=%async_computation.1 | async-start | bytes 18382848 | tf_op jit(solution)/shard_map/all_gather | solution.py:201
  11.0 2.7 %copy-start.1 = (bf16[512,768]{1,0:T(8,128)(2,1)S(1)}, bf16[512,768]{1,0:T(8,128)(2,1)}, u32[]{:S(2)}) copy-start(bf16[512,768]{1,0:T(8,128)(2,1)} %param.4) | copy-start | bytes 2359300
  11.0 144.1 %all-gather.3.cloned.1.call-start = ((), (), s32[]{:S(2)}) async-start(), calls=%async_computation | async-start | bytes 8355840 | tf_op jit(solution)/shard_map/all_gather | solution.py:201
  13.9 20.6 %collective-permute-start = (bf16[512,768]{0,1:T(8,128)(2,1)S(1)}, bf16[512,768]{0,1:T(8,128)(2,1)S(1)}, u32[]{:S(2)}, u32[]{:S(2)}) collective-permute-start(bf16[512,768]{0,1:T(8,128)(2,1)S(1)} %copy.11), channel_id=1, source_target_pairs={{0,1},{1,0},{2,3},{3,2},{4,5},{5,4},{6,7},{7,6},{8,9},{9,8},{10,11... | collective-permute-start | bytes 2359304 | tf_op jit(solution)/shard_map/ppermute | solution.py:207
  168.4 19.9 %collective-permute-start.1 = (bf16[512,768]{1,0:T(8,128)(2,1)}, bf16[512,768]{1,0:T(8,128)(2,1)S(1)}, u32[]{:S(2)}, u32[]{:S(2)}) collective-permute-start(bf16[512,768]{1,0:T(8,128)(2,1)} %bitcast.3), channel_id=1, source_target_pairs={{0,1},{1,0},{2,3},{3,2},{4,5},{5,4},{6,7},{7,6},{8,9},{9,8},{10,11... | collective-permute-start | bytes 2359304 | tf_op jit(solution)/shard_map/ppermute | solution.py:220
  169.8 18.4 %copy-start = (f32[512,768]{1,0:T(8,128)S(1)}, f32[512,768]{1,0:T(8,128)}, u32[]{:S(2)}) copy-start(f32[512,768]{1,0:T(8,128)} %get-tuple-element.14) | copy-start | bytes 4718596
Sparse Core Ops, SparseCore 0:
  11.1 94.2 all-gather.4
  107.6 47.0 all-gather.2
